TPU v7x, 32 devices: a whole 2x2x4 slice. The times are simulated.
32 devices in a mesh: grp: 2 (over x), mem: 16 (over z, y, core).
Axes of the slice: x: 2, y: 2, z: 4, core: 2. Of those that a mesh axis runs over, the one named last changes fastest.
Arguments:
- field: bfloat16 [128, 16, 64, 256], P(('grp', 'mem')), parts along dimension 0, may hold values from -8 to 8
- norm_gain: float32 [2, 2, 256], replicated, may hold values from 0.1 to 1.9
- conv_weight: bfloat16 [2, 3, 3, 256, 512], replicated, may hold values from -0.125 to 0.125
- qkv_weight: bfloat16 [2, 256, 768], replicated, may hold values from -8 to 8
- out_weight: bfloat16 [2, 256, 256], replicated, may hold values from -0.375 to 0.375
Outputs:
- result: bfloat16 [128, 16, 64, 256], P(('grp', 'mem')), parts along dimension 0
There are 2 independent parts, one for each index of `grp`. A program takes and returns all parts, laid end to end along the dimension named above; an argument that names none is the same for every part. Nothing has to cross between parts.
All inputs are finite; a program needn't handle non-finite values.
Results may differ from a plain program's by a relative error of at most 0.014.
Values may be sent and summed in bfloat16 or wider, within the bound.
No kernel may reach another device: no remote copies, remote signals or barrier semaphores. Data moves between devices by JAX's collectives and lax.ppermute only.
A program may use at most 128 MiB of HBM per device.

v0:
```python
import functools

import jax
import jax.numpy as jnp
import numpy as np
from jax import lax
from jax.experimental import pallas as pl
from jax.experimental.pallas import tpu as pltpu
from jax.sharding import PartitionSpec as P

HEADS = 8
BLOCKS = 2
LANES = 128
epsilon = 1e-06
VMEM_LIMIT = 48 * 1024 * 1024

F32 = jnp.float32
BF16 = jnp.bfloat16


def tile_of(device, count):
    if count % 4:
        return device
    group, inner = device // 4, device % 4
    if group % 2:
        inner = (2, 3, 0, 1)[inner]
    return group * 4 + inner


def one_hot(sources):
    matrix = np.zeros((len(sources), len(sources)), np.float32)
    matrix[np.arange(len(sources)), np.asarray(sources)] = 1.0
    return jnp.asarray(matrix, BF16)


def shuffles(count, local, cols):
    width = cols // count
    members = count * local
    tiles = [tile_of(d, count) for d in range(count)]
    to_message = [
        m * cols + tiles[d] * width + c
        for d in range(count)
        for m in range(local)
        for c in range(width)
    ]
    to_slab = np.argsort(to_message)
    to_tile = [
        d * local * width + m * width + c
        for c in range(width)
        for d in range(count)
        for m in range(local)
    ]
    from_tile = np.argsort(to_tile)
    return one_hot(to_message), one_hot(to_tile), one_hot(from_tile), one_hot(to_slab)


def normalize(widened, gain):
    inverse = lax.rsqrt(jnp.mean(widened * widened, axis=-1, keepdims=True) + epsilon)
    return widened * inverse * gain


def gated(conv_out, channels):
    return conv_out[:, :channels] * jax.nn.sigmoid(conv_out[:, channels:])


def shuffled(matrix, rows):
    return jnp.dot(matrix, rows, preferred_element_type=F32)


def attention_rows(state, gain, wqv_t, wk, wout, members):
    count, channels = state.shape
    size = channels // HEADS
    group = LANES // size
    packed = LANES // members
    factor = float(np.log2(np.e) / np.sqrt(size))
    normed = normalize(state, gain).astype(BF16)
    keys = jnp.dot(normed, wk, preferred_element_type=F32).astype(BF16)
    qv_t = lax.dot_general(
        wqv_t, normed, (((1,), (1,)), ((), ())), preferred_element_type=F32
    ).astype(BF16)
    lane = lax.broadcasted_iota(jnp.int32, (members, LANES), 1)
    columns = []
    for j in range(count // LANES):
        span = slice(j * LANES, (j + 1) * LANES)
        pieces = []
        for q in range(channels // LANES):
            blocks = []
            for h in range(group):
                row = q * LANES + h * size
                parts = [jnp.zeros((size, LANES), BF16)] * group
                parts[h] = qv_t[row : row + size, span]
                blocks.append(jnp.concatenate(parts, axis=1))
            spread = jnp.concatenate(blocks, axis=0)
            scores = jnp.dot(
                keys[span, q * LANES : (q + 1) * LANES], spread, preferred_element_type=F32
            )
            for h in range(group):
                square = scores[:, h * LANES : (h + 1) * LANES]
                dense = square[:members]
                for k in range(1, packed):
                    dense = jnp.where(
                        lane < k * members, dense, square[k * members : (k + 1) * members]
                    )
                top = jnp.max(dense, axis=0, keepdims=True)
                expo = jnp.exp2((dense - top) * factor)
                total = jnp.sum(expo, axis=0, keepdims=True)
                if packed == 1:
                    weights = expo.astype(BF16)
                else:
                    weights = jnp.concatenate(
                        [
                            jnp.where(
                                (lane >= k * members) & (lane < (k + 1) * members), expo, 0.0
                            ).astype(BF16)
                            for k in range(packed)
                        ],
                        axis=0,
                    )
                row = channels + q * LANES + h * size
                mixed = jnp.dot(
                    qv_t[row : row + size, span], weights, preferred_element_type=F32
                )
                pieces.append((mixed * (1.0 / total)).astype(BF16))
        columns.append(jnp.concatenate(pieces, axis=0))
    attended_t = jnp.concatenate(columns, axis=1)
    update = lax.dot_general(
        attended_t, wout, (((0,), (0,)), ((), ())), preferred_element_type=F32
    )
    return state + update


def conv_slab_kernel(first, last, field_ref, gain_ref, weight_ref, order_ref, out_ref, padded):
    local, rows, cols, channels = field_ref.shape
    count = local * cols
    column = lax.broadcasted_iota(jnp.int32, (count, 1), 0) % cols

    def prepare(slot, row):
        widened = field_ref[:, row].reshape(count, channels).astype(F32)
        normed = normalize(widened, gain_ref[...])
        left = jnp.where(column == 0, 0.0, pltpu.roll(normed, 1, 0))
        right = jnp.where(column == cols - 1, 0.0, pltpu.roll(normed, count - 1, 0))
        padded[slot, 0] = left.astype(BF16)
        padded[slot, 1] = normed.astype(BF16)
        padded[slot, 2] = right.astype(BF16)

    total = last - first
    low = 1 if first == 0 else 0
    high = total + 1 if last == rows else total + 2
    if low:
        padded[0] = jnp.zeros(padded.shape[1:], BF16)
    if high < total + 2:
        padded[total + 1] = jnp.zeros(padded.shape[1:], BF16)

    def prepare_step(slot, carry):
        prepare(slot, slot + (first - 1))
        return carry

    lax.fori_loop(low, high, prepare_step, 0)

    def step(i, carry):
        taps = [padded[i + di, dj] for di in range(3) for dj in range(3)]
        conv_out = jnp.dot(
            jnp.concatenate(taps, axis=1), weight_ref[...], preferred_element_type=F32
        )
        widened = field_ref[:, first + i].reshape(count, channels).astype(F32)
        state = (widened + gated(conv_out, channels)).astype(BF16)
        moved = shuffled(order_ref[...], state)
        out_ref[:, i] = moved.reshape(out_ref.shape[0], out_ref.shape[2], channels).astype(BF16)
        return carry

    lax.fori_loop(0, total, step, 0)


def attend_kernel(
    members, arrived_ref, gain_ref, next_gain_ref, wqv_ref, wk_ref, wout_ref, order_ref,
    state_ref, normed_ref, low_ref, high_ref,
):
    channels = state_ref.shape[-1]
    count = state_ref.shape[1]
    rows = arrived_ref[:, 0].reshape(count, channels)
    state = shuffled(order_ref[...], rows)
    state = attention_rows(
        state, gain_ref[...], wqv_ref[...], wk_ref[...], wout_ref[...], members
    ).astype(BF16)
    state_ref[0] = state
    normed = normalize(state.astype(F32), next_gain_ref[...]).astype(BF16)
    normed_ref[0] = normed
    low_ref[0] = normed[:members]
    high_ref[0] = normed[count - members :]


def conv_tile_kernel(
    first, last, rows, spans, members, *refs,
):
    pieces = len(spans)
    states, normeds = refs[:pieces], refs[pieces : 2 * pieces]
    lows, highs = refs[2 * pieces : 3 * pieces], refs[3 * pieces : 4 * pieces]
    weight_ref, gain_ref, wqv_ref, wk_ref, wout_ref, order_ref, out_ref, padded, held = refs[
        4 * pieces :
    ]
    count, channels = states[0].shape[1:]
    total = last - first
    if first == 0:
        padded[0] = jnp.zeros(padded.shape[1:], BF16)
    if last == rows:
        padded[total + 1] = jnp.zeros(padded.shape[1:], BF16)
    for k, (begin, end) in enumerate(spans):
        begin_row, end_row = max(begin, first - 1), min(end, last + 1)
        for row in range(begin_row, end_row):
            slot = row - first + 1
            padded[slot, :members] = lows[k][row - begin]
            padded[slot, members : members + count] = normeds[k][row - begin]
            padded[slot, members + count :] = highs[k][row - begin]
            if first <= row < last:
                held[row - first] = states[k][row - begin]

    def step(i, carry):
        taps = [
            padded[i + di, dj * members : dj * members + count]
            for di in range(3)
            for dj in range(3)
        ]
        conv_out = jnp.dot(
            jnp.concatenate(taps, axis=1), weight_ref[...], preferred_element_type=F32
        )
        state = (held[i].astype(F32) + gated(conv_out, channels)).astype(BF16).astype(F32)
        state = attention_rows(
            state, gain_ref[...], wqv_ref[...], wk_ref[...], wout_ref[...], members
        ).astype(BF16)
        moved = shuffled(order_ref[...], state)
        out_ref[:, i] = moved.reshape(out_ref.shape[0], out_ref.shape[2], channels).astype(BF16)
        return carry

    lax.fori_loop(0, total, step, 0)


def place_kernel(arrived_ref, order_ref, *refs):
    out_ref = refs[-1]
    local, _, cols, channels = out_ref.shape
    rows = arrived_ref[:, 0].reshape(local * cols, channels)
    moved = shuffled(order_ref[...], rows)
    out_ref[:, 0] = moved.reshape(local, cols, channels).astype(BF16)


def params():
    return pltpu.CompilerParams(vmem_limit_bytes=VMEM_LIMIT)


def whole():
    return pl.BlockSpec(memory_space=pltpu.VMEM)


def body(field, norm_gain, conv_weight, qkv_weight, out_weight):
    local, rows, cols, channels = field.shape
    devices = lax.axis_size("mem")
    width = cols // devices
    members = devices * local
    count = local * cols
    block = local * width
    to_message, to_tile, from_tile, to_slab = shuffles(devices, local, cols)
    taps = conv_weight.shape[1] * conv_weight.shape[2] * channels
    conv_weight = conv_weight.reshape(BLOCKS, taps, 2 * channels)
    wk = qkv_weight[:, :, channels : 2 * channels]
    wqv_t = jnp.concatenate(
        [qkv_weight[:, :, :channels], qkv_weight[:, :, 2 * channels :]], axis=2
    ).transpose(0, 2, 1)
    gains = norm_gain.reshape(BLOCKS, 2, 1, channels)

    split_in = rows // 2 + 1
    split_out = split_in - 1
    spans_in = ((0, split_in), (split_in, rows))
    spans_out = ((0, split_out), (split_out, rows))

    def conv_slab(first, last):
        total = last - first
        return pl.pallas_call(
            functools.partial(conv_slab_kernel, first, last),
            out_shape=jax.ShapeDtypeStruct((devices, total, block, channels), BF16),
            in_specs=[whole()] * 4,
            out_specs=whole(),
            scratch_shapes=[pltpu.VMEM((total + 2, 3, count, channels), BF16)],
            compiler_params=params(),
            cost_estimate=pl.CostEstimate(
                flops=2 * total * count * taps * 2 * channels,
                bytes_accessed=2 * total * count * channels * 2,
                transcendentals=total * count * channels,
            ),
            name="conv_slab",
        )(field, gains[0, 0], conv_weight[0], to_message)

    def exchange(messages):
        return lax.all_to_all(messages, "mem", split_axis=0, concat_axis=0, tiled=True)

    def attend(arrived):
        total = arrived.shape[1]
        fixed = lambda shape: pl.BlockSpec(shape, lambda i: (0,) * len(shape))
        per_row = lambda n: pl.BlockSpec((1, n, channels), lambda i: (i, 0, 0))
        return pl.pallas_call(
            functools.partial(attend_kernel, members),
            grid=(total,),
            out_shape=[
                jax.ShapeDtypeStruct((total, count, channels), BF16),
                jax.ShapeDtypeStruct((total, count, channels), BF16),
                jax.ShapeDtypeStruct((total, members, channels), BF16),
                jax.ShapeDtypeStruct((total, members, channels), BF16),
            ],
            in_specs=[
                pl.BlockSpec((devices, 1, block, channels), lambda i: (0, i, 0, 0)),
                fixed((1, channels)),
                fixed((1, channels)),
                fixed((2 * channels, channels)),
                fixed((channels, channels)),
                fixed((channels, channels)),
                fixed((count, count)),
            ],
            out_specs=[per_row(count), per_row(count), per_row(members), per_row(members)],
            compiler_params=params(),
            cost_estimate=pl.CostEstimate(
                flops=2 * total * count * channels * 6 * channels,
                bytes_accessed=4 * total * count * channels * 2,
                transcendentals=total * count * members * HEADS,
            ),
            name="attend",
        )(arrived, gains[0, 1], gains[1, 0], wqv_t[0], wk[0], out_weight[0], to_tile)

    tiles = [tile_of(d, devices) for d in range(devices)]
    owner = {t: d for d, t in enumerate(tiles)}
    rightward = [(owner[t], owner[t + 1]) for t in range(devices - 1)]
    leftward = [(target, source) for source, target in rightward]

    def conv_tile(first, last, spans, parts):
        total = last - first
        operands = [p[k] for k in range(4) for p in parts]
        return pl.pallas_call(
            functools.partial(conv_tile_kernel, first, last, rows, spans, members),
            out_shape=jax.ShapeDtypeStruct((devices, total, block, channels), BF16),
            in_specs=[whole()] * (len(operands) + 6),
            out_specs=whole(),
            scratch_shapes=[
                pltpu.VMEM((total + 2, count + 2 * members, channels), BF16),
                pltpu.VMEM((total, count, channels), BF16),
            ],
            compiler_params=params(),
            cost_estimate=pl.CostEstimate(
                flops=2 * total * count * channels * (6 * channels + 2 * taps),
                bytes_accessed=4 * total * count * channels * 2,
                transcendentals=total * count * members * HEADS,
            ),
            name="conv_tile",
        )(
            *operands, conv_weight[1], gains[1, 1], wqv_t[1], wk[1], out_weight[1], from_tile,
        )

    def place(first, last, arrived, earlier):
        total = last - first
        in_specs = [
            pl.BlockSpec((devices, 1, block, channels), lambda i: (0, i, 0, 0)),
            pl.BlockSpec((count, count), lambda i: (0, 0)),
        ]
        operands = [arrived, to_slab]
        aliases = {}
        if earlier is not None:
            in_specs.append(pl.BlockSpec(memory_space=pl.ANY))
            operands.append(earlier)
            aliases = {2: 0}
        return pl.pallas_call(
            place_kernel,
            grid=(total,),
            out_shape=jax.ShapeDtypeStruct((local, rows, cols, channels), BF16),
            in_specs=in_specs,
            out_specs=pl.BlockSpec(
                (local, 1, cols, channels), lambda i: (0, first + i, 0, 0)
            ),
            input_output_aliases=aliases,
            compiler_params=params(),
            cost_estimate=pl.CostEstimate(
                flops=2 * total * count * count * channels,
                bytes_accessed=2 * total * count * channels * 2,
                transcendentals=0,
            ),
            name="place",
        )(*operands)

    arrived = [exchange(conv_slab(*span)) for span in spans_in]
    parts = []
    result = None
    for k, (first, last) in enumerate(spans_out):
        state, normed, low, high = attend(arrived[k])
        from_left = lax.ppermute(high, "mem", rightward)
        from_right = lax.ppermute(low, "mem", leftward)
        parts.append((state, normed, from_left, from_right))
    returned = []
    for k, (first, last) in enumerate(spans_out):
        lo = 0 if k == 0 else k - 1
        spans = spans_in[lo : k + 1]
        messages = conv_tile(first, last, spans, parts[lo : k + 1])
        returned.append(exchange(messages))
    for span, arrival in zip(spans_out, returned):
        result = place(*span, arrival, result)
    return result


def solution(mesh):
    return jax.shard_map(
        body,
        mesh=mesh,
        in_specs=(P(("grp", "mem"), None, None, None), P(), P(), P(), P()),
        out_specs=P(("grp", "mem"), None, None, None),
        check_vma=False,
    )
```

profile of v0, /device:TPU:15, one launch (start us, length us, event | category | flops | bytes accessed | tf_op | source)
XLA Modules:
  0.0 195.9 jit_solution(5980706402108386217)
XLA Ops:
  0.0 0.8 slice_bitcast_fusion.6
  0.8 4.4 %fusion = (bf16[1,3,3,256,512]{4,3,2,1,0:T(8,128)(2,1)}, bf16[1,3,3,256,512]{4,3,2,1,0:T(8,128)(2,1)S(1)}) fusion(bf16[2,3,3,256,512]{4,3,2,1,0:T(8,128)(2,1)} %param.11), kind=kLoop, calls=%fused_computation.11 | loop fusion | bytes 9437184 | tf_op jit(solution)/shard_map/slice | solution.py:351
  5.2 10.8 %conv_slab.2 = bf16[16,9,16,256]{3,2,1,0:T(8,128)(2,1)S(1)} custom-call(bf16[4,16,64,256]{3,2,1,0:T(8,128)(2,1)S(1)} %copy-done.3, f32[1,256]{1,0:T(1,128)S(1)} %get-tuple-element.34.gain_ref, bf16[2304,512]{1,0:T(8,128)(2,1)S(1)} %bitcast.25, bf16[256,256]{1,0:T(8,128)(2,1)S(1)} %copy-done.11), custom_call_target="tpu_custom_call" | custom-call | flops 5435817984 | bytes 2359296 | tf_op jit(solution)/shard_map/conv_slab/pallas_call | solution.py:276
  16.0 1.0 copy-done
  17.1 6.6 %all-to-all-start = ((bf16[16,9,16,256]{3,2,1,0:T(8,128)(2,1)}), bf16[16,9,16,256]{3,2,1,0:T(8,128)(2,1)S(1)}, u32[]{:S(2)}, u32[]{:S(2)}) async-start(bf16[16,9,16,256]{3,2,1,0:T(8,128)(2,1)} %copy-done), calls=%async_computation | async-start | bytes 2359296 | tf_op jit(solution)/shard_map/all_to_all | solution.py:292
  23.6 1.6 copy-done.4
  25.2 0.9 copy-done.12
  26.1 8.5 %conv_slab.3 = bf16[16,7,16,256]{3,2,1,0:T(8,128)(2,1)S(1)} custom-call(bf16[4,16,64,256]{3,2,1,0:T(8,128)(2,1)S(1)} %copy-done.4, f32[1,256]{1,0:T(1,128)S(1)} %get-tuple-element.34.gain_ref, bf16[2304,512]{1,0:T(8,128)(2,1)S(1)} %bitcast.26, bf16[256,256]{1,0:T(8,128)(2,1)S(1)} %copy-done.12), custom_call_target="tpu_custom_call" | custom-call | flops 4227858432 | bytes 1835008 | tf_op jit(solution)/shard_map/conv_slab/pallas_call | solution.py:276
  34.6 1.0 copy-done.1
  35.6 15.8 %all-to-all-done.arrived_ref = bf16[16,9,16,256]{3,2,1,0:T(8,128)(2,1)S(1)} async-done(((bf16[16,9,16,256]{3,2,1,0:T(8,128)(2,1)}), bf16[16,9,16,256]{3,2,1,0:T(8,128)(2,1)S(1)}, u32[]{:S(2)}, u32[]{:S(2)}) %all-to-all-start) | async-done | bytes 1179680 | tf_op jit(solution)/shard_map/all_to_all | solution.py:292
  51.4 4.9 %all-to-all-start.1 = ((bf16[16,7,16,256]{3,2,1,0:T(8,128)(2,1)}), bf16[16,7,16,256]{3,2,1,0:T(8,128)(2,1)S(1)}, u32[]{:S(2)}, u32[]{:S(2)}) async-start(bf16[16,7,16,256]{3,2,1,0:T(8,128)(2,1)} %copy-done.1), calls=%async_computation.1 | async-start | bytes 1835008 | tf_op jit(solution)/shard_map/all_to_all | solution.py:292
  56.6 1.1 slice_bitcast_fusion.2
  57.8 15.6 %attend.2 = (bf16[9,256,256]{2,1,0:T(8,128)(2,1)S(1)}, bf16[9,256,256]{2,1,0:T(8,128)(2,1)S(1)}, bf16[9,64,256]{2,1,0:T(8,128)(2,1)S(1)}, bf16[9,64,256]{2,1,0:T(8,128)(2,1)S(1)}) custom-call(bf16[16,9,16,256]{3,2,1,0:T(8,128)(2,1)S(1)} %all-to-all-done.arrived_ref, f32[1,256]{1,0:T(1,128)S(1)} %get-tuple-element.33.gain_ref, ...), custom_call_target="tpu_custom_call" | custom-call | flops 1811939328 | bytes 4718592 | tf_op jit(solution)/shard_map/attend/pallas_call | solution.py:298
  73.4 2.4 %collective-permute-start = (bf16[9,64,256]{2,1,0:T(8,128)(2,1)S(1)}, bf16[9,64,256]{2,1,0:T(8,128)(2,1)S(1)}, u32[]{:S(2)}, u32[]{:S(2)}) collective-permute-start(bf16[9,64,256]{2,1,0:T(8,128)(2,1)S(1)} %get-tuple-element.17), channel_id=1, source_target_pairs={{0,1},{1,2},{2,3},{3,6},{6,7},{7,4},{4,5},{5,8},{8,9},{9,10},{10,1... | collective-permute-start | bytes 884744 | tf_op jit(solution)/shard_map/ppermute | solution.py:389
  75.9 1.9 collective-permute-start.2
  77.8 1.9 collective-permute-done.refs_4_.refs_2_
  79.7 4.2 %collective-permute-done.2.refs_6_.refs_3_ = bf16[9,64,256]{2,1,0:T(8,128)(2,1)S(1)} collective-permute-done((bf16[9,64,256]{2,1,0:T(8,128)(2,1)S(1)}, bf16[9,64,256]{2,1,0:T(8,128)(2,1)S(1)}, u32[]{:S(2)}, u32[]{:S(2)}) %collective-permute-start.2) | collective-permute-done | bytes 294944 | tf_op jit(solution)/shard_map/ppermute | solution.py:390
  83.9 21.7 %conv_tile.3 = bf16[16,8,16,256]{3,2,1,0:T(8,128)(2,1)} custom-call(bf16[9,256,256]{2,1,0:T(8,128)(2,1)S(1)} %get-tuple-element.13.refs_0_, bf16[9,256,256]{2,1,0:T(8,128)(2,1)S(1)} %get-tuple-element.15.refs_2_.refs_1_, bf16[9,64,256]{2,1,0:T(8,128)(2,1)S(1)} %collective-permute-done.refs_4_.refs_2_, ...), custom_call_target="tpu_custom_call" | custom-call | flops 6442450944 | bytes 4194304 | tf_op jit(solution)/shard_map/conv_tile/pallas_call | solution.py:334
  106.3 1.0 copy-done.13
  107.3 1.0 copy-done.15
  108.4 5.8 %all-to-all-start.3 = ((bf16[16,8,16,256]{3,2,1,0:T(8,128)(2,1)}), bf16[16,8,16,256]{3,2,1,0:T(8,128)(2,1)S(1)}, u32[]{:S(2)}, u32[]{:S(2)}) async-start(bf16[16,8,16,256]{3,2,1,0:T(8,128)(2,1)} %conv_tile.3), calls=%async_computation.3 | async-start | bytes 2097152 | tf_op jit(solution)/shard_map/all_to_all | solution.py:292
  114.1 0.9 copy-done.10
  115.0 12.1 %attend.3 = (bf16[7,256,256]{2,1,0:T(8,128)(2,1)S(1)}, bf16[7,256,256]{2,1,0:T(8,128)(2,1)S(1)}, bf16[7,64,256]{2,1,0:T(8,128)(2,1)S(1)}, bf16[7,64,256]{2,1,0:T(8,128)(2,1)S(1)}) custom-call(bf16[16,7,16,256]{3,2,1,0:T(8,128)(2,1)S(1)} %all-to-all-done.1.arrived_ref, f32[1,256]{1,0:T(1,128)S(1)} %get-tuple-element.33.gain_ref, ...), custom_call_target="tpu_custom_call" | custom-call | flops 1409286144 | bytes 3670016 | tf_op jit(solution)/shard_map/attend/pallas_call | solution.py:298
  127.2 2.4 %collective-permute-start.1 = (bf16[7,64,256]{2,1,0:T(8,128)(2,1)S(1)}, bf16[7,64,256]{2,1,0:T(8,128)(2,1)S(1)}, u32[]{:S(2)}, u32[]{:S(2)}) collective-permute-start(bf16[7,64,256]{2,1,0:T(8,128)(2,1)S(1)} %get-tuple-element.18), channel_id=1, source_target_pairs={{0,1},{1,2},{2,3},{3,6},{6,7},{7,4},{4,5},{5,8},{8,9},{9,10},{10,1... | collective-permute-start | bytes 688136 | tf_op jit(solution)/shard_map/ppermute | solution.py:389
  129.6 1.9 collective-permute-start.3
  131.6 2.4 %collective-permute-done.1.refs_5_ = bf16[7,64,256]{2,1,0:T(8,128)(2,1)S(1)} collective-permute-done((bf16[7,64,256]{2,1,0:T(8,128)(2,1)S(1)}, bf16[7,64,256]{2,1,0:T(8,128)(2,1)S(1)}, u32[]{:S(2)}, u32[]{:S(2)}) %collective-permute-start.1) | collective-permute-done | bytes 229408 | tf_op jit(solution)/shard_map/ppermute | solution.py:389
  134.0 3.0 %collective-permute-done.3.refs_7_ = bf16[7,64,256]{2,1,0:T(8,128)(2,1)S(1)} collective-permute-done((bf16[7,64,256]{2,1,0:T(8,128)(2,1)S(1)}, bf16[7,64,256]{2,1,0:T(8,128)(2,1)S(1)}, u32[]{:S(2)}, u32[]{:S(2)}) %collective-permute-start.3) | collective-permute-done | bytes 229408 | tf_op jit(solution)/shard_map/ppermute | solution.py:390
  137.0 22.1 %conv_tile.2 = bf16[16,8,16,256]{3,2,1,0:T(8,128)(2,1)} custom-call(bf16[9,256,256]{2,1,0:T(8,128)(2,1)S(1)} %copy-done.14, bf16[7,256,256]{2,1,0:T(8,128)(2,1)S(1)} %get-tuple-element.14.refs_1_, bf16[9,256,256]{2,1,0:T(8,128)(2,1)} %copy-done.15, bf16[7,256,256]{2,1,0:T(8,128)(2,1)S(1)} %get-tuple-element.16.refs_3_, ...), custom_call_target="tpu_custom_call" | custom-call | flops 6442450944 | bytes 4194304 | tf_op jit(solution)/shard_map/conv_tile/pallas_call | solution.py:334
  159.1 8.3 %all-to-all-start.2 = ((bf16[16,8,16,256]{3,2,1,0:T(8,128)(2,1)}), bf16[16,8,16,256]{3,2,1,0:T(8,128)(2,1)S(1)}, u32[]{:S(2)}, u32[]{:S(2)}) async-start(bf16[16,8,16,256]{3,2,1,0:T(8,128)(2,1)} %conv_tile.2), calls=%async_computation.2 | async-start | bytes 2097152 | tf_op jit(solution)/shard_map/all_to_all | solution.py:292
  167.3 3.7 %place.2.refs_0_ = bf16[4,16,64,256]{3,2,1,0:T(8,128)(2,1)} custom-call(bf16[16,8,16,256]{3,2,1,0:T(8,128)(2,1)S(1)} %all-to-all-done.3.arrived_ref, bf16[256,256]{1,0:T(8,128)(2,1)S(1)} %copy-done.2), custom_call_target="tpu_custom_call" | custom-call | flops 268435456 | bytes 2097152 | tf_op jit(solution)/shard_map/place/pallas_call | solution.py:366
  171.0 21.2 %all-to-all-done.2.arrived_ref = bf16[16,8,16,256]{3,2,1,0:T(8,128)(2,1)S(1)} async-done(((bf16[16,8,16,256]{3,2,1,0:T(8,128)(2,1)}), bf16[16,8,16,256]{3,2,1,0:T(8,128)(2,1)S(1)}, u32[]{:S(2)}, u32[]{:S(2)}) %all-to-all-start.2) | async-done | bytes 1048608 | tf_op jit(solution)/shard_map/all_to_all | solution.py:292
  192.2 3.6 %place.3 = bf16[4,16,64,256]{3,2,1,0:T(8,128)(2,1)} custom-call(bf16[16,8,16,256]{3,2,1,0:T(8,128)(2,1)S(1)} %all-to-all-done.2.arrived_ref, bf16[256,256]{1,0:T(8,128)(2,1)S(1)} %copy-done.2, bf16[4,16,64,256]{3,2,1,0:T(8,128)(2,1)} %place.2.refs_0_), custom_call_target="tpu_custom_call", output_to_operand_aliasing={{}: (2, {})} | custom-call | flops 268435456 | bytes 2097152 | tf_op jit(solution)/shard_map/place/pallas_call | solution.py:366
  (34 shorter events, 1.1 us)
Async XLA Ops:
  0.8 4.4 %copy-start.3 = (bf16[4,16,64,256]{3,2,1,0:T(8,128)(2,1)S(1)}, bf16[4,16,64,256]{3,2,1,0:T(8,128)(2,1)}, u32[]{:S(2)}) copy-start(bf16[4,16,64,256]{3,2,1,0:T(8,128)(2,1)} %field_ref.3) | copy-start | bytes 6291460
  0.8 4.4 %copy-start.11 = (bf16[256,256]{1,0:T(8,128)(2,1)S(1)}, bf16[256,256]{1,0:T(8,128)(2,1)}, u32[]{:S(2)}) copy-start(bf16[256,256]{1,0:T(8,128)(2,1)} %constant.8.clone.order_ref) | copy-start | bytes 393220
  16.0 1.0 copy-start
  17.1 34.3 %all-to-all-start = ((bf16[16,9,16,256]{3,2,1,0:T(8,128)(2,1)}), bf16[16,9,16,256]{3,2,1,0:T(8,128)(2,1)S(1)}, u32[]{:S(2)}, u32[]{:S(2)}) async-start(bf16[16,9,16,256]{3,2,1,0:T(8,128)(2,1)} %copy-done), calls=%async_computation | async-start | bytes 2359296 | tf_op jit(solution)/shard_map/all_to_all | solution.py:292
  23.6 1.6 copy-start.4
  25.2 0.9 copy-start.12
  34.6 1.0 copy-start.1
  35.6 20.7 %copy-start.16 = (bf16[2,256,768]{2,1,0:T(8,128)(2,1)S(1)}, bf16[2,256,768]{2,1,0:T(8,128)(2,1)}, u32[]{:S(2)}) copy-start(bf16[2,256,768]{2,1,0:T(8,128)(2,1)} %param.12) | copy-start | bytes 2359300
  51.4 57.0 %all-to-all-start.1 = ((bf16[16,7,16,256]{3,2,1,0:T(8,128)(2,1)}), bf16[16,7,16,256]{3,2,1,0:T(8,128)(2,1)S(1)}, u32[]{:S(2)}, u32[]{:S(2)}) async-start(bf16[16,7,16,256]{3,2,1,0:T(8,128)(2,1)} %copy-done.1), calls=%async_computation.1 | async-start | bytes 1835008 | tf_op jit(solution)/shard_map/all_to_all | solution.py:292
  56.3 1.5 copy-start.9
  57.8 26.1 %copy-start.7 = (bf16[256,256]{1,0:T(8,128)(2,1)S(1)}, bf16[256,256]{1,0:T(8,128)(2,1)}, u32[]{:S(2)}) copy-start(bf16[256,256]{1,0:T(8,128)(2,1)} %constant.10.clone.refs_13_.refs_9_) | copy-start | bytes 393220
  73.4 6.3 %collective-permute-start = (bf16[9,64,256]{2,1,0:T(8,128)(2,1)S(1)}, bf16[9,64,256]{2,1,0:T(8,128)(2,1)S(1)}, u32[]{:S(2)}, u32[]{:S(2)}) collective-permute-start(bf16[9,64,256]{2,1,0:T(8,128)(2,1)S(1)} %get-tuple-element.17), channel_id=1, source_target_pairs={{0,1},{1,2},{2,3},{3,6},{6,7},{7,4},{4,5},{5,8},{8,9},{9,10},{10,1... | collective-permute-start | bytes 884744 | tf_op jit(solution)/shard_map/ppermute | solution.py:389
  75.9 8.0 %collective-permute-start.2 = (bf16[9,64,256]{2,1,0:T(8,128)(2,1)S(1)}, bf16[9,64,256]{2,1,0:T(8,128)(2,1)S(1)}, u32[]{:S(2)}, u32[]{:S(2)}) collective-permute-start(bf16[9,64,256]{2,1,0:T(8,128)(2,1)S(1)} %get-tuple-element.19), channel_id=1, source_target_pairs={{1,0},{2,1},{3,2},{6,3},{7,6},{4,7},{5,4},{8,5},{9,8},{10,9},{11,1... | collective-permute-start | bytes 884744 | tf_op jit(solution)/shard_map/ppermute | solution.py:390
  105.6 0.7 copy-start.5
  106.3 1.0 copy-start.13
  107.3 1.0 copy-start.15
  108.4 50.7 %all-to-all-start.3 = ((bf16[16,8,16,256]{3,2,1,0:T(8,128)(2,1)}), bf16[16,8,16,256]{3,2,1,0:T(8,128)(2,1)S(1)}, u32[]{:S(2)}, u32[]{:S(2)}) async-start(bf16[16,8,16,256]{3,2,1,0:T(8,128)(2,1)} %conv_tile.3), calls=%async_computation.3 | async-start | bytes 2097152 | tf_op jit(solution)/shard_map/all_to_all | solution.py:292
  114.1 0.9 copy-start.10
  115.0 21.9 %copy-start.6 = (bf16[9,64,256]{2,1,0:T(8,128)(2,1)S(1)}, bf16[9,64,256]{2,1,0:T(8,128)(2,1)}, u32[]{:S(2)}) copy-start(bf16[9,64,256]{2,1,0:T(8,128)(2,1)} %copy-done.5) | copy-start | bytes 884740
  115.0 21.9 %copy-start.8 = (bf16[256,256]{1,0:T(8,128)(2,1)S(1)}, bf16[256,256]{1,0:T(8,128)(2,1)}, u32[]{:S(2)}) copy-start(bf16[256,256]{1,0:T(8,128)(2,1)} %constant.10.clone.refs_13_.refs_9_) | copy-start | bytes 393220
  115.0 21.9 %copy-start.14 = (bf16[9,256,256]{2,1,0:T(8,128)(2,1)S(1)}, bf16[9,256,256]{2,1,0:T(8,128)(2,1)}, u32[]{:S(2)}) copy-start(bf16[9,256,256]{2,1,0:T(8,128)(2,1)} %copy-done.13) | copy-start | bytes 3538948
  127.2 6.8 %collective-permute-start.1 = (bf16[7,64,256]{2,1,0:T(8,128)(2,1)S(1)}, bf16[7,64,256]{2,1,0:T(8,128)(2,1)S(1)}, u32[]{:S(2)}, u32[]{:S(2)}) collective-permute-start(bf16[7,64,256]{2,1,0:T(8,128)(2,1)S(1)} %get-tuple-element.18), channel_id=1, source_target_pairs={{0,1},{1,2},{2,3},{3,6},{6,7},{7,4},{4,5},{5,8},{8,9},{9,10},{10,1... | collective-permute-start | bytes 688136 | tf_op jit(solution)/shard_map/ppermute | solution.py:389
  129.6 7.3 %collective-permute-start.3 = (bf16[7,64,256]{2,1,0:T(8,128)(2,1)S(1)}, bf16[7,64,256]{2,1,0:T(8,128)(2,1)S(1)}, u32[]{:S(2)}, u32[]{:S(2)}) collective-permute-start(bf16[7,64,256]{2,1,0:T(8,128)(2,1)S(1)} %get-tuple-element.20), channel_id=1, source_target_pairs={{1,0},{2,1},{3,2},{6,3},{7,6},{4,7},{5,4},{8,5},{9,8},{10,9},{11,1... | collective-permute-start | bytes 688136 | tf_op jit(solution)/shard_map/ppermute | solution.py:390
  159.1 8.3 %copy-start.2 = (bf16[256,256]{1,0:T(8,128)(2,1)S(1)}, bf16[256,256]{1,0:T(8,128)(2,1)}, u32[]{:S(2)}) copy-start(bf16[256,256]{1,0:T(8,128)(2,1)} %constant.11.clone.order_ref) | copy-start | bytes 393220
  159.1 33.1 %all-to-all-start.2 = ((bf16[16,8,16,256]{3,2,1,0:T(8,128)(2,1)}), bf16[16,8,16,256]{3,2,1,0:T(8,128)(2,1)S(1)}, u32[]{:S(2)}, u32[]{:S(2)}) async-start(bf16[16,8,16,256]{3,2,1,0:T(8,128)(2,1)} %conv_tile.2), calls=%async_computation.2 | async-start | bytes 2097152 | tf_op jit(solution)/shard_map/all_to_all | solution.py:292
where the time goes:
time: 197 us; the launch traced here: 196 us
  Pallas kernels  98.1 us (50%)
  waiting for transfers between devices  48.6 us (25%)
  starting transfers between devices  34.2 us (17%)
  local copies, waits for them, and re-layouts  14.8 us (8%)
    pallas_call x2, Pallas kernels, conv_tile(): pl.pallas_call(functools.partial(conv_tile_kernel, first, last, rows, spa...  43.8 us
    all_to_all x4, waiting for transfers between devices, exchange(): lax.all_to_all(messages, 'mem', split_axis=0, concat_axis=0, tiled=True)  37 us
    pallas_call x2, Pallas kernels, attend(): pl.pallas_call(functools.partial(attend_kernel, members), grid=(total,),...  27.7 us
    all_to_all x4, starting transfers between devices, exchange(): lax.all_to_all(messages, 'mem', split_axis=0, concat_axis=0, tiled=True)  25.5 us
    pallas_call x2, Pallas kernels, conv_slab(): pl.pallas_call(functools.partial(conv_slab_kernel, first, last), out_shap...  19.3 us
    unnamed x36, local copies, waits for them, and re-layouts  8.4 us
    pallas_call x2, Pallas kernels, place(): pl.pallas_call(place_kernel, grid=(total,), out_shape=jax.ShapeDtypeStruc...  7.3 us
    ppermute x2, waiting for transfers between devices, body(): from_right = lax.ppermute(low, 'mem', leftward)  7.17 us
  transfers between devices with their start and end apart: 8, of which 6 were waited for; matrix products, arithmetic and copies ran while one was open for 1% of the time, Pallas kernels for 43%

commit v1 on v0

v1 whole, which is shorter than its diff:
```python
import functools

import jax
import jax.numpy as jnp
import numpy as np
from jax import lax
from jax.experimental import pallas as pl
from jax.experimental.pallas import tpu as pltpu
from jax.sharding import PartitionSpec as P

HEADS = 8
BLOCKS = 2
LANES = 128
epsilon = 1e-06
VMEM_LIMIT = 60 * 1024 * 1024
UNROLL = 4

F32 = jnp.float32
BF16 = jnp.bfloat16


def tile_of(device, count):
    if count % 4:
        return device
    group, inner = device // 4, device % 4
    if group % 2:
        inner = (2, 3, 0, 1)[inner]
    return group * 4 + inner


def one_hot(sources):
    matrix = np.zeros((len(sources), len(sources)), np.float32)
    matrix[np.arange(len(sources)), np.asarray(sources)] = 1.0
    return jnp.asarray(matrix, BF16)


def shuffles(count, local, cols):
    width = cols // count
    members = count * local
    tiles = [tile_of(d, count) for d in range(count)]
    to_message = [
        m * cols + tiles[d] * width + c
        for d in range(count)
        for m in range(local)
        for c in range(width)
    ]
    to_slab = np.argsort(to_message)
    to_tile = [
        d * local * width + m * width + c
        for c in range(width)
        for d in range(count)
        for m in range(local)
    ]
    from_tile = np.argsort(to_tile)
    return one_hot(to_message), one_hot(to_tile), one_hot(from_tile), one_hot(to_slab)


def normalize(widened, gain):
    inverse = lax.rsqrt(jnp.mean(widened * widened, axis=-1, keepdims=True) + epsilon)
    return widened * inverse * gain


def gated(conv_out, channels):
    return conv_out[:, :channels] * jax.nn.sigmoid(conv_out[:, channels:])


def shuffled(matrix, rows):
    return jnp.dot(matrix, rows, preferred_element_type=F32)


def groups_of(total, most=UNROLL):
    pieces = -(-total // most)
    edges = [total * k // pieces for k in range(pieces + 1)]
    return [(edges[k], edges[k + 1]) for k in range(pieces)]


def attention_rows(state, gain, wqv_t, wk, wout, members, count):
    total, channels = state.shape
    size = channels // HEADS
    group = LANES // size
    packed = LANES // members
    factor = float(np.log2(np.e) / np.sqrt(size))
    normed = normalize(state, gain).astype(BF16)
    keys = jnp.dot(normed, wk, preferred_element_type=F32).astype(BF16)
    qv_t = lax.dot_general(
        wqv_t, normed, (((1,), (1,)), ((), ())), preferred_element_type=F32
    ).astype(BF16)
    lane = lax.broadcasted_iota(jnp.int32, (members, LANES), 1)
    masks = [
        ((lane >= k * members) & (lane < (k + 1) * members)).astype(F32).astype(BF16)
        for k in range(packed)
    ]
    spans = [slice(j * LANES, (j + 1) * LANES) for j in range(total // LANES)]
    quads = range(channels // LANES)
    scores = {}
    for j, span in enumerate(spans):
        for q in quads:
            blocks = []
            for h in range(group):
                row = q * LANES + h * size
                parts = [jnp.zeros((size, LANES), BF16)] * group
                parts[h] = qv_t[row : row + size, span]
                blocks.append(jnp.concatenate(parts, axis=1))
            scores[j, q] = jnp.dot(
                keys[span, q * LANES : (q + 1) * LANES],
                jnp.concatenate(blocks, axis=0),
                preferred_element_type=F32,
            )
    weights = {}
    for j in range(len(spans)):
        for q in quads:
            for h in range(group):
                square = scores[j, q][:, h * LANES : (h + 1) * LANES]
                dense = square[:members]
                for k in range(1, packed):
                    dense = jnp.where(
                        lane < k * members, dense, square[k * members : (k + 1) * members]
                    )
                top = jnp.max(dense, axis=0, keepdims=True)
                expo = jnp.exp2((dense - top) * factor)
                inverse = 1.0 / jnp.sum(expo, axis=0, keepdims=True)
                spread = expo.astype(BF16)
                if packed > 1:
                    spread = jnp.concatenate([spread * mask for mask in masks], axis=0)
                weights[j, q, h] = spread, inverse
    columns = []
    for j, span in enumerate(spans):
        pieces = []
        for q in quads:
            for h in range(group):
                spread, inverse = weights[j, q, h]
                row = channels + q * LANES + h * size
                mixed = jnp.dot(
                    qv_t[row : row + size, span], spread, preferred_element_type=F32
                )
                pieces.append((mixed * inverse).astype(BF16))
        columns.append(jnp.concatenate(pieces, axis=0))
    attended_t = jnp.concatenate(columns, axis=1)
    update = lax.dot_general(
        attended_t, wout, (((0,), (0,)), ((), ())), preferred_element_type=F32
    )
    return state + update


class Copies:
    def __init__(self, semaphores):
        self.semaphores = semaphores
        self.used = 0

    def start(self, source, target):
        copy = pltpu.make_async_copy(source, target, self.semaphores.at[self.used])
        self.used += 1
        copy.start()
        return copy


def wait_all(copies):
    for copy in copies:
        copy.wait()


def split_weights(qkv, wqv_t):
    channels = qkv.shape[0]
    wqv_t[:channels] = qkv[:, :channels].T
    wqv_t[channels:] = qkv[:, 2 * channels :].T


def conv_slab_kernel(
    layer, first, last, field_hbm, gain_hbm, weight_hbm, order_hbm, out_hbm,
    field, gain, weight, order, padded, out, semaphores,
):
    local, rows, cols, channels = field_hbm.shape
    count = local * cols
    copies = Copies(semaphores)
    low, high = max(first - 1, 0), min(last + 1, rows)
    inputs = [
        copies.start(gain_hbm, gain),
        copies.start(field_hbm.at[:, low:high], field),
    ]
    late = [
        copies.start(weight_hbm.at[layer], weight),
        copies.start(order_hbm, order),
    ]
    column = lax.broadcasted_iota(jnp.int32, (count, 1), 0) % cols
    zeros = jnp.zeros(padded.shape[1:], BF16)
    if first == 0:
        padded[0] = zeros
    if last == rows:
        padded[last - first + 1] = zeros
    wait_all(inputs)
    gain_row = gain[layer, 0:1]

    def prepare(row):
        widened = field[:, row - low].reshape(count, channels).astype(F32)
        normed = normalize(widened, gain_row)
        left = jnp.where(column == 0, 0.0, pltpu.roll(normed, 1, 0))
        right = jnp.where(column == cols - 1, 0.0, pltpu.roll(normed, count - 1, 0))
        slot = row - first + 1
        padded[slot, 0] = left.astype(BF16)
        padded[slot, 1] = normed.astype(BF16)
        padded[slot, 2] = right.astype(BF16)

    ready = low
    outputs = []
    for k, (begin, end) in enumerate(groups_of(last - first)):
        needed = min(first + end + 1, rows)
        for row in range(ready, needed):
            prepare(row)
        ready = needed
        if k == 0:
            wait_all(late)
        taps = [
            jnp.concatenate(
                [padded[i + di, dj] for di in range(3) for dj in range(3)], axis=1
            )
            for i in range(begin, end)
        ]
        conv_out = jnp.dot(
            jnp.concatenate(taps, axis=0),
            weight[...].reshape(9 * channels, 2 * channels),
            preferred_element_type=F32,
        )
        update = gated(conv_out, channels)
        for i in range(begin, end):
            widened = field[:, first + i - low].reshape(count, channels).astype(F32)
            part = update[(i - begin) * count : (i - begin + 1) * count]
            moved = shuffled(order[...], (widened + part).astype(BF16))
            out[:, i] = moved.reshape(out.shape[0], out.shape[2], channels).astype(BF16)
        outputs.append(copies.start(out.at[:, begin:end], out_hbm.at[:, begin:end]))
    wait_all(outputs)


def attend_kernel(
    layer, members, arrived_hbm, gain_hbm, qkv_hbm, wout_hbm, order_hbm,
    state_hbm, normed_hbm, low_hbm, high_hbm,
    arrived, gain, qkv, wqv_t, wout, order, state, normed, semaphores,
):
    total, count, channels = state.shape
    groups = groups_of(total)
    copies = Copies(semaphores)
    inputs = [
        copies.start(qkv_hbm.at[layer], qkv),
        copies.start(gain_hbm, gain),
        copies.start(order_hbm, order),
        copies.start(wout_hbm.at[layer], wout),
    ]
    rows_in = [
        copies.start(arrived_hbm.at[:, begin:end], arrived.at[:, begin:end])
        for begin, end in groups
    ]
    wait_all(inputs)
    split_weights(qkv, wqv_t)
    outputs = []
    for (begin, end), copy in zip(groups, rows_in):
        copy.wait()
        joined = jnp.concatenate(
            [
                shuffled(order[...], arrived[:, i].reshape(count, channels))
                for i in range(begin, end)
            ],
            axis=0,
        )
        joined = attention_rows(
            joined, gain[layer, 1:2], wqv_t[...], qkv[:, channels : 2 * channels], wout[...],
            members, count,
        ).astype(BF16)
        following = normalize(joined.astype(F32), gain[layer + 1, 0:1]).astype(BF16)
        for i in range(begin, end):
            span = slice((i - begin) * count, (i - begin + 1) * count)
            state[i] = joined[span]
            normed[i] = following[span]
        part = slice(begin, end)
        outputs += [
            copies.start(state.at[part], state_hbm.at[part]),
            copies.start(normed.at[part], normed_hbm.at[part]),
            copies.start(normed.at[part, :members], low_hbm.at[part]),
            copies.start(normed.at[part, count - members :], high_hbm.at[part]),
        ]
    wait_all(outputs)


def conv_tile_kernel(layer, first, last, rows, spans, members, *refs):
    pieces = len(spans)
    states, normeds = refs[:pieces], refs[pieces : 2 * pieces]
    lows, highs = refs[2 * pieces : 3 * pieces], refs[3 * pieces : 4 * pieces]
    (
        weight_hbm, gain_hbm, qkv_hbm, wout_hbm, order_hbm, out_hbm,
        padded, held, weight, gain, qkv, wqv_t, wout, order, out, semaphores,
    ) = refs[4 * pieces :]
    total, count, channels = held.shape
    copies = Copies(semaphores)
    inputs = []
    for k, (begin, end) in enumerate(spans):
        lo, hi = max(begin, first - 1), min(end, last + 1)
        source, slots = slice(lo - begin, hi - begin), slice(lo - first + 1, hi - first + 1)
        inputs += [
            copies.start(normeds[k].at[source], padded.at[slots, members : members + count]),
            copies.start(lows[k].at[source], padded.at[slots, :members]),
            copies.start(highs[k].at[source], padded.at[slots, members + count :]),
        ]
    inputs.append(copies.start(weight_hbm.at[layer], weight))
    late = [
        copies.start(qkv_hbm.at[layer], qkv),
        copies.start(gain_hbm, gain),
        copies.start(order_hbm, order),
        copies.start(wout_hbm.at[layer], wout),
    ]
    for k, (begin, end) in enumerate(spans):
        lo, hi = max(begin, first), min(end, last)
        if lo < hi:
            late.append(
                copies.start(states[k].at[lo - begin : hi - begin], held.at[lo - first : hi - first])
            )
    zeros = jnp.zeros(padded.shape[1:], BF16)
    if first == 0:
        padded[0] = zeros
    if last == rows:
        padded[total + 1] = zeros
    wait_all(late)
    split_weights(qkv, wqv_t)
    wait_all(inputs)
    outputs = []
    for begin, end in groups_of(total):
        taps = [
            jnp.concatenate(
                [
                    padded[i + di, dj * members : dj * members + count]
                    for di in range(3)
                    for dj in range(3)
                ],
                axis=1,
            )
            for i in range(begin, end)
        ]
        conv_out = jnp.dot(
            jnp.concatenate(taps, axis=0),
            weight[...].reshape(9 * channels, 2 * channels),
            preferred_element_type=F32,
        )
        joined = held[begin:end].reshape((end - begin) * count, channels).astype(F32)
        joined = (joined + gated(conv_out, channels)).astype(BF16).astype(F32)
        joined = attention_rows(
            joined, gain[layer, 1:2], wqv_t[...], qkv[:, channels : 2 * channels], wout[...],
            members, count,
        ).astype(BF16)
        for i in range(begin, end):
            moved = shuffled(order[...], joined[(i - begin) * count : (i - begin + 1) * count])
            out[:, i] = moved.reshape(out.shape[0], out.shape[2], channels).astype(BF16)
        outputs.append(copies.start(out.at[:, begin:end], out_hbm.at[:, begin:end]))
    wait_all(outputs)


def place_kernel(first, arrived_hbm, order_hbm, *refs):
    out_hbm, arrived, order, out, semaphores = refs[-5:]
    local, total, cols, channels = out.shape
    copies = Copies(semaphores)
    inputs = [copies.start(order_hbm, order)]
    groups = groups_of(total)
    rows_in = [
        copies.start(arrived_hbm.at[:, begin:end], arrived.at[:, begin:end])
        for begin, end in groups
    ]
    wait_all(inputs)
    outputs = []
    for (begin, end), copy in zip(groups, rows_in):
        copy.wait()
        for i in range(begin, end):
            moved = shuffled(order[...], arrived[:, i].reshape(local * cols, channels))
            out[:, i] = moved.reshape(local, cols, channels).astype(BF16)
        outputs.append(
            copies.start(out.at[:, begin:end], out_hbm.at[:, first + begin : first + end])
        )
    wait_all(outputs)


def anywhere():
    return pl.BlockSpec(memory_space=pl.ANY)


def call(kernel, name, operands, outs, scratch, flops, moved, transcendentals=0, aliases=None):
    return pl.pallas_call(
        kernel,
        out_shape=[jax.ShapeDtypeStruct(shape, BF16) for shape in outs],
        in_specs=[anywhere()] * len(operands),
        out_specs=[anywhere()] * len(outs),
        scratch_shapes=[pltpu.VMEM(shape, dtype) for shape, dtype in scratch]
        + [pltpu.SemaphoreType.DMA((48,))],
        input_output_aliases=aliases or {},
        compiler_params=pltpu.CompilerParams(vmem_limit_bytes=VMEM_LIMIT),
        cost_estimate=pl.CostEstimate(
            flops=flops, bytes_accessed=moved, transcendentals=transcendentals
        ),
        name=name,
    )(*operands)


def body(field, norm_gain, conv_weight, qkv_weight, out_weight):
    local, rows, cols, channels = field.shape
    devices = lax.axis_size("mem")
    width = cols // devices
    members = devices * local
    count = local * cols
    block = local * width
    to_message, to_tile, from_tile, to_slab = shuffles(devices, local, cols)
    taps = conv_weight.shape[1] * conv_weight.shape[2] * channels
    conv_shape = conv_weight.shape[1:]
    gain_shape = norm_gain.shape

    split_in = rows // 2 + 1
    split_out = split_in - 1
    spans_in = ((0, split_in), (split_in, rows))
    spans_out = ((0, split_out), (split_out, rows))

    square = ((count, count), BF16)
    attention_weights = [
        (gain_shape, F32),
        ((channels, 3 * channels), BF16),
        ((2 * channels, channels), BF16),
        ((channels, channels), BF16),
        square,
    ]

    def conv_slab(first, last):
        total = last - first
        held = min(last + 1, rows) - max(first - 1, 0)
        messages = (devices, total, block, channels)
        return call(
            functools.partial(conv_slab_kernel, 0, first, last),
            "conv_slab",
            (field, norm_gain, conv_weight, to_message),
            [messages],
            [
                ((local, held, cols, channels), BF16),
                (gain_shape, F32),
                (conv_shape, BF16),
                square,
                ((total + 2, 3, count, channels), BF16),
                (messages, BF16),
            ],
            2 * total * count * taps * 2 * channels,
            4 * total * count * channels,
            total * count * channels,
        )[0]

    def exchange(messages):
        return lax.all_to_all(messages, "mem", split_axis=0, concat_axis=0, tiled=True)

    def attend(arrived):
        total = arrived.shape[1]
        whole, edge = (total, count, channels), (total, members, channels)
        return call(
            functools.partial(attend_kernel, 0, members),
            "attend",
            (arrived, norm_gain, qkv_weight, out_weight, to_tile),
            [whole, whole, edge, edge],
            [(arrived.shape, BF16)] + attention_weights + [(whole, BF16), (whole, BF16)],
            2 * total * count * channels * 6 * channels,
            8 * total * count * channels,
            total * count * members * HEADS,
        )

    tiles = [tile_of(d, devices) for d in range(devices)]
    owner = {t: d for d, t in enumerate(tiles)}
    rightward = [(owner[t], owner[t + 1]) for t in range(devices - 1)]
    leftward = [(target, source) for source, target in rightward]

    def conv_tile(first, last, spans, parts):
        total = last - first
        operands = [p[k] for k in range(4) for p in parts]
        messages = (devices, total, block, channels)
        return call(
            functools.partial(conv_tile_kernel, 1, first, last, rows, spans, members),
            "conv_tile",
            (*operands, conv_weight, norm_gain, qkv_weight, out_weight, from_tile),
            [messages],
            [
                ((total + 2, count + 2 * members, channels), BF16),
                ((total, count, channels), BF16),
                (conv_shape, BF16),
            ]
            + attention_weights
            + [(messages, BF16)],
            2 * total * count * channels * (6 * channels + 2 * taps),
            8 * total * count * channels,
            total * count * members * HEADS,
        )[0]

    def place(first, last, arrived, earlier):
        total = last - first
        operands = [arrived, to_slab] + ([] if earlier is None else [earlier])
        return call(
            functools.partial(place_kernel, first),
            "place",
            operands,
            [(local, rows, cols, channels)],
            [(arrived.shape, BF16), square, ((local, total, cols, channels), BF16)],
            2 * total * count * count * channels,
            4 * total * count * channels,
            aliases={} if earlier is None else {2: 0},
        )[0]

    arrived = [exchange(conv_slab(*span)) for span in spans_in]
    parts = []
    result = None
    for rows_in in arrived:
        state, normed, low, high = attend(rows_in)
        from_left = lax.ppermute(high, "mem", rightward)
        from_right = lax.ppermute(low, "mem", leftward)
        parts.append((state, normed, from_left, from_right))
    returned = []
    for k, (first, last) in enumerate(spans_out):
        lo = 0 if k == 0 else k - 1
        messages = conv_tile(first, last, spans_in[lo : k + 1], parts[lo : k + 1])
        returned.append(exchange(messages))
    for span, arrival in zip(spans_out, returned):
        result = place(*span, arrival, result)
    return result


def solution(mesh):
    return jax.shard_map(
        body,
        mesh=mesh,
        in_specs=(P(("grp", "mem"), None, None, None), P(), P(), P(), P()),
        out_specs=P(("grp", "mem"), None, None, None),
        check_vma=False,
    )
```

time: 197 us -> 166 us (0.84)
  Pallas kernels: 98.1 us -> 64.8 us
  local copies, waits for them, and re-layouts: 14.8 us -> 2.38 us
  waiting for transfers between devices: 48.6 us -> 57.1 us
  starting transfers between devices: 34.2 us -> 40.9 us
    pallas_call x8, Pallas kernels: 98.1 us -> 64.8 us  [call(): pl.pallas_call(kernel, out_shape=[jax.ShapeDtypeStruct(shape, BF16) for s...]
    all_to_all x4, starting transfers between devices: 25.5 us -> 31.7 us  [exchange(): lax.all_to_all(messages, 'mem', split_axis=0, concat_axis=0, tiled=True)]
    unnamed x36 -> x16, local copies, waits for them, and re-layouts: 8.4 us -> 2.38 us
    all_to_all x4, waiting for transfers between devices: 37 us -> 41.6 us  [exchange(): lax.all_to_all(messages, 'mem', split_axis=0, concat_axis=0, tiled=True)]
    slice x2 -> x0, local copies, waits for them, and re-layouts: 4.43 us -> none  [the longest x1 4.4 us: conv_tile(): conv_weight[1]]
    ppermute x2, waiting for transfers between devices: 7.17 us -> 9.54 us  [body(): from_right = lax.ppermute(low, 'mem', leftward)]
  transfers between devices with their start and end apart: 8 -> 8, of which waited for: 6 -> 6; matrix products, arithmetic and copies ran while one was open for 1% -> 0% of each run, Pallas kernels for 43% -> 32%
where the time goes in v1:
time: 166 us
  Pallas kernels  64.8 us (39%)
  waiting for transfers between devices  57.1 us (34%)
  starting transfers between devices  40.9 us (25%)
  local copies, waits for them, and re-layouts  2.38 us (1%)
    pallas_call x8, Pallas kernels, call(): pl.pallas_call(kernel, out_shape=[jax.ShapeDtypeStruct(shape, BF16) for s...  64.8 us
    all_to_all x4, waiting for transfers between devices, exchange(): lax.all_to_all(messages, 'mem', split_axis=0, concat_axis=0, tiled=True)  41.6 us
    all_to_all x4, starting transfers between devices, exchange(): lax.all_to_all(messages, 'mem', split_axis=0, concat_axis=0, tiled=True)  31.7 us
    ppermute x2, waiting for transfers between devices, body(): from_right = lax.ppermute(low, 'mem', leftward)  9.54 us
    ppermute x2, waiting for transfers between devices, body(): from_left = lax.ppermute(high, 'mem', rightward)  5.99 us
    ppermute x2, starting transfers between devices, body(): from_left = lax.ppermute(high, 'mem', rightward)  4.87 us
    ppermute x2, starting transfers between devices, body(): from_right = lax.ppermute(low, 'mem', leftward)  4.32 us
  transfers between devices with their start and end apart: 8, of which 6 were waited for; matrix products, arithmetic and copies ran while one was open for 0% of the time, Pallas kernels for 32%

profile of v1, /device:TPU:15, one launch (start us, length us, event | category | flops | bytes accessed | tf_op | source)
XLA Modules:
  0.0 165.5 jit_solution(1993885473927976540)
XLA Ops:
  0.0 9.5 %conv_slab.2 = bf16[16,9,16,256]{3,2,1,0:T(8,128)(2,1)} custom-call(bf16[4,16,64,256]{3,2,1,0:T(8,128)(2,1)} %field_hbm.3, f32[2,2,256]{2,1,0:T(2,128)} %refs_5_.1, bf16[2,3,3,256,512]{4,3,2,1,0:T(8,128)(2,1)} %refs_4_.1, bf16[256,256]{1,0:T(8,128)(2,1)} %constant.8.clone.order_hbm), custom_call_target="tpu_custom_call" | custom-call | flops 5435817984 | bytes 2359296 | tf_op jit(solution)/shard_map/conv_slab/pallas_call | solution.py:381
  9.5 6.6 %all-to-all-start = ((bf16[16,9,16,256]{3,2,1,0:T(8,128)(2,1)}), bf16[16,9,16,256]{3,2,1,0:T(8,128)(2,1)S(1)}, u32[]{:S(2)}, u32[]{:S(2)}) async-start(bf16[16,9,16,256]{3,2,1,0:T(8,128)(2,1)} %conv_slab.2), calls=%async_computation | async-start | bytes 2359296 | tf_op jit(solution)/shard_map/all_to_all | solution.py:446
  16.1 8.1 %conv_slab.3 = bf16[16,7,16,256]{3,2,1,0:T(8,128)(2,1)} custom-call(bf16[4,16,64,256]{3,2,1,0:T(8,128)(2,1)} %field_hbm.3, f32[2,2,256]{2,1,0:T(2,128)} %refs_5_.1, bf16[2,3,3,256,512]{4,3,2,1,0:T(8,128)(2,1)} %refs_4_.1, bf16[256,256]{1,0:T(8,128)(2,1)} %constant.8.clone.order_hbm), custom_call_target="tpu_custom_call" | custom-call | flops 4227858432 | bytes 1835008 | tf_op jit(solution)/shard_map/conv_slab/pallas_call | solution.py:381
  24.2 19.6 %all-to-all-done.arrived_hbm = bf16[16,9,16,256]{3,2,1,0:T(8,128)(2,1)S(1)} async-done(((bf16[16,9,16,256]{3,2,1,0:T(8,128)(2,1)}), bf16[16,9,16,256]{3,2,1,0:T(8,128)(2,1)S(1)}, u32[]{:S(2)}, u32[]{:S(2)}) %all-to-all-start) | async-done | bytes 1179680 | tf_op jit(solution)/shard_map/all_to_all | solution.py:446
  43.9 4.9 %all-to-all-start.1 = ((bf16[16,7,16,256]{3,2,1,0:T(8,128)(2,1)}), bf16[16,7,16,256]{3,2,1,0:T(8,128)(2,1)S(1)}, u32[]{:S(2)}, u32[]{:S(2)}) async-start(bf16[16,7,16,256]{3,2,1,0:T(8,128)(2,1)} %conv_slab.3), calls=%async_computation.1 | async-start | bytes 1835008 | tf_op jit(solution)/shard_map/all_to_all | solution.py:446
  48.7 0.0 copy-done.2
  48.7 8.2 %attend.2 = (bf16[9,256,256]{2,1,0:T(8,128)(2,1)}, bf16[9,256,256]{2,1,0:T(8,128)(2,1)}, bf16[9,64,256]{2,1,0:T(8,128)(2,1)}, bf16[9,64,256]{2,1,0:T(8,128)(2,1)}) custom-call(bf16[16,9,16,256]{3,2,1,0:T(8,128)(2,1)} %copy-done.2, f32[2,2,256]{2,1,0:T(2,128)} %refs_5_.1, bf16[2,256,768]{2,1,0:T(8,128)(2,1)} %refs_6_.1, bf16[2,256,256]{2,1,0:T(8,128)(2,1)} %refs_7_.1, ...), custom_call_target="tpu_custom_call" | custom-call | flops 1811939328 | bytes 4718592 | tf_op jit(solution)/shard_map/attend/pallas_call | solution.py:381
  56.9 2.4 %collective-permute-start = (bf16[9,64,256]{2,1,0:T(8,128)(2,1)}, bf16[9,64,256]{2,1,0:T(8,128)(2,1)S(1)}, u32[]{:S(2)}, u32[]{:S(2)}) collective-permute-start(bf16[9,64,256]{2,1,0:T(8,128)(2,1)} %get-tuple-element.17), channel_id=1, source_target_pairs={{0,1},{1,2},{2,3},{3,6},{6,7},{7,4},{4,5},{5,8},{8,9},{9,10},{10,1... | collective-permute-start | bytes 884744 | tf_op jit(solution)/shard_map/ppermute | solution.py:507
  59.4 2.1 %collective-permute-start.2 = (bf16[9,64,256]{2,1,0:T(8,128)(2,1)}, bf16[9,64,256]{2,1,0:T(8,128)(2,1)S(1)}, u32[]{:S(2)}, u32[]{:S(2)}) collective-permute-start(bf16[9,64,256]{2,1,0:T(8,128)(2,1)} %get-tuple-element.19), channel_id=1, source_target_pairs={{1,0},{2,1},{3,2},{6,3},{7,6},{4,7},{5,4},{8,5},{9,8},{10,9},{11,1... | collective-permute-start | bytes 884744 | tf_op jit(solution)/shard_map/ppermute | solution.py:508
  61.5 4.3 %collective-permute-done.refs_4_.refs_2_ = bf16[9,64,256]{2,1,0:T(8,128)(2,1)S(1)} collective-permute-done((bf16[9,64,256]{2,1,0:T(8,128)(2,1)}, bf16[9,64,256]{2,1,0:T(8,128)(2,1)S(1)}, u32[]{:S(2)}, u32[]{:S(2)}) %collective-permute-start) | collective-permute-done | bytes 294944 | tf_op jit(solution)/shard_map/ppermute | solution.py:507
  65.9 2.9 %collective-permute-done.2.refs_6_.refs_3_ = bf16[9,64,256]{2,1,0:T(8,128)(2,1)S(1)} collective-permute-done((bf16[9,64,256]{2,1,0:T(8,128)(2,1)}, bf16[9,64,256]{2,1,0:T(8,128)(2,1)S(1)}, u32[]{:S(2)}, u32[]{:S(2)}) %collective-permute-start.2) | collective-permute-done | bytes 294944 | tf_op jit(solution)/shard_map/ppermute | solution.py:508
  68.8 0.0 copy-done.4
  68.8 0.7 copy-done.5
  69.5 13.1 %conv_tile.3 = bf16[16,8,16,256]{3,2,1,0:T(8,128)(2,1)} custom-call(bf16[9,256,256]{2,1,0:T(8,128)(2,1)} %get-tuple-element.13.refs_0_, bf16[9,256,256]{2,1,0:T(8,128)(2,1)} %get-tuple-element.15.refs_2_.refs_1_, bf16[9,64,256]{2,1,0:T(8,128)(2,1)} %copy-done.4, bf16[9,64,256]{2,1,0:T(8,128)(2,1)} %copy-done.5, bf16[2,3,3,256,512]{4,3,2,1,0:T(8,128)(2,1)} %refs_4_.1, ...), custom_call_target="tpu_custom_call" | custom-call | flops 6442450944 | bytes 4194304 | tf_op jit(solution)/shard_map/conv_tile/pallas_call | solution.py:381
  82.6 0.0 all-to-all-done.1.arrived_hbm
  82.7 0.0 copy-start.3
  82.7 8.9 %all-to-all-start.3 = ((bf16[16,8,16,256]{3,2,1,0:T(8,128)(2,1)}), bf16[16,8,16,256]{3,2,1,0:T(8,128)(2,1)S(1)}, u32[]{:S(2)}, u32[]{:S(2)}) async-start(bf16[16,8,16,256]{3,2,1,0:T(8,128)(2,1)} %conv_tile.3), calls=%async_computation.3 | async-start | bytes 2097152 | tf_op jit(solution)/shard_map/all_to_all | solution.py:446
  91.6 0.0 copy-done.3
  91.6 6.8 %attend.3 = (bf16[7,256,256]{2,1,0:T(8,128)(2,1)}, bf16[7,256,256]{2,1,0:T(8,128)(2,1)}, bf16[7,64,256]{2,1,0:T(8,128)(2,1)}, bf16[7,64,256]{2,1,0:T(8,128)(2,1)}) custom-call(bf16[16,7,16,256]{3,2,1,0:T(8,128)(2,1)} %copy-done.3, f32[2,2,256]{2,1,0:T(2,128)} %refs_5_.1, bf16[2,256,768]{2,1,0:T(8,128)(2,1)} %refs_6_.1, bf16[2,256,256]{2,1,0:T(8,128)(2,1)} %refs_7_.1, ...), custom_call_target="tpu_custom_call" | custom-call | flops 1409286144 | bytes 3670016 | tf_op jit(solution)/shard_map/attend/pallas_call | solution.py:381
  98.4 2.4 %collective-permute-start.1 = (bf16[7,64,256]{2,1,0:T(8,128)(2,1)}, bf16[7,64,256]{2,1,0:T(8,128)(2,1)S(1)}, u32[]{:S(2)}, u32[]{:S(2)}) collective-permute-start(bf16[7,64,256]{2,1,0:T(8,128)(2,1)} %get-tuple-element.18), channel_id=1, source_target_pairs={{0,1},{1,2},{2,3},{3,6},{6,7},{7,4},{4,5},{5,8},{8,9},{9,10},{10,1... | collective-permute-start | bytes 688136 | tf_op jit(solution)/shard_map/ppermute | solution.py:507
  100.8 2.2 %collective-permute-start.3 = (bf16[7,64,256]{2,1,0:T(8,128)(2,1)}, bf16[7,64,256]{2,1,0:T(8,128)(2,1)S(1)}, u32[]{:S(2)}, u32[]{:S(2)}) collective-permute-start(bf16[7,64,256]{2,1,0:T(8,128)(2,1)} %get-tuple-element.20), channel_id=1, source_target_pairs={{1,0},{2,1},{3,2},{6,3},{7,6},{4,7},{5,4},{8,5},{9,8},{10,9},{11,1... | collective-permute-start | bytes 688136 | tf_op jit(solution)/shard_map/ppermute | solution.py:508
  103.0 1.6 collective-permute-done.1.refs_5_
  104.7 6.6 %collective-permute-done.3.refs_7_ = bf16[7,64,256]{2,1,0:T(8,128)(2,1)S(1)} collective-permute-done((bf16[7,64,256]{2,1,0:T(8,128)(2,1)}, bf16[7,64,256]{2,1,0:T(8,128)(2,1)S(1)}, u32[]{:S(2)}, u32[]{:S(2)}) %collective-permute-start.3) | collective-permute-done | bytes 229408 | tf_op jit(solution)/shard_map/ppermute | solution.py:508
  111.3 0.0 copy-done.6
  111.3 0.7 copy-done.7
  111.9 13.2 %conv_tile.2 = bf16[16,8,16,256]{3,2,1,0:T(8,128)(2,1)} custom-call(bf16[9,256,256]{2,1,0:T(8,128)(2,1)} %get-tuple-element.13.refs_0_, bf16[7,256,256]{2,1,0:T(8,128)(2,1)} %get-tuple-element.14.refs_1_, bf16[9,256,256]{2,1,0:T(8,128)(2,1)} %get-tuple-element.15.refs_2_.refs_1_, bf16[7,256,256]{2,1,0:T(8,128)(2,1)} %get-tuple-element.16.refs_3_, ...), custom_call_target="tpu_custom_call" | custom-call | flops 6442450944 | bytes 4194304 | tf_op jit(solution)/shard_map/conv_tile/pallas_call | solution.py:381
  125.1 0.0 all-to-all-done.3.arrived_hbm
  125.1 11.4 %all-to-all-start.2 = ((bf16[16,8,16,256]{3,2,1,0:T(8,128)(2,1)}), bf16[16,8,16,256]{3,2,1,0:T(8,128)(2,1)S(1)}, u32[]{:S(2)}, u32[]{:S(2)}) async-start(bf16[16,8,16,256]{3,2,1,0:T(8,128)(2,1)} %conv_tile.2), calls=%async_computation.2 | async-start | bytes 2097152 | tf_op jit(solution)/shard_map/all_to_all | solution.py:446
  136.5 2.9 %place.2.refs_0_ = bf16[4,16,64,256]{3,2,1,0:T(8,128)(2,1)} custom-call(bf16[16,8,16,256]{3,2,1,0:T(8,128)(2,1)} %copy-done, bf16[256,256]{1,0:T(8,128)(2,1)} %constant.11.clone.order_hbm), custom_call_target="tpu_custom_call" | custom-call | flops 268435456 | bytes 2097152 | tf_op jit(solution)/shard_map/place/pallas_call | solution.py:381
  139.5 21.9 %all-to-all-done.2.arrived_hbm = bf16[16,8,16,256]{3,2,1,0:T(8,128)(2,1)S(1)} async-done(((bf16[16,8,16,256]{3,2,1,0:T(8,128)(2,1)}), bf16[16,8,16,256]{3,2,1,0:T(8,128)(2,1)S(1)}, u32[]{:S(2)}, u32[]{:S(2)}) %all-to-all-start.2) | async-done | bytes 1048608 | tf_op jit(solution)/shard_map/all_to_all | solution.py:446
  161.4 1.0 copy-done.1
  162.4 2.9 %place.3 = bf16[4,16,64,256]{3,2,1,0:T(8,128)(2,1)} custom-call(bf16[16,8,16,256]{3,2,1,0:T(8,128)(2,1)} %copy-done.1, bf16[256,256]{1,0:T(8,128)(2,1)} %constant.11.clone.order_hbm, bf16[4,16,64,256]{3,2,1,0:T(8,128)(2,1)} %place.2.refs_0_), custom_call_target="tpu_custom_call", output_to_operand_aliasing={{}: (2, {})} | custom-call | flops 268435456 | bytes 2097152 | tf_op jit(solution)/shard_map/place/pallas_call | solution.py:381
  (8 shorter events, 0.0 us)
Async XLA Ops:
  9.5 34.3 %all-to-all-start = ((bf16[16,9,16,256]{3,2,1,0:T(8,128)(2,1)}), bf16[16,9,16,256]{3,2,1,0:T(8,128)(2,1)S(1)}, u32[]{:S(2)}, u32[]{:S(2)}) async-start(bf16[16,9,16,256]{3,2,1,0:T(8,128)(2,1)} %conv_slab.2), calls=%async_computation | async-start | bytes 2359296 | tf_op jit(solution)/shard_map/all_to_all | solution.py:446
  43.9 4.9 %copy-start.2 = (bf16[16,9,16,256]{3,2,1,0:T(8,128)(2,1)}, bf16[16,9,16,256]{3,2,1,0:T(8,128)(2,1)S(1)}, u32[]{:S(2)}) copy-start(bf16[16,9,16,256]{3,2,1,0:T(8,128)(2,1)S(1)} %all-to-all-done.arrived_hbm) | copy-start | bytes 3538948
  43.9 38.8 %all-to-all-start.1 = ((bf16[16,7,16,256]{3,2,1,0:T(8,128)(2,1)}), bf16[16,7,16,256]{3,2,1,0:T(8,128)(2,1)S(1)}, u32[]{:S(2)}, u32[]{:S(2)}) async-start(bf16[16,7,16,256]{3,2,1,0:T(8,128)(2,1)} %conv_slab.3), calls=%async_computation.1 | async-start | bytes 1835008 | tf_op jit(solution)/shard_map/all_to_all | solution.py:446
  56.9 8.9 %collective-permute-start = (bf16[9,64,256]{2,1,0:T(8,128)(2,1)}, bf16[9,64,256]{2,1,0:T(8,128)(2,1)S(1)}, u32[]{:S(2)}, u32[]{:S(2)}) collective-permute-start(bf16[9,64,256]{2,1,0:T(8,128)(2,1)} %get-tuple-element.17), channel_id=1, source_target_pairs={{0,1},{1,2},{2,3},{3,6},{6,7},{7,4},{4,5},{5,8},{8,9},{9,10},{10,1... | collective-permute-start | bytes 884744 | tf_op jit(solution)/shard_map/ppermute | solution.py:507
  59.4 9.4 %collective-permute-start.2 = (bf16[9,64,256]{2,1,0:T(8,128)(2,1)}, bf16[9,64,256]{2,1,0:T(8,128)(2,1)S(1)}, u32[]{:S(2)}, u32[]{:S(2)}) collective-permute-start(bf16[9,64,256]{2,1,0:T(8,128)(2,1)} %get-tuple-element.19), channel_id=1, source_target_pairs={{1,0},{2,1},{3,2},{6,3},{7,6},{4,7},{5,4},{8,5},{9,8},{10,9},{11,1... | collective-permute-start | bytes 884744 | tf_op jit(solution)/shard_map/ppermute | solution.py:508
  65.9 2.9 %copy-start.4 = (bf16[9,64,256]{2,1,0:T(8,128)(2,1)}, bf16[9,64,256]{2,1,0:T(8,128)(2,1)S(1)}, u32[]{:S(2)}) copy-start(bf16[9,64,256]{2,1,0:T(8,128)(2,1)S(1)} %collective-permute-done.refs_4_.refs_2_) | copy-start | bytes 884740
  68.8 0.7 copy-start.5
  82.7 8.9 %copy-start.3 = (bf16[16,7,16,256]{3,2,1,0:T(8,128)(2,1)}, bf16[16,7,16,256]{3,2,1,0:T(8,128)(2,1)S(1)}, u32[]{:S(2)}) copy-start(bf16[16,7,16,256]{3,2,1,0:T(8,128)(2,1)S(1)} %all-to-all-done.1.arrived_hbm) | copy-start | bytes 2752516
  82.7 42.5 %all-to-all-start.3 = ((bf16[16,8,16,256]{3,2,1,0:T(8,128)(2,1)}), bf16[16,8,16,256]{3,2,1,0:T(8,128)(2,1)S(1)}, u32[]{:S(2)}, u32[]{:S(2)}) async-start(bf16[16,8,16,256]{3,2,1,0:T(8,128)(2,1)} %conv_tile.3), calls=%async_computation.3 | async-start | bytes 2097152 | tf_op jit(solution)/shard_map/all_to_all | solution.py:446
  98.4 6.3 %collective-permute-start.1 = (bf16[7,64,256]{2,1,0:T(8,128)(2,1)}, bf16[7,64,256]{2,1,0:T(8,128)(2,1)S(1)}, u32[]{:S(2)}, u32[]{:S(2)}) collective-permute-start(bf16[7,64,256]{2,1,0:T(8,128)(2,1)} %get-tuple-element.18), channel_id=1, source_target_pairs={{0,1},{1,2},{2,3},{3,6},{6,7},{7,4},{4,5},{5,8},{8,9},{9,10},{10,1... | collective-permute-start | bytes 688136 | tf_op jit(solution)/shard_map/ppermute | solution.py:507
  100.8 10.4 %collective-permute-start.3 = (bf16[7,64,256]{2,1,0:T(8,128)(2,1)}, bf16[7,64,256]{2,1,0:T(8,128)(2,1)S(1)}, u32[]{:S(2)}, u32[]{:S(2)}) collective-permute-start(bf16[7,64,256]{2,1,0:T(8,128)(2,1)} %get-tuple-element.20), channel_id=1, source_target_pairs={{1,0},{2,1},{3,2},{6,3},{7,6},{4,7},{5,4},{8,5},{9,8},{10,9},{11,1... | collective-permute-start | bytes 688136 | tf_op jit(solution)/shard_map/ppermute | solution.py:508
  104.7 6.6 %copy-start.6 = (bf16[7,64,256]{2,1,0:T(8,128)(2,1)}, bf16[7,64,256]{2,1,0:T(8,128)(2,1)S(1)}, u32[]{:S(2)}) copy-start(bf16[7,64,256]{2,1,0:T(8,128)(2,1)S(1)} %collective-permute-done.1.refs_5_) | copy-start | bytes 688132
  111.3 0.7 copy-start.7
  125.1 11.4 %copy-start = (bf16[16,8,16,256]{3,2,1,0:T(8,128)(2,1)}, bf16[16,8,16,256]{3,2,1,0:T(8,128)(2,1)S(1)}, u32[]{:S(2)}) copy-start(bf16[16,8,16,256]{3,2,1,0:T(8,128)(2,1)S(1)} %all-to-all-done.3.arrived_hbm) | copy-start | bytes 3145732
  125.1 36.2 %all-to-all-start.2 = ((bf16[16,8,16,256]{3,2,1,0:T(8,128)(2,1)}), bf16[16,8,16,256]{3,2,1,0:T(8,128)(2,1)S(1)}, u32[]{:S(2)}, u32[]{:S(2)}) async-start(bf16[16,8,16,256]{3,2,1,0:T(8,128)(2,1)} %conv_tile.2), calls=%async_computation.2 | async-start | bytes 2097152 | tf_op jit(solution)/shard_map/all_to_all | solution.py:446
  161.4 1.0 copy-start.1

commit v2 on v1

v2 whole, which is shorter than its diff:
```python
import functools

import jax
import jax.numpy as jnp
import numpy as np
from jax import lax
from jax.experimental import pallas as pl
from jax.experimental.pallas import tpu as pltpu
from jax.sharding import PartitionSpec as P

HEADS = 8
BLOCKS = 2
LANES = 128
epsilon = 1e-06
VMEM_LIMIT = 40 * 1024 * 1024
UNROLL = 4

F32 = jnp.float32
BF16 = jnp.bfloat16


def tile_of(device, count):
    if count % 4:
        return device
    group, inner = device // 4, device % 4
    if group % 2:
        inner = (2, 3, 0, 1)[inner]
    return group * 4 + inner


def one_hot(sources):
    matrix = np.zeros((len(sources), len(sources)), np.float32)
    matrix[np.arange(len(sources)), np.asarray(sources)] = 1.0
    return jnp.asarray(matrix, BF16)


def shuffles(count, local, cols):
    width = cols // count
    members = count * local
    tiles = [tile_of(d, count) for d in range(count)]
    to_message = [
        m * cols + tiles[d] * width + c
        for d in range(count)
        for m in range(local)
        for c in range(width)
    ]
    to_slab = np.argsort(to_message)
    to_tile = [
        d * local * width + m * width + c
        for c in range(width)
        for d in range(count)
        for m in range(local)
    ]
    from_tile = np.argsort(to_tile)
    return one_hot(to_message), one_hot(to_tile), one_hot(from_tile), one_hot(to_slab)


def normalize(widened, gain):
    inverse = lax.rsqrt(jnp.mean(widened * widened, axis=-1, keepdims=True) + epsilon)
    return widened * inverse * gain


def gated(conv_out, channels):
    return conv_out[:, :channels] * jax.nn.sigmoid(conv_out[:, channels:])


def shuffled(matrix, rows):
    return jnp.dot(matrix, rows, preferred_element_type=F32)


def groups_of(total, most=UNROLL):
    pieces = -(-total // most)
    edges = [total * k // pieces for k in range(pieces + 1)]
    return [(edges[k], edges[k + 1]) for k in range(pieces)]


def attention_rows(state, gain, wqv_t, wk, wout, members):
    total, channels = state.shape
    size = channels // HEADS
    group = LANES // size
    packed = LANES // members
    factor = float(np.log2(np.e) / np.sqrt(size))
    normed = normalize(state, gain).astype(BF16)
    keys = jnp.dot(normed, wk, preferred_element_type=F32).astype(BF16)
    qv_t = lax.dot_general(
        wqv_t, normed, (((1,), (1,)), ((), ())), preferred_element_type=F32
    ).astype(BF16)
    lane = lax.broadcasted_iota(jnp.int32, (members, LANES), 1)
    masks = [
        ((lane >= k * members) & (lane < (k + 1) * members)).astype(F32).astype(BF16)
        for k in range(packed)
    ]
    spans = [slice(j * LANES, (j + 1) * LANES) for j in range(total // LANES)]
    quads = range(channels // LANES)
    scores = {}
    for j, span in enumerate(spans):
        for q in quads:
            blocks = []
            for h in range(group):
                row = q * LANES + h * size
                parts = [jnp.zeros((size, LANES), BF16)] * group
                parts[h] = qv_t[row : row + size, span]
                blocks.append(jnp.concatenate(parts, axis=1))
            scores[j, q] = jnp.dot(
                keys[span, q * LANES : (q + 1) * LANES],
                jnp.concatenate(blocks, axis=0),
                preferred_element_type=F32,
            )
    weights = {}
    for j in range(len(spans)):
        for q in quads:
            for h in range(group):
                square = scores[j, q][:, h * LANES : (h + 1) * LANES]
                dense = square[:members]
                for k in range(1, packed):
                    dense = jnp.where(
                        lane < k * members, dense, square[k * members : (k + 1) * members]
                    )
                top = jnp.max(dense, axis=0, keepdims=True)
                expo = jnp.exp2((dense - top) * factor)
                inverse = 1.0 / jnp.sum(expo, axis=0, keepdims=True)
                spread = expo.astype(BF16)
                if packed > 1:
                    spread = jnp.concatenate([spread * mask for mask in masks], axis=0)
                weights[j, q, h] = spread, inverse
    columns = []
    for j, span in enumerate(spans):
        pieces = []
        for q in quads:
            for h in range(0, group, 2):
                row = channels + q * LANES + h * size
                mixed = jnp.dot(
                    qv_t[row : row + 2 * size, span],
                    jnp.concatenate([weights[j, q, h + k][0] for k in range(2)], axis=1),
                    preferred_element_type=F32,
                )
                for k in range(2):
                    own = mixed[k * size : (k + 1) * size, k * LANES : (k + 1) * LANES]
                    pieces.append((own * weights[j, q, h + k][1]).astype(BF16))
        columns.append(jnp.concatenate(pieces, axis=0))
    attended_t = jnp.concatenate(columns, axis=1)
    update = lax.dot_general(
        attended_t, wout, (((0,), (0,)), ((), ())), preferred_element_type=F32
    )
    return state + update


class Copies:
    def __init__(self, semaphores):
        self.semaphores = semaphores
        self.used = 0

    def start(self, source, target):
        copy = pltpu.make_async_copy(source, target, self.semaphores.at[self.used])
        self.used += 1
        copy.start()
        return copy


def wait_all(copies):
    for copy in copies:
        copy.wait()


def conv_slab_kernel(
    layer, first, last, staging, field_hbm, gain_hbm, weight_hbm, order_hbm, *refs,
):
    if staging:
        (qkv_hbm, wout_hbm, to_tile_hbm, from_tile_hbm, to_slab_hbm, out,
         later_gain, later_weight, wqv_t, wk, wout, to_tile, from_tile, to_slab,
         field, gain, weight, order, padded, qkv, semaphores) = refs
    else:
        out, field, gain, weight, order, padded, semaphores = refs
    local, rows, cols, channels = field_hbm.shape
    count = local * cols
    copies = Copies(semaphores)
    low = max(first - 1, 0)
    groups = groups_of(last - first)
    gain_copy = copies.start(gain_hbm, gain)
    fields, late, staged = [], [], []
    ready = low
    for k, (begin, end) in enumerate(groups):
        needed = min(first + end + 1, rows)
        part = slice(ready - low, needed - low)
        fields.append(copies.start(field_hbm.at[:, ready:needed], field.at[:, part]))
        ready = needed
        if k == 0:
            late.append(copies.start(weight_hbm.at[layer], weight))
            late.append(copies.start(order_hbm, order))
    if staging:
        staged = [
            copies.start(qkv_hbm, qkv),
            copies.start(gain_hbm, later_gain),
            copies.start(weight_hbm.at[layer + 1], later_weight),
            copies.start(wout_hbm, wout),
            copies.start(to_tile_hbm, to_tile),
            copies.start(from_tile_hbm, from_tile),
            copies.start(to_slab_hbm, to_slab),
        ]
    column = lax.broadcasted_iota(jnp.int32, (count, 1), 0) % cols
    zeros = jnp.zeros(padded.shape[1:], BF16)
    if first == 0:
        padded[0] = zeros
    if last == rows:
        padded[last - first + 1] = zeros
    gain_copy.wait()
    gain_row = gain[layer, 0:1]

    def prepare(row):
        widened = field[:, row - low].reshape(count, channels).astype(F32)
        normed = normalize(widened, gain_row)
        left = jnp.where(column == 0, 0.0, pltpu.roll(normed, 1, 0))
        right = jnp.where(column == cols - 1, 0.0, pltpu.roll(normed, count - 1, 0))
        slot = row - first + 1
        padded[slot, 0] = left.astype(BF16)
        padded[slot, 1] = normed.astype(BF16)
        padded[slot, 2] = right.astype(BF16)

    ready = low
    for k, (begin, end) in enumerate(groups):
        needed = min(first + end + 1, rows)
        fields[k].wait()
        for row in range(ready, needed):
            prepare(row)
        ready = needed
        if k == 0:
            wait_all(late)
        taps = [
            jnp.concatenate(
                [padded[i + di, dj] for di in range(3) for dj in range(3)], axis=1
            )
            for i in range(begin, end)
        ]
        conv_out = jnp.dot(
            jnp.concatenate(taps, axis=0),
            weight[...].reshape(9 * channels, 2 * channels),
            preferred_element_type=F32,
        )
        update = gated(conv_out, channels)
        for i in range(begin, end):
            widened = field[:, first + i - low].reshape(count, channels).astype(F32)
            part = update[(i - begin) * count : (i - begin + 1) * count]
            moved = shuffled(order[...], (widened + part).astype(BF16))
            out[:, i] = moved.reshape(out.shape[0], out.shape[2], channels).astype(BF16)
    if staging:
        wait_all(staged)
        for b in range(BLOCKS):
            wqv_t[b, :channels] = qkv[b, :, :channels].T
            wqv_t[b, channels:] = qkv[b, :, 2 * channels :].T
            wk[b] = qkv[b, :, channels : 2 * channels]


def attend_kernel(
    layer, members, arrived, gain, wqv_t, wk, wout, order, state, normed, low, high,
):
    total, count, channels = state.shape
    for begin, end in groups_of(total):
        joined = jnp.concatenate(
            [
                shuffled(order[...], arrived[:, i].reshape(count, channels))
                for i in range(begin, end)
            ],
            axis=0,
        )
        joined = attention_rows(
            joined, gain[layer, 1:2], wqv_t[layer], wk[layer], wout[layer], members
        ).astype(BF16)
        following = normalize(joined.astype(F32), gain[layer + 1, 0:1]).astype(BF16)
        for i in range(begin, end):
            span = slice((i - begin) * count, (i - begin + 1) * count)
            state[i] = joined[span]
            normed[i] = following[span]
            low[i] = following[span][:members]
            high[i] = following[span][count - members :]


def conv_tile_kernel(layer, first, last, rows, spans, members, cells, halo, *refs):
    pieces = len(spans)
    states, refs = refs[:pieces], refs[pieces:]
    normeds, refs = refs[:pieces], refs[pieces:]
    if halo:
        lows, refs = refs[:pieces], refs[pieces:]
        highs, refs = refs[:pieces], refs[pieces:]
        inner, order, refs = refs[0], refs[1], refs[2:]
    weight, gain, wqv_t, wk, wout, out = refs
    count, channels = states[0].shape[1:]
    total = last - first
    size = len(cells) * members
    zeros = jnp.zeros((members, channels), BF16)

    def piece_of(row):
        for k, (begin, end) in enumerate(spans):
            if begin <= row < end:
                return k, row - begin

    def tap(row, cell):
        if not 0 <= row < rows:
            return zeros
        k, place = piece_of(row)
        if cell < 0:
            return lows[k][place]
        if cell * members == count:
            return highs[k][place]
        return normeds[k][place, cell * members : (cell + 1) * members]

    def held(row, cell):
        k, place = piece_of(row)
        return states[k][place, cell * members : (cell + 1) * members]

    for begin, end in groups_of(total, UNROLL * count // size):
        taps = [
            jnp.concatenate(
                [
                    jnp.concatenate(
                        [tap(first + i + di - 1, cell + dj - 1) for cell in cells], axis=0
                    )
                    for di in range(3)
                    for dj in range(3)
                ],
                axis=1,
            )
            for i in range(begin, end)
        ]
        conv_out = jnp.dot(
            jnp.concatenate(taps, axis=0),
            weight[...].reshape(9 * channels, 2 * channels),
            preferred_element_type=F32,
        )
        joined = jnp.concatenate(
            [held(first + i, cell) for i in range(begin, end) for cell in cells], axis=0
        ).astype(F32)
        joined = (joined + gated(conv_out, channels)).astype(BF16).astype(F32)
        joined = attention_rows(
            joined, gain[layer, 1:2], wqv_t[layer], wk[layer], wout[layer], members
        ).astype(BF16)
        for i in range(begin, end):
            own = joined[(i - begin) * size : (i - begin + 1) * size]
            if halo:
                full = jnp.concatenate(
                    [own[:members], inner[i], own[members:]] if size < count else [own], axis=0
                )
                moved = shuffled(order[...], full)
                out[:, i] = moved.reshape(out.shape[0], out.shape[2], channels).astype(BF16)
            else:
                out[i] = own


def place_kernel(first, *refs):
    arrived, order, out_hbm, out, semaphores = refs[-5:]
    local, total, cols, channels = out.shape
    copies = Copies(semaphores)
    outputs = []
    for begin, end in groups_of(total, 2):
        for i in range(begin, end):
            moved = shuffled(order[...], arrived[:, i].reshape(local * cols, channels))
            out[:, i] = moved.reshape(local, cols, channels).astype(BF16)
        outputs.append(
            copies.start(out.at[:, begin:end], out_hbm.at[:, first + begin : first + end])
        )
    wait_all(outputs)


def call(kernel, name, far, near, outs, scratch, flops, moved, transcendentals=0, aliases=None):
    far = [pltpu.with_memory_space_constraint(x, pltpu.HBM) for x in far]
    near = [pltpu.with_memory_space_constraint(x, pltpu.VMEM) for x in near]
    anywhere, vmem = pl.BlockSpec(memory_space=pl.ANY), pl.BlockSpec(memory_space=pltpu.VMEM)
    scratch_shapes = [pltpu.VMEM(shape, dtype) for shape, dtype in scratch]
    if scratch:
        scratch_shapes.append(pltpu.SemaphoreType.DMA((32,)))
    return pl.pallas_call(
        kernel,
        out_shape=[
            pltpu.VMEM(shape, dtype) if is_near else jax.ShapeDtypeStruct(shape, dtype)
            for shape, dtype, is_near in outs
        ],
        in_specs=[anywhere] * len(far) + [vmem] * len(near),
        out_specs=[vmem if is_near else anywhere for _, _, is_near in outs],
        scratch_shapes=scratch_shapes,
        input_output_aliases=aliases or {},
        compiler_params=pltpu.CompilerParams(vmem_limit_bytes=VMEM_LIMIT),
        cost_estimate=pl.CostEstimate(
            flops=flops, bytes_accessed=moved, transcendentals=transcendentals
        ),
        name=name,
    )(*far, *near)


def body(field, norm_gain, conv_weight, qkv_weight, out_weight):
    local, rows, cols, channels = field.shape
    devices = lax.axis_size("mem")
    width = cols // devices
    members = devices * local
    count = local * cols
    block = local * width
    to_message, to_tile, from_tile, to_slab = shuffles(devices, local, cols)
    taps = conv_weight.shape[1] * conv_weight.shape[2] * channels
    conv_shape = conv_weight.shape[1:]

    split_in = rows // 2 + 1
    split_out = split_in - 1
    spans_in = ((0, split_in), (split_in, rows))
    spans_out = ((0, split_out), (split_out, rows))
    square = ((count, count), BF16)

    def conv_slab(first, last):
        total = last - first
        held = min(last + 1, rows) - max(first - 1, 0)
        staging = last == rows
        far = [field, norm_gain, conv_weight, to_message]
        outs = [((devices, total, block, channels), BF16, True)]
        scratch = [
            ((local, held, cols, channels), BF16),
            (norm_gain.shape, F32),
            (conv_shape, BF16),
            square,
            ((total + 2, 3, count, channels), BF16),
        ]
        if staging:
            far += [qkv_weight, out_weight, to_tile, from_tile, to_slab]
            outs += [
                (norm_gain.shape, F32, True),
                (conv_shape, BF16, True),
                ((BLOCKS, 2 * channels, channels), BF16, True),
                ((BLOCKS, channels, channels), BF16, True),
                (out_weight.shape, BF16, True),
            ] + [(*square, True)] * 3
            scratch.append((qkv_weight.shape, BF16))
        return call(
            functools.partial(conv_slab_kernel, 0, first, last, staging),
            "conv_slab",
            far,
            [],
            outs,
            scratch,
            2 * total * count * taps * 2 * channels,
            4 * total * count * channels,
            total * count * channels,
        )

    def exchange(messages):
        return lax.all_to_all(messages, "mem", split_axis=0, concat_axis=0, tiled=True)

    tiles = [tile_of(d, devices) for d in range(devices)]
    owner = {t: d for d, t in enumerate(tiles)}
    rightward = [(owner[t], owner[t + 1]) for t in range(devices - 1)]
    leftward = [(target, source) for source, target in rightward]

    arrived = []
    for span in spans_in:
        messages, *staged = conv_slab(*span)
        arrived.append(exchange(messages))
    gain, later_weight, wqv_t, wk, wout, to_tile, from_tile, to_slab = staged

    def attend(arrival):
        total = arrival.shape[1]
        whole, edge = (total, count, channels), (total, members, channels)
        return call(
            functools.partial(attend_kernel, 0, members),
            "attend",
            [],
            [arrival, gain, wqv_t, wk, wout, to_tile],
            [(shape, BF16, True) for shape in (whole, whole, edge, edge)],
            [],
            2 * total * count * channels * 6 * channels,
            8 * total * count * channels,
            total * count * members * HEADS,
        )

    def conv_tile(first, last, spans, parts, inner):
        total = last - first
        halo = inner is not None
        cells = (0, width - 1) if halo else tuple(range(1, width - 1))
        if not cells:
            return jnp.zeros((1, members, channels), BF16)
        operands = [p[k] for k in range(4 if halo else 2) for p in parts]
        if halo:
            operands += [inner, from_tile]
        size = len(cells) * members
        shape = (devices, total, block, channels) if halo else (total, size, channels)
        return call(
            functools.partial(
                conv_tile_kernel, 1, first, last, rows, spans, members, cells, halo
            ),
            "conv_edges" if halo else "conv_inner",
            [],
            [*operands, later_weight, gain, wqv_t, wk, wout],
            [(shape, BF16, True)],
            [],
            2 * total * size * channels * (6 * channels + 2 * taps),
            8 * total * count * channels,
            total * size * members * HEADS,
        )[0]

    def place(first, last, arrival, earlier):
        total = last - first
        return call(
            functools.partial(place_kernel, first),
            "place",
            [] if earlier is None else [earlier],
            [arrival, to_slab],
            [((local, rows, cols, channels), BF16, False)],
            [((local, total, cols, channels), BF16)],
            2 * total * count * count * channels,
            4 * total * count * channels,
            aliases={} if earlier is None else {0: 0},
        )[0]

    parts = []
    for arrival in arrived:
        state, normed, low, high = attend(arrival)
        from_left = lax.ppermute(high, "mem", rightward)
        from_right = lax.ppermute(low, "mem", leftward)
        parts.append((state, normed, from_left, from_right))
    returned = []
    for k, (first, last) in enumerate(spans_out):
        lo = 0 if k == 0 else k - 1
        spans = spans_in[lo : k + 1]
        inner = conv_tile(first, last, spans, parts[lo : k + 1], None)
        messages = conv_tile(first, last, spans, parts[lo : k + 1], inner)
        returned.append(exchange(messages))
    result = None
    for span, arrival in zip(spans_out, returned):
        result = place(*span, arrival, result)
    return result


def solution(mesh):
    return jax.shard_map(
        body,
        mesh=mesh,
        in_specs=(P(("grp", "mem"), None, None, None), P(), P(), P(), P()),
        out_specs=P(("grp", "mem"), None, None, None),
        check_vma=False,
    )
```

time: 166 us -> 147 us (0.89)
  Pallas kernels: 64.8 us -> 49.4 us
  waiting for transfers between devices: 57.1 us -> 47.9 us
  local copies, waits for them, and re-layouts: 2.38 us -> 6.78 us
    pallas_call x8 -> x10, Pallas kernels: 64.8 us -> 49.4 us  [call(): pl.pallas_call(kernel, out_shape=[pltpu.VMEM(shape, dtype) if is_near els...]
    ppermute x2, waiting for transfers between devices: 5.99 us -> 0.01 us  [body(): from_left = lax.ppermute(high, 'mem', rightward)]
    ppermute x2, waiting for transfers between devices: 9.54 us -> 3.58 us  [body(): from_right = lax.ppermute(low, 'mem', leftward)]
    unnamed x16 -> x32, local copies, waits for them, and re-layouts: 2.38 us -> 6.78 us
    all_to_all x4, waiting for transfers between devices: 41.6 us -> 44.4 us  [exchange(): lax.all_to_all(messages, 'mem', split_axis=0, concat_axis=0, tiled=True)]
    all_to_all x4, starting transfers between devices: 31.7 us -> 33.4 us  [exchange(): lax.all_to_all(messages, 'mem', split_axis=0, concat_axis=0, tiled=True)]
  transfers between devices with their start and end apart: 8 -> 8, of which waited for: 6 -> 5; matrix products, arithmetic and copies ran while one was open for 0% -> 0% of each run, Pallas kernels for 32% -> 26%
where the time goes in v2:
time: 147 us
  Pallas kernels  49.4 us (34%)
  waiting for transfers between devices  47.9 us (33%)
  starting transfers between devices  42.1 us (29%)
  local copies, waits for them, and re-layouts  6.78 us (5%)
    pallas_call x10, Pallas kernels, call(): pl.pallas_call(kernel, out_shape=[pltpu.VMEM(shape, dtype) if is_near els...  49.4 us
    all_to_all x4, waiting for transfers between devices, exchange(): lax.all_to_all(messages, 'mem', split_axis=0, concat_axis=0, tiled=True)  44.4 us
    all_to_all x4, starting transfers between devices, exchange(): lax.all_to_all(messages, 'mem', split_axis=0, concat_axis=0, tiled=True)  33.4 us
    unnamed x32, local copies, waits for them, and re-layouts  6.78 us
    ppermute x2, starting transfers between devices, body(): from_left = lax.ppermute(high, 'mem', rightward)  4.88 us
    ppermute x2, starting transfers between devices, body(): from_right = lax.ppermute(low, 'mem', leftward)  3.84 us
    ppermute x2, waiting for transfers between devices, body(): from_right = lax.ppermute(low, 'mem', leftward)  3.58 us
  transfers between devices with their start and end apart: 8, of which 5 were waited for; matrix products, arithmetic and copies ran while one was open for 0% of the time, Pallas kernels for 26%

profile of v2, /device:TPU:15, one launch (start us, length us, event | category | flops | bytes accessed | tf_op | source)
XLA Modules:
  0.0 146.6 jit_solution(8402527654177980719)
XLA Ops:
  0.0 9.7 %conv_slab.2 = bf16[16,9,16,256]{3,2,1,0:T(8,128)(2,1)} custom-call(bf16[4,16,64,256]{3,2,1,0:T(8,128)(2,1)} %field_hbm.3, f32[2,2,256]{2,1,0:T(2,128)} %gain_hbm.3, bf16[2,3,3,256,512]{4,3,2,1,0:T(8,128)(2,1)} %weight_hbm.3, bf16[256,256]{1,0:T(8,128)(2,1)} %constant.8.clone.order_hbm), custom_call_target="tpu_custom_call" | custom-call | flops 5435817984 | bytes 2359296 | tf_op jit(solution)/shard_map/conv_slab/pallas_call | solution.py:370
  9.8 6.6 %all-to-all-start = ((bf16[16,9,16,256]{3,2,1,0:T(8,128)(2,1)}), bf16[16,9,16,256]{3,2,1,0:T(8,128)(2,1)S(1)}, u32[]{:S(2)}, u32[]{:S(2)}) async-start(bf16[16,9,16,256]{3,2,1,0:T(8,128)(2,1)} %conv_slab.2), calls=%async_computation | async-start | bytes 2359296 | tf_op jit(solution)/shard_map/all_to_all | solution.py:441
  16.3 8.2 %conv_slab.3 = (bf16[16,7,16,256]{3,2,1,0:T(8,128)(2,1)}, f32[2,2,256]{2,1,0:T(2,128)S(1)}, bf16[3,3,256,512]{3,2,1,0:T(8,128)(2,1)S(1)}, bf16[2,512,256]{2,1,0:...) custom-call(bf16[4,16,64,256]{3,2,1,0:T(8,128)(2,1)} %field_hbm.3, ...), custom_call_target="tpu_custom_call" | custom-call | flops 4227858432 | bytes 1835008 | tf_op jit(solution)/shard_map/conv_slab/pallas_call | solution.py:370
  24.6 1.4 copy-done
  26.0 0.6 copy-done.13
  26.6 17.5 %all-to-all-done.arrived = bf16[16,9,16,256]{3,2,1,0:T(8,128)(2,1)S(1)} async-done(((bf16[16,9,16,256]{3,2,1,0:T(8,128)(2,1)}), bf16[16,9,16,256]{3,2,1,0:T(8,128)(2,1)S(1)}, u32[]{:S(2)}, u32[]{:S(2)}) %all-to-all-start) | async-done | bytes 1179680 | tf_op jit(solution)/shard_map/all_to_all | solution.py:441
  44.1 4.9 %all-to-all-start.2 = ((bf16[16,7,16,256]{3,2,1,0:T(8,128)(2,1)}), bf16[16,7,16,256]{3,2,1,0:T(8,128)(2,1)S(1)}, u32[]{:S(2)}, u32[]{:S(2)}) async-start(bf16[16,7,16,256]{3,2,1,0:T(8,128)(2,1)} %get-tuple-element.34), calls=%async_computation.2 | async-start | bytes 1835008 | tf_op jit(solution)/shard_map/all_to_all | solution.py:441
  49.0 0.9 copy-done.14
  49.9 4.7 %attend.2 = (bf16[9,256,256]{2,1,0:T(8,128)(2,1)S(1)}, bf16[9,256,256]{2,1,0:T(8,128)(2,1)S(1)}, bf16[9,64,256]{2,1,0:T(8,128)(2,1)S(1)}, bf16[9,64,256]{2,1,0:T(8,128)(2,1)S(1)}) custom-call(bf16[16,9,16,256]{3,2,1,0:T(8,128)(2,1)S(1)} %all-to-all-done.arrived, f32[2,2,256]{2,1,0:T(2,128)S(1)} %get-tuple-element.22.gain.refs_3_.refs_7_.refs_5_.refs_11_, ...), custom_call_target="tpu_custom_call" | custom-call | flops 1811939328 | bytes 4718592 | tf_op jit(solution)/shard_map/attend/pallas_call | solution.py:370
  54.6 0.0 copy-start.3
  54.6 2.4 %collective-permute-start = (bf16[9,64,256]{2,1,0:T(8,128)(2,1)S(1)}, bf16[9,64,256]{2,1,0:T(8,128)(2,1)S(1)}, u32[]{:S(2)}, u32[]{:S(2)}) collective-permute-start(bf16[9,64,256]{2,1,0:T(8,128)(2,1)S(1)} %get-tuple-element.29), channel_id=1, source_target_pairs={{0,1},{1,2},{2,3},{3,6},{6,7},{7,4},{4,5},{5,8},{8,9},{9,10},{10,1... | collective-permute-start | bytes 884744 | tf_op jit(solution)/shard_map/ppermute | solution.py:511
  57.1 1.9 %collective-permute-start.1 = (bf16[9,64,256]{2,1,0:T(8,128)(2,1)S(1)}, bf16[9,64,256]{2,1,0:T(8,128)(2,1)S(1)}, u32[]{:S(2)}, u32[]{:S(2)}) collective-permute-start(bf16[9,64,256]{2,1,0:T(8,128)(2,1)S(1)} %get-tuple-element.30), channel_id=1, source_target_pairs={{1,0},{2,1},{3,2},{6,3},{7,6},{4,7},{5,4},{8,5},{9,8},{10,9},{11,1... | collective-permute-start | bytes 884744 | tf_op jit(solution)/shard_map/ppermute | solution.py:512
  59.0 0.9 copy-done.8
  59.9 0.9 copy-done.11
  60.9 4.4 %conv_inner.2.refs_4_ = bf16[8,128,256]{2,1,0:T(8,128)(2,1)S(1)} custom-call(bf16[9,256,256]{2,1,0:T(8,128)(2,1)S(1)} %get-tuple-element.27.refs_0_, bf16[9,256,256]{2,1,0:T(8,128)(2,1)S(1)} %get-tuple-element.28.refs_1_.refs_2_, bf16[3,3,256,512]{3,2,1,0:T(8,128)(2,1)S(1)} %copy-done.1, ...), custom_call_target="tpu_custom_call" | custom-call | flops 3221225472 | bytes 4194304 | tf_op jit(solution)/shard_map/conv_inner/pallas_call | solution.py:370
  65.3 0.0 collective-permute-done.refs_2_.refs_4_
  65.3 2.4 %collective-permute-done.1.refs_3_.refs_6_ = bf16[9,64,256]{2,1,0:T(8,128)(2,1)S(1)} collective-permute-done((bf16[9,64,256]{2,1,0:T(8,128)(2,1)S(1)}, bf16[9,64,256]{2,1,0:T(8,128)(2,1)S(1)}, u32[]{:S(2)}, u32[]{:S(2)}) %collective-permute-start.1) | collective-permute-done | bytes 294944 | tf_op jit(solution)/shard_map/ppermute | solution.py:512
  67.7 5.6 %conv_edges.2 = bf16[16,8,16,256]{3,2,1,0:T(8,128)(2,1)} custom-call(bf16[9,256,256]{2,1,0:T(8,128)(2,1)S(1)} %get-tuple-element.27.refs_0_, bf16[9,256,256]{2,1,0:T(8,128)(2,1)S(1)} %get-tuple-element.28.refs_1_.refs_2_, bf16[9,64,256]{2,1,0:T(8,128)(2,1)S(1)} %collective-permute-done.refs_2_.refs_4_, ...), custom_call_target="tpu_custom_call" | custom-call | flops 3221225472 | bytes 4194304 | tf_op jit(solution)/shard_map/conv_edges/pallas_call | solution.py:370
  73.3 10.2 %all-to-all-start.1 = ((bf16[16,8,16,256]{3,2,1,0:T(8,128)(2,1)}), bf16[16,8,16,256]{3,2,1,0:T(8,128)(2,1)S(1)}, u32[]{:S(2)}, u32[]{:S(2)}) async-start(bf16[16,8,16,256]{3,2,1,0:T(8,128)(2,1)} %conv_edges.2), calls=%async_computation.1 | async-start | bytes 2097152 | tf_op jit(solution)/shard_map/all_to_all | solution.py:441
  83.5 0.9 copy-done.9
  84.5 0.9 copy-done.12
  85.4 3.8 %attend.3 = (bf16[7,256,256]{2,1,0:T(8,128)(2,1)S(1)}, bf16[7,256,256]{2,1,0:T(8,128)(2,1)S(1)}, bf16[7,64,256]{2,1,0:T(8,128)(2,1)S(1)}, bf16[7,64,256]{2,1,0:T(8,128)(2,1)S(1)}) custom-call(bf16[16,7,16,256]{3,2,1,0:T(8,128)(2,1)S(1)} %all-to-all-done.2.arrived, f32[2,2,256]{2,1,0:T(2,128)S(1)} %get-tuple-element.22.gain.refs_3_.refs_7_.refs_5_.refs_11_, ...), custom_call_target="tpu_custom_call" | custom-call | flops 1409286144 | bytes 3670016 | tf_op jit(solution)/shard_map/attend/pallas_call | solution.py:370
  89.2 2.4 %collective-permute-start.2 = (bf16[7,64,256]{2,1,0:T(8,128)(2,1)S(1)}, bf16[7,64,256]{2,1,0:T(8,128)(2,1)S(1)}, u32[]{:S(2)}, u32[]{:S(2)}) collective-permute-start(bf16[7,64,256]{2,1,0:T(8,128)(2,1)S(1)} %get-tuple-element.37), channel_id=1, source_target_pairs={{0,1},{1,2},{2,3},{3,6},{6,7},{7,4},{4,5},{5,8},{8,9},{9,10},{10,1... | collective-permute-start | bytes 688136 | tf_op jit(solution)/shard_map/ppermute | solution.py:511
  91.7 1.9 %collective-permute-start.3 = (bf16[7,64,256]{2,1,0:T(8,128)(2,1)S(1)}, bf16[7,64,256]{2,1,0:T(8,128)(2,1)S(1)}, u32[]{:S(2)}, u32[]{:S(2)}) collective-permute-start(bf16[7,64,256]{2,1,0:T(8,128)(2,1)S(1)} %get-tuple-element.38), channel_id=1, source_target_pairs={{1,0},{2,1},{3,2},{6,3},{7,6},{4,7},{5,4},{8,5},{9,8},{10,9},{11,1... | collective-permute-start | bytes 688136 | tf_op jit(solution)/shard_map/ppermute | solution.py:512
  93.6 4.4 %conv_inner.3.refs_8_ = bf16[8,128,256]{2,1,0:T(8,128)(2,1)S(1)} custom-call(bf16[9,256,256]{2,1,0:T(8,128)(2,1)S(1)} %copy-done.4, bf16[7,256,256]{2,1,0:T(8,128)(2,1)S(1)} %get-tuple-element.35.refs_1_, bf16[9,256,256]{2,1,0:T(8,128)(2,1)S(1)} %copy-done.6, bf16[7,256,256]{2,1,0:T(8,128)(2,1)S(1)} %get-tuple-element.36.refs_3_, ...), custom_call_target="tpu_custom_call" | custom-call | flops 3221225472 | bytes 4194304 | tf_op jit(solution)/shard_map/conv_inner/pallas_call | solution.py:370
  98.1 1.2 collective-permute-done.3.refs_7_
  99.3 5.6 %conv_edges.3 = bf16[16,8,16,256]{3,2,1,0:T(8,128)(2,1)} custom-call(bf16[9,256,256]{2,1,0:T(8,128)(2,1)S(1)} %copy-done.4, bf16[7,256,256]{2,1,0:T(8,128)(2,1)S(1)} %get-tuple-element.35.refs_1_, bf16[9,256,256]{2,1,0:T(8,128)(2,1)S(1)} %copy-done.6, bf16[7,256,256]{2,1,0:T(8,128)(2,1)S(1)} %get-tuple-element.36.refs_3_, ...), custom_call_target="tpu_custom_call" | custom-call | flops 3221225472 | bytes 4194304 | tf_op jit(solution)/shard_map/conv_edges/pallas_call | solution.py:370
  104.9 3.5 %all-to-all-done.1.refs_0_ = bf16[16,8,16,256]{3,2,1,0:T(8,128)(2,1)S(1)} async-done(((bf16[16,8,16,256]{3,2,1,0:T(8,128)(2,1)}), bf16[16,8,16,256]{3,2,1,0:T(8,128)(2,1)S(1)}, u32[]{:S(2)}, u32[]{:S(2)}) %all-to-all-start.1) | async-done | bytes 1048608 | tf_op jit(solution)/shard_map/all_to_all | solution.py:441
  108.4 11.7 %all-to-all-start.3 = ((bf16[16,8,16,256]{3,2,1,0:T(8,128)(2,1)}), bf16[16,8,16,256]{3,2,1,0:T(8,128)(2,1)S(1)}, u32[]{:S(2)}, u32[]{:S(2)}) async-start(bf16[16,8,16,256]{3,2,1,0:T(8,128)(2,1)} %conv_edges.3), calls=%async_computation.3 | async-start | bytes 2097152 | tf_op jit(solution)/shard_map/all_to_all | solution.py:441
  120.1 1.5 %place.2.refs_0_ = bf16[4,16,64,256]{3,2,1,0:T(8,128)(2,1)} custom-call(bf16[16,8,16,256]{3,2,1,0:T(8,128)(2,1)S(1)} %all-to-all-done.1.refs_0_, bf16[256,256]{1,0:T(8,128)(2,1)S(1)} %get-tuple-element.33.refs_1_.refs_2_), custom_call_target="tpu_custom_call" | custom-call | flops 268435456 | bytes 2097152 | tf_op jit(solution)/shard_map/place/pallas_call | solution.py:370
  121.6 23.4 %all-to-all-done.3.refs_1_ = bf16[16,8,16,256]{3,2,1,0:T(8,128)(2,1)S(1)} async-done(((bf16[16,8,16,256]{3,2,1,0:T(8,128)(2,1)}), bf16[16,8,16,256]{3,2,1,0:T(8,128)(2,1)S(1)}, u32[]{:S(2)}, u32[]{:S(2)}) %all-to-all-start.3) | async-done | bytes 1048608 | tf_op jit(solution)/shard_map/all_to_all | solution.py:441
  145.0 1.5 %place.3 = bf16[4,16,64,256]{3,2,1,0:T(8,128)(2,1)} custom-call(bf16[4,16,64,256]{3,2,1,0:T(8,128)(2,1)} %place.2.refs_0_, bf16[16,8,16,256]{3,2,1,0:T(8,128)(2,1)S(1)} %all-to-all-done.3.refs_1_, bf16[256,256]{1,0:T(8,128)(2,1)S(1)} %get-tuple-element.33.refs_1_.refs_2_), custom_call_target="tpu_custom_call", output_to_operand_aliasing={{}: (0, {})} | custom-call | flops 268435456 | bytes 2097152 | tf_op jit(solution)/shard_map/place/pallas_call | solution.py:370
  (26 shorter events, 0.0 us)
Async XLA Ops:
  9.8 34.3 %all-to-all-start = ((bf16[16,9,16,256]{3,2,1,0:T(8,128)(2,1)}), bf16[16,9,16,256]{3,2,1,0:T(8,128)(2,1)S(1)}, u32[]{:S(2)}, u32[]{:S(2)}) async-start(bf16[16,9,16,256]{3,2,1,0:T(8,128)(2,1)} %conv_slab.2), calls=%async_computation | async-start | bytes 2359296 | tf_op jit(solution)/shard_map/all_to_all | solution.py:441
  24.6 1.4 copy-start
  26.0 0.6 copy-start.13
  26.6 27.9 %copy-start.7 = (bf16[2,256,256]{2,1,0:T(8,128)(2,1)}, bf16[2,256,256]{2,1,0:T(8,128)(2,1)S(1)}, u32[]{:S(2)}) copy-start(bf16[2,256,256]{2,1,0:T(8,128)(2,1)S(1)} %get-tuple-element.24.wk.refs_5_.refs_9_.refs_7_.refs_13_) | copy-start | bytes 786436
  26.6 28.0 %copy-start.10 = (bf16[2,256,256]{2,1,0:T(8,128)(2,1)}, bf16[2,256,256]{2,1,0:T(8,128)(2,1)S(1)}, u32[]{:S(2)}) copy-start(bf16[2,256,256]{2,1,0:T(8,128)(2,1)S(1)} %get-tuple-element.25.wout.refs_6_.refs_10_.refs_8_.refs_14_) | copy-start | bytes 786436
  44.1 29.2 %all-to-all-start.2 = ((bf16[16,7,16,256]{3,2,1,0:T(8,128)(2,1)}), bf16[16,7,16,256]{3,2,1,0:T(8,128)(2,1)S(1)}, u32[]{:S(2)}, u32[]{:S(2)}) async-start(bf16[16,7,16,256]{3,2,1,0:T(8,128)(2,1)} %get-tuple-element.34), calls=%async_computation.2 | async-start | bytes 1835008 | tf_op jit(solution)/shard_map/all_to_all | solution.py:441
  49.0 0.9 copy-start.14
  49.9 9.1 %copy-start.1 = (bf16[3,3,256,512]{3,2,1,0:T(8,128)(2,1)S(1)}, bf16[3,3,256,512]{3,2,1,0:T(8,128)(2,1)}, u32[]{:S(2)}) copy-start(bf16[3,3,256,512]{3,2,1,0:T(8,128)(2,1)} %copy-done) | copy-start | bytes 7077892
  54.6 13.1 %copy-start.3 = (bf16[9,256,256]{2,1,0:T(8,128)(2,1)}, bf16[9,256,256]{2,1,0:T(8,128)(2,1)S(1)}, u32[]{:S(2)}) copy-start(bf16[9,256,256]{2,1,0:T(8,128)(2,1)S(1)} %get-tuple-element.27.refs_0_) | copy-start | bytes 3538948
  54.6 13.1 %copy-start.5 = (bf16[9,256,256]{2,1,0:T(8,128)(2,1)}, bf16[9,256,256]{2,1,0:T(8,128)(2,1)S(1)}, u32[]{:S(2)}) copy-start(bf16[9,256,256]{2,1,0:T(8,128)(2,1)S(1)} %get-tuple-element.28.refs_1_.refs_2_) | copy-start | bytes 3538948
  54.6 10.7 %collective-permute-start = (bf16[9,64,256]{2,1,0:T(8,128)(2,1)S(1)}, bf16[9,64,256]{2,1,0:T(8,128)(2,1)S(1)}, u32[]{:S(2)}, u32[]{:S(2)}) collective-permute-start(bf16[9,64,256]{2,1,0:T(8,128)(2,1)S(1)} %get-tuple-element.29), channel_id=1, source_target_pairs={{0,1},{1,2},{2,3},{3,6},{6,7},{7,4},{4,5},{5,8},{8,9},{9,10},{10,1... | collective-permute-start | bytes 884744 | tf_op jit(solution)/shard_map/ppermute | solution.py:511
  57.1 10.6 %collective-permute-start.1 = (bf16[9,64,256]{2,1,0:T(8,128)(2,1)S(1)}, bf16[9,64,256]{2,1,0:T(8,128)(2,1)S(1)}, u32[]{:S(2)}, u32[]{:S(2)}) collective-permute-start(bf16[9,64,256]{2,1,0:T(8,128)(2,1)S(1)} %get-tuple-element.30), channel_id=1, source_target_pairs={{1,0},{2,1},{3,2},{6,3},{7,6},{4,7},{5,4},{8,5},{9,8},{10,9},{11,1... | collective-permute-start | bytes 884744 | tf_op jit(solution)/shard_map/ppermute | solution.py:512
  59.0 1.0 copy-start.8
  59.9 0.9 copy-start.11
  73.3 10.2 %copy-start.15 = (bf16[256,256]{1,0:T(8,128)(2,1)S(1)}, bf16[256,256]{1,0:T(8,128)(2,1)}, u32[]{:S(2)}) copy-start(bf16[256,256]{1,0:T(8,128)(2,1)} %copy-done.13) | copy-start | bytes 393220
  73.3 35.1 %all-to-all-start.1 = ((bf16[16,8,16,256]{3,2,1,0:T(8,128)(2,1)}), bf16[16,8,16,256]{3,2,1,0:T(8,128)(2,1)S(1)}, u32[]{:S(2)}, u32[]{:S(2)}) async-start(bf16[16,8,16,256]{3,2,1,0:T(8,128)(2,1)} %conv_edges.2), calls=%async_computation.1 | async-start | bytes 2097152 | tf_op jit(solution)/shard_map/all_to_all | solution.py:441
  83.5 1.0 copy-start.9
  84.5 0.9 copy-start.12
  85.4 8.2 %copy-start.2 = (bf16[3,3,256,512]{3,2,1,0:T(8,128)(2,1)S(1)}, bf16[3,3,256,512]{3,2,1,0:T(8,128)(2,1)}, u32[]{:S(2)}) copy-start(bf16[3,3,256,512]{3,2,1,0:T(8,128)(2,1)} %copy-done) | copy-start | bytes 7077892
  85.4 8.2 %copy-start.4 = (bf16[9,256,256]{2,1,0:T(8,128)(2,1)S(1)}, bf16[9,256,256]{2,1,0:T(8,128)(2,1)}, u32[]{:S(2)}) copy-start(bf16[9,256,256]{2,1,0:T(8,128)(2,1)} %copy-done.3) | copy-start | bytes 3538948
  85.4 8.2 %copy-start.6 = (bf16[9,256,256]{2,1,0:T(8,128)(2,1)S(1)}, bf16[9,256,256]{2,1,0:T(8,128)(2,1)}, u32[]{:S(2)}) copy-start(bf16[9,256,256]{2,1,0:T(8,128)(2,1)} %copy-done.5) | copy-start | bytes 3538948
  89.2 8.8 %collective-permute-start.2 = (bf16[7,64,256]{2,1,0:T(8,128)(2,1)S(1)}, bf16[7,64,256]{2,1,0:T(8,128)(2,1)S(1)}, u32[]{:S(2)}, u32[]{:S(2)}) collective-permute-start(bf16[7,64,256]{2,1,0:T(8,128)(2,1)S(1)} %get-tuple-element.37), channel_id=1, source_target_pairs={{0,1},{1,2},{2,3},{3,6},{6,7},{7,4},{4,5},{5,8},{8,9},{9,10},{10,1... | collective-permute-start | bytes 688136 | tf_op jit(solution)/shard_map/ppermute | solution.py:511
  91.7 7.6 %collective-permute-start.3 = (bf16[7,64,256]{2,1,0:T(8,128)(2,1)S(1)}, bf16[7,64,256]{2,1,0:T(8,128)(2,1)S(1)}, u32[]{:S(2)}, u32[]{:S(2)}) collective-permute-start(bf16[7,64,256]{2,1,0:T(8,128)(2,1)S(1)} %get-tuple-element.38), channel_id=1, source_target_pairs={{1,0},{2,1},{3,2},{6,3},{7,6},{4,7},{5,4},{8,5},{9,8},{10,9},{11,1... | collective-permute-start | bytes 688136 | tf_op jit(solution)/shard_map/ppermute | solution.py:512
  108.4 36.6 %all-to-all-start.3 = ((bf16[16,8,16,256]{3,2,1,0:T(8,128)(2,1)}), bf16[16,8,16,256]{3,2,1,0:T(8,128)(2,1)S(1)}, u32[]{:S(2)}, u32[]{:S(2)}) async-start(bf16[16,8,16,256]{3,2,1,0:T(8,128)(2,1)} %conv_edges.3), calls=%async_computation.3 | async-start | bytes 2097152 | tf_op jit(solution)/shard_map/all_to_all | solution.py:441

commit v3 on v2

--- a/solution.py
+++ b/solution.py
@@ -14,6 +14,10 @@
 epsilon = 1e-06
 VMEM_LIMIT = 40 * 1024 * 1024
 UNROLL = 4
+CUTS = (7,)
+AHEAD = 0
+SPLIT_TILE = True
+WQ_T, WV_T, WK, WOUT, ORDER, FINAL = range(6)
 
 F32 = jnp.float32
 BF16 = jnp.bfloat16
@@ -74,14 +78,15 @@
     return [(edges[k], edges[k + 1]) for k in range(pieces)]
 
 
-def attention_rows(state, gain, wqv_t, wk, wout, members):
+def attention_rows(state, gain, squares, members):
     total, channels = state.shape
     size = channels // HEADS
     group = LANES // size
     packed = LANES // members
     factor = float(np.log2(np.e) / np.sqrt(size))
     normed = normalize(state, gain).astype(BF16)
-    keys = jnp.dot(normed, wk, preferred_element_type=F32).astype(BF16)
+    keys = jnp.dot(normed, squares[WK], preferred_element_type=F32).astype(BF16)
+    wqv_t = squares[WQ_T : WV_T + 1].reshape(2 * channels, channels)
     qv_t = lax.dot_general(
         wqv_t, normed, (((1,), (1,)), ((), ())), preferred_element_type=F32
     ).astype(BF16)
@@ -140,7 +145,7 @@
         columns.append(jnp.concatenate(pieces, axis=0))
     attended_t = jnp.concatenate(columns, axis=1)
     update = lax.dot_general(
-        attended_t, wout, (((0,), (0,)), ((), ())), preferred_element_type=F32
+        attended_t, squares[WOUT], (((0,), (0,)), ((), ())), preferred_element_type=F32
     )
     return state + update
 
@@ -166,11 +171,11 @@
     layer, first, last, staging, field_hbm, gain_hbm, weight_hbm, order_hbm, *refs,
 ):
     if staging:
-        (qkv_hbm, wout_hbm, to_tile_hbm, from_tile_hbm, to_slab_hbm, out,
-         later_gain, later_weight, wqv_t, wk, wout, to_tile, from_tile, to_slab,
-         field, gain, weight, order, padded, qkv, semaphores) = refs
+        (qkv_hbm, wout_hbm, to_tile_hbm, from_tile_hbm, to_slab_hbm, out_hbm,
+         later_gain, later_weight, stacks,
+         field, gain, weight, order, padded, out, qkv, semaphores) = refs
     else:
-        out, field, gain, weight, order, padded, semaphores = refs
+        out_hbm, field, gain, weight, order, padded, out, semaphores = refs
     local, rows, cols, channels = field_hbm.shape
     count = local * cols
     copies = Copies(semaphores)
@@ -185,17 +190,18 @@
         fields.append(copies.start(field_hbm.at[:, ready:needed], field.at[:, part]))
         ready = needed
         if k == 0:
-            late.append(copies.start(weight_hbm.at[layer], weight))
-            late.append(copies.start(order_hbm, order))
+            late = [copies.start(weight_hbm.at[layer, di], weight.at[di]) for di in range(3)]
+            order_copy = copies.start(order_hbm, order)
     if staging:
         staged = [
             copies.start(qkv_hbm, qkv),
             copies.start(gain_hbm, later_gain),
             copies.start(weight_hbm.at[layer + 1], later_weight),
-            copies.start(wout_hbm, wout),
-            copies.start(to_tile_hbm, to_tile),
-            copies.start(from_tile_hbm, from_tile),
-            copies.start(to_slab_hbm, to_slab),
+            copies.start(wout_hbm.at[0], stacks.at[0, WOUT]),
+            copies.start(wout_hbm.at[1], stacks.at[1, WOUT]),
+            copies.start(to_tile_hbm, stacks.at[0, ORDER]),
+            copies.start(from_tile_hbm, stacks.at[1, ORDER]),
+            copies.start(to_slab_hbm, stacks.at[0, FINAL]),
         ]
     column = lax.broadcasted_iota(jnp.int32, (count, 1), 0) % cols
     zeros = jnp.zeros(padded.shape[1:], BF16)
@@ -217,53 +223,75 @@
         padded[slot, 2] = right.astype(BF16)
 
     ready = low
+    outputs = []
     for k, (begin, end) in enumerate(groups):
         needed = min(first + end + 1, rows)
         fields[k].wait()
         for row in range(ready, needed):
             prepare(row)
         ready = needed
-        if k == 0:
-            wait_all(late)
         taps = [
             jnp.concatenate(
-                [padded[i + di, dj] for di in range(3) for dj in range(3)], axis=1
+                [
+                    jnp.concatenate([padded[i + di, dj] for dj in range(3)], axis=1)
+                    for i in range(begin, end)
+                ],
+                axis=0,
             )
-            for i in range(begin, end)
+            for di in range(3)
         ]
-        conv_out = jnp.dot(
-            jnp.concatenate(taps, axis=0),
-            weight[...].reshape(9 * channels, 2 * channels),
-            preferred_element_type=F32,
-        )
+        if k == 0:
+            conv_out = 0.0
+            for di in range(3):
+                late[di].wait()
+                conv_out += jnp.dot(
+                    taps[di],
+                    weight[di].reshape(3 * channels, 2 * channels),
+                    preferred_element_type=F32,
+                )
+            order_copy.wait()
+        else:
+            conv_out = jnp.dot(
+                jnp.concatenate(taps, axis=1),
+                weight[...].reshape(9 * channels, 2 * channels),
+                preferred_element_type=F32,
+            )
         update = gated(conv_out, channels)
         for i in range(begin, end):
             widened = field[:, first + i - low].reshape(count, channels).astype(F32)
             part = update[(i - begin) * count : (i - begin + 1) * count]
             moved = shuffled(order[...], (widened + part).astype(BF16))
             out[:, i] = moved.reshape(out.shape[0], out.shape[2], channels).astype(BF16)
+        outputs.append(copies.start(out.at[:, begin:end], out_hbm.at[:, begin:end]))
     if staging:
         wait_all(staged)
         for b in range(BLOCKS):
-            wqv_t[b, :channels] = qkv[b, :, :channels].T
-            wqv_t[b, channels:] = qkv[b, :, 2 * channels :].T
-            wk[b] = qkv[b, :, channels : 2 * channels]
+            stacks[b, WQ_T] = qkv[b, :, :channels].T
+            stacks[b, WV_T] = qkv[b, :, 2 * channels :].T
+            stacks[b, WK] = qkv[b, :, channels : 2 * channels]
+    wait_all(outputs)
 
 
 def attend_kernel(
-    layer, members, arrived, gain, wqv_t, wk, wout, order, state, normed, low, high,
+    layer, members, arrived, gain, stacks, state, normed, low, high, *local_copy,
 ):
     total, count, channels = state.shape
+    squares = stacks.at[layer]
+    if local_copy:
+        copy = pltpu.make_async_copy(arrived, local_copy[0], local_copy[1].at[0])
+        copy.start()
+        copy.wait()
+        arrived = local_copy[0]
     for begin, end in groups_of(total):
         joined = jnp.concatenate(
             [
-                shuffled(order[...], arrived[:, i].reshape(count, channels))
+                shuffled(squares[ORDER], arrived[:, i].reshape(count, channels))
                 for i in range(begin, end)
             ],
             axis=0,
         )
         joined = attention_rows(
-            joined, gain[layer, 1:2], wqv_t[layer], wk[layer], wout[layer], members
+            joined, gain[layer, 1:2], squares, members
         ).astype(BF16)
         following = normalize(joined.astype(F32), gain[layer + 1, 0:1]).astype(BF16)
         for i in range(begin, end):
@@ -281,8 +309,16 @@
     if halo:
         lows, refs = refs[:pieces], refs[pieces:]
         highs, refs = refs[:pieces], refs[pieces:]
-        inner, order, refs = refs[0], refs[1], refs[2:]
-    weight, gain, wqv_t, wk, wout, out = refs
+        if len(cells) * members < states[0].shape[1]:
+            inner, partial, refs = *refs[:2], refs[2:]
+    if halo:
+        gain, stacks, weight, out_hbm, out, semaphores = refs
+        copies = Copies(semaphores)
+    else:
+        gain, stacks, weight, out, partial = refs
+    squares = stacks.at[layer]
+    end_cell = states[0].shape[1] // members - 1
+    outputs = []
     count, channels = states[0].shape[1:]
     total = last - first
     size = len(cells) * members
@@ -307,7 +343,7 @@
         k, place = piece_of(row)
         return states[k][place, cell * members : (cell + 1) * members]
 
-    for begin, end in groups_of(total, UNROLL * count // size):
+    def conv(begin, end, cells, sides):
         taps = [
             jnp.concatenate(
                 [
@@ -315,23 +351,40 @@
                         [tap(first + i + di - 1, cell + dj - 1) for cell in cells], axis=0
                     )
                     for di in range(3)
-                    for dj in range(3)
+                    for dj in sides
                 ],
                 axis=1,
             )
             for i in range(begin, end)
         ]
-        conv_out = jnp.dot(
+        return jnp.dot(
             jnp.concatenate(taps, axis=0),
-            weight[...].reshape(9 * channels, 2 * channels),
+            weight[:, sides.start : sides.stop].reshape(3 * len(sides) * channels, 2 * channels),
             preferred_element_type=F32,
         )
+
+    for begin, end in groups_of(total, UNROLL * count // size):
+        run = end - begin
+        if not halo or size == count:
+            conv_out = conv(begin, end, cells, range(3))
+        else:
+            beside = [
+                conv(begin, end, cells[:1], range(1)).reshape(run, members, 2 * channels),
+                conv(begin, end, cells[1:], range(2, 3)).reshape(run, members, 2 * channels),
+            ]
+            conv_out = jnp.concatenate(beside, axis=1) + partial[begin:end]
+            conv_out = conv_out.reshape(run * size, 2 * channels)
+        if not halo:
+            own = conv(begin, end, (0,), range(1, 3))
+            partial[begin:end, :members] = own.reshape(run, members, 2 * channels)
+            own = conv(begin, end, (end_cell,), range(2))
+            partial[begin:end, members:] = own.reshape(run, members, 2 * channels)
         joined = jnp.concatenate(
             [held(first + i, cell) for i in range(begin, end) for cell in cells], axis=0
         ).astype(F32)
         joined = (joined + gated(conv_out, channels)).astype(BF16).astype(F32)
         joined = attention_rows(
-            joined, gain[layer, 1:2], wqv_t[layer], wk[layer], wout[layer], members
+            joined, gain[layer, 1:2], squares, members
         ).astype(BF16)
         for i in range(begin, end):
             own = joined[(i - begin) * size : (i - begin + 1) * size]
@@ -339,20 +392,29 @@
                 full = jnp.concatenate(
                     [own[:members], inner[i], own[members:]] if size < count else [own], axis=0
                 )
-                moved = shuffled(order[...], full)
+                moved = shuffled(squares[ORDER], full)
                 out[:, i] = moved.reshape(out.shape[0], out.shape[2], channels).astype(BF16)
             else:
                 out[i] = own
-
-
-def place_kernel(first, *refs):
-    arrived, order, out_hbm, out, semaphores = refs[-5:]
+        if halo:
+            outputs.append(copies.start(out.at[:, begin:end], out_hbm.at[:, begin:end]))
+    wait_all(outputs)
+
+
+def place_kernel(first, earlier, *refs):
+    if earlier:
+        arrived, stacks, out_hbm, out, semaphores = refs[-5:]
+    else:
+        arrived_hbm, stacks, out_hbm, arrived, out, semaphores = refs
+        copy = pltpu.make_async_copy(arrived_hbm, arrived, semaphores.at[31])
+        copy.start()
+        copy.wait()
     local, total, cols, channels = out.shape
     copies = Copies(semaphores)
     outputs = []
     for begin, end in groups_of(total, 2):
         for i in range(begin, end):
-            moved = shuffled(order[...], arrived[:, i].reshape(local * cols, channels))
+            moved = shuffled(stacks[0, FINAL], arrived[:, i].reshape(local * cols, channels))
             out[:, i] = moved.reshape(local, cols, channels).astype(BF16)
         outputs.append(
             copies.start(out.at[:, begin:end], out_hbm.at[:, first + begin : first + end])
@@ -360,7 +422,9 @@
     wait_all(outputs)
 
 
-def call(kernel, name, far, near, outs, scratch, flops, moved, transcendentals=0, aliases=None):
+def call(
+    kernel, name, far, near, outs, scratch, flops, moved, transcendentals=0, aliases=None
+):
     far = [pltpu.with_memory_space_constraint(x, pltpu.HBM) for x in far]
     near = [pltpu.with_memory_space_constraint(x, pltpu.VMEM) for x in near]
     anywhere, vmem = pl.BlockSpec(memory_space=pl.ANY), pl.BlockSpec(memory_space=pltpu.VMEM)
@@ -370,7 +434,7 @@
     return pl.pallas_call(
         kernel,
         out_shape=[
-            pltpu.VMEM(shape, dtype) if is_near else jax.ShapeDtypeStruct(shape, dtype)
+            (pltpu.VMEM if is_near else pltpu.HBM)(shape, dtype)
             for shape, dtype, is_near in outs
         ],
         in_specs=[anywhere] * len(far) + [vmem] * len(near),
@@ -385,6 +449,13 @@
     )(*far, *near)
 
 
+def chunks(rows):
+    edges = [0, *(round(rows * cut / 16) for cut in CUTS), rows]
+    inner = [edge - 1 for edge in edges[1:-1]]
+    outer = [0, *inner, rows]
+    return tuple(zip(edges, edges[1:])), tuple(zip(outer, outer[1:]))
+
+
 def body(field, norm_gain, conv_weight, qkv_weight, out_weight):
     local, rows, cols, channels = field.shape
     devices = lax.axis_size("mem")
@@ -396,10 +467,7 @@
     taps = conv_weight.shape[1] * conv_weight.shape[2] * channels
     conv_shape = conv_weight.shape[1:]
 
-    split_in = rows // 2 + 1
-    split_out = split_in - 1
-    spans_in = ((0, split_in), (split_in, rows))
-    spans_out = ((0, split_out), (split_out, rows))
+    spans_in, spans_out = chunks(rows)
     square = ((count, count), BF16)
 
     def conv_slab(first, last):
@@ -407,23 +475,23 @@
         held = min(last + 1, rows) - max(first - 1, 0)
         staging = last == rows
         far = [field, norm_gain, conv_weight, to_message]
-        outs = [((devices, total, block, channels), BF16, True)]
+        messages = (devices, total, block, channels)
+        outs = [(messages, BF16, False)]
         scratch = [
             ((local, held, cols, channels), BF16),
             (norm_gain.shape, F32),
             (conv_shape, BF16),
             square,
             ((total + 2, 3, count, channels), BF16),
+            (messages, BF16),
         ]
         if staging:
             far += [qkv_weight, out_weight, to_tile, from_tile, to_slab]
             outs += [
                 (norm_gain.shape, F32, True),
                 (conv_shape, BF16, True),
-                ((BLOCKS, 2 * channels, channels), BF16, True),
-                ((BLOCKS, channels, channels), BF16, True),
-                (out_weight.shape, BF16, True),
-            ] + [(*square, True)] * 3
+                ((BLOCKS, 6, channels, channels), BF16, True),
+            ]
             scratch.append((qkv_weight.shape, BF16))
         return call(
             functools.partial(conv_slab_kernel, 0, first, last, staging),
@@ -449,32 +517,27 @@
     for span in spans_in:
         messages, *staged = conv_slab(*span)
         arrived.append(exchange(messages))
-    gain, later_weight, wqv_t, wk, wout, to_tile, from_tile, to_slab = staged
-
-    def attend(arrival):
+    gain, later_weight, stacks = staged
+
+    def attend(arrival, is_far):
         total = arrival.shape[1]
         whole, edge = (total, count, channels), (total, members, channels)
         return call(
             functools.partial(attend_kernel, 0, members),
             "attend",
-            [],
-            [arrival, gain, wqv_t, wk, wout, to_tile],
+            [arrival] if is_far else [],
+            [gain, stacks] if is_far else [arrival, gain, stacks],
             [(shape, BF16, True) for shape in (whole, whole, edge, edge)],
-            [],
+            [(arrival.shape, BF16)] if is_far else [],
             2 * total * count * channels * 6 * channels,
             8 * total * count * channels,
             total * count * members * HEADS,
         )
 
-    def conv_tile(first, last, spans, parts, inner):
+    def conv_tile(first, last, spans, parts, cells, halo, inner=()):
         total = last - first
-        halo = inner is not None
-        cells = (0, width - 1) if halo else tuple(range(1, width - 1))
-        if not cells:
-            return jnp.zeros((1, members, channels), BF16)
         operands = [p[k] for k in range(4 if halo else 2) for p in parts]
-        if halo:
-            operands += [inner, from_tile]
+        operands += inner
         size = len(cells) * members
         shape = (devices, total, block, channels) if halo else (total, size, channels)
         return call(
@@ -483,41 +546,53 @@
             ),
             "conv_edges" if halo else "conv_inner",
             [],
-            [*operands, later_weight, gain, wqv_t, wk, wout],
-            [(shape, BF16, True)],
-            [],
+            [*operands, gain, stacks, later_weight],
+            [(shape, BF16, not halo)]
+            + ([] if halo else [((total, 2 * members, 2 * channels), F32, True)]),
+            [(shape, BF16)] if halo else [],
             2 * total * size * channels * (6 * channels + 2 * taps),
             8 * total * count * channels,
             total * size * members * HEADS,
-        )[0]
+        )
 
     def place(first, last, arrival, earlier):
         total = last - first
         return call(
-            functools.partial(place_kernel, first),
+            functools.partial(place_kernel, first, earlier is not None),
             "place",
-            [] if earlier is None else [earlier],
-            [arrival, to_slab],
+            [arrival] if earlier is None else [earlier],
+            [stacks] if earlier is None else [arrival, stacks],
             [((local, rows, cols, channels), BF16, False)],
-            [((local, total, cols, channels), BF16)],
+            ([(arrival.shape, BF16)] if earlier is None else [])
+            + [((local, total, cols, channels), BF16)],
             2 * total * count * count * channels,
             4 * total * count * channels,
             aliases={} if earlier is None else {0: 0},
         )[0]
 
-    parts = []
-    for arrival in arrived:
-        state, normed, low, high = attend(arrival)
+    parts, returned = [], []
+
+    def attend_chunk(k):
+        state, normed, low, high = attend(arrived[k], k == 0)
         from_left = lax.ppermute(high, "mem", rightward)
         from_right = lax.ppermute(low, "mem", leftward)
         parts.append((state, normed, from_left, from_right))
-    returned = []
-    for k, (first, last) in enumerate(spans_out):
-        lo = 0 if k == 0 else k - 1
-        spans = spans_in[lo : k + 1]
-        inner = conv_tile(first, last, spans, parts[lo : k + 1], None)
-        messages = conv_tile(first, last, spans, parts[lo : k + 1], inner)
+
+    def tile_chunk(k):
+        lo = max(k - 1, 0)
+        rest = (*spans_out[k], spans_in[lo : k + 1], parts[lo : k + 1])
+        if SPLIT_TILE and width > 2:
+            inner = conv_tile(*rest, tuple(range(1, width - 1)), False)
+            (messages,) = conv_tile(*rest, (0, width - 1), True, inner)
+        else:
+            (messages,) = conv_tile(*rest, tuple(range(width)), True)
         returned.append(exchange(messages))
+
+    for k in range(len(spans_in) + AHEAD):
+        if k < len(spans_in):
+            attend_chunk(k)
+        if k >= AHEAD:
+            tile_chunk(k - AHEAD)
     result = None
     for span, arrival in zip(spans_out, returned):
         result = place(*span, arrival, result)

time: 147 us -> 145 us (0.986)
  local copies, waits for them, and re-layouts: 6.78 us -> 2.39 us
  Pallas kernels: 49.4 us -> 53.1 us
  starting transfers between devices: 42.1 us -> 39.3 us
    unnamed x32 -> x16, local copies, waits for them, and re-layouts: 6.78 us -> 2.39 us
    pallas_call x10, Pallas kernels: 49.4 us -> 53.1 us  [call(): pl.pallas_call(kernel, out_shape=[(pltpu.VMEM if is_near else pltpu.HBM)(...]
    all_to_all x4, starting transfers between devices: 33.4 us -> 30.3 us  [exchange(): lax.all_to_all(messages, 'mem', split_axis=0, concat_axis=0, tiled=True)]
    all_to_all x4, waiting for transfers between devices: 44.4 us -> 46.4 us  [exchange(): lax.all_to_all(messages, 'mem', split_axis=0, concat_axis=0, tiled=True)]
  transfers between devices with their start and end apart: 8 -> 8, of which waited for: 5 -> 5; matrix products, arithmetic and copies ran while one was open for 0% -> 0% of each run, Pallas kernels for 26% -> 30%
where the time goes in v3:
time: 145 us; the launch traced here: 144 us
  Pallas kernels  53.1 us (37%)
  waiting for transfers between devices  49.1 us (34%)
  starting transfers between devices  39.3 us (27%)
  local copies, waits for them, and re-layouts  2.39 us (2%)
    pallas_call x10, Pallas kernels, call(): pl.pallas_call(kernel, out_shape=[(pltpu.VMEM if is_near else pltpu.HBM)(...  53.1 us
    all_to_all x4, waiting for transfers between devices, exchange(): lax.all_to_all(messages, 'mem', split_axis=0, concat_axis=0, tiled=True)  46.4 us
    all_to_all x4, starting transfers between devices, exchange(): lax.all_to_all(messages, 'mem', split_axis=0, concat_axis=0, tiled=True)  30.3 us
    ppermute x2, starting transfers between devices, attend_chunk(): from_left = lax.ppermute(high, 'mem', rightward)  4.88 us
    ppermute x2, starting transfers between devices, attend_chunk(): from_right = lax.ppermute(low, 'mem', leftward)  4.06 us
  transfers between devices with their start and end apart: 8, of which 5 were waited for; matrix products, arithmetic and copies ran while one was open for 0% of the time, Pallas kernels for 30%

profile of v3, /device:TPU:15, one launch (start us, length us, event | category | flops | bytes accessed | tf_op | source)
XLA Modules:
  0.0 144.3 jit_solution(6208414046543512864)
XLA Ops:
  0.0 7.9 %conv_slab.2 = bf16[16,7,16,256]{3,2,1,0:T(8,128)(2,1)} custom-call(bf16[4,16,64,256]{3,2,1,0:T(8,128)(2,1)} %field_hbm.3, f32[2,2,256]{2,1,0:T(2,128)} %gain_hbm.3, bf16[2,3,3,256,512]{4,3,2,1,0:T(8,128)(2,1)} %weight_hbm.3, bf16[256,256]{1,0:T(8,128)(2,1)} %constant.8.clone.order_hbm), custom_call_target="tpu_custom_call" | custom-call | flops 4227858432 | bytes 1835008 | tf_op jit(solution)/shard_map/conv_slab/pallas_call | solution.py:434
  7.9 6.6 %all-to-all-start = ((bf16[16,7,16,256]{3,2,1,0:T(8,128)(2,1)}), bf16[16,7,16,256]{3,2,1,0:T(8,128)(2,1)S(1)}, u32[]{:S(2)}, u32[]{:S(2)}) async-start(bf16[16,7,16,256]{3,2,1,0:T(8,128)(2,1)} %conv_slab.2), calls=%async_computation | async-start | bytes 1835008 | tf_op jit(solution)/shard_map/all_to_all | solution.py:509
  14.5 9.5 %conv_slab.3 = (bf16[16,9,16,256]{3,2,1,0:T(8,128)(2,1)}, f32[2,2,256]{2,1,0:T(2,128)S(1)}, bf16[3,3,256,512]{3,2,1,0:T(8,128)(2,1)S(1)}, bf16[2,6,256,256]{3,2,1,0:T(8,128)(2,1)S(1)}) custom-call(bf16[4,16,64,256]{3,2,1,0:T(8,128)(2,1)} %field_hbm.3, f32[2,2,256]{2,1,0:T(2,128)} %gain_hbm.3, bf16[2,3,3,256,512]{4,3,2,1,0:T(8,128)(2,1)} %weight_hbm.3, ...), custom_call_target="tpu_custom_call" | custom-call | flops 5435817984 | bytes 2359296 | tf_op jit(solution)/shard_map/conv_slab/pallas_call | solution.py:434
  24.0 0.0 copy-start
  24.0 1.4 copy-done
  25.4 11.1 %all-to-all-done.arrived = bf16[16,7,16,256]{3,2,1,0:T(8,128)(2,1)S(1)} async-done(((bf16[16,7,16,256]{3,2,1,0:T(8,128)(2,1)}), bf16[16,7,16,256]{3,2,1,0:T(8,128)(2,1)S(1)}, u32[]{:S(2)}, u32[]{:S(2)}) %all-to-all-start) | async-done | bytes 917536 | tf_op jit(solution)/shard_map/all_to_all | solution.py:509
  36.5 0.9 copy-done.7
  37.5 5.0 %all-to-all-start.2 = ((bf16[16,9,16,256]{3,2,1,0:T(8,128)(2,1)}), bf16[16,9,16,256]{3,2,1,0:T(8,128)(2,1)S(1)}, u32[]{:S(2)}, u32[]{:S(2)}) async-start(bf16[16,9,16,256]{3,2,1,0:T(8,128)(2,1)} %get-tuple-element.30), calls=%async_computation.2 | async-start | bytes 2359296 | tf_op jit(solution)/shard_map/all_to_all | solution.py:509
  42.4 5.4 %attend.2 = (bf16[7,256,256]{2,1,0:T(8,128)(2,1)S(1)}, bf16[7,256,256]{2,1,0:T(8,128)(2,1)S(1)}, bf16[7,64,256]{2,1,0:T(8,128)(2,1)S(1)}, bf16[7,64,256]{2,1,0:T(8,128)(2,1)S(1)}) custom-call(bf16[16,7,16,256]{3,2,1,0:T(8,128)(2,1)} %copy-done.7, f32[2,2,256]{2,1,0:T(2,128)S(1)} %get-tuple-element.21.gain.refs_2_.refs_6_.refs_4_.refs_10_, ...), custom_call_target="tpu_custom_call" | custom-call | flops 1409286144 | bytes 3670016 | tf_op jit(solution)/shard_map/attend/pallas_call | solution.py:434
  47.8 0.0 copy-start.3
  47.8 0.0 copy-start.5
  47.8 2.4 %collective-permute-start = (bf16[7,64,256]{2,1,0:T(8,128)(2,1)S(1)}, bf16[7,64,256]{2,1,0:T(8,128)(2,1)S(1)}, u32[]{:S(2)}, u32[]{:S(2)}) collective-permute-start(bf16[7,64,256]{2,1,0:T(8,128)(2,1)S(1)} %get-tuple-element.25), channel_id=1, source_target_pairs={{0,1},{1,2},{2,3},{3,6},{6,7},{7,4},{4,5},{5,8},{8,9},{9,10},{10,1... | collective-permute-start | bytes 688136 | tf_op jit(solution)/shard_map/ppermute | solution.py:577
  50.3 1.9 %collective-permute-start.1 = (bf16[7,64,256]{2,1,0:T(8,128)(2,1)S(1)}, bf16[7,64,256]{2,1,0:T(8,128)(2,1)S(1)}, u32[]{:S(2)}, u32[]{:S(2)}) collective-permute-start(bf16[7,64,256]{2,1,0:T(8,128)(2,1)S(1)} %get-tuple-element.26), channel_id=1, source_target_pairs={{1,0},{2,1},{3,2},{6,3},{7,6},{4,7},{5,4},{8,5},{9,8},{10,9},{11,1... | collective-permute-start | bytes 688136 | tf_op jit(solution)/shard_map/ppermute | solution.py:578
  52.2 0.0 copy-done.1
  52.2 4.6 %conv_inner.2 = (bf16[6,128,256]{2,1,0:T(8,128)(2,1)S(1)}, f32[6,128,512]{2,1,0:T(8,128)S(1)}) custom-call(bf16[7,256,256]{2,1,0:T(8,128)(2,1)S(1)} %get-tuple-element.23.refs_0_, bf16[7,256,256]{2,1,0:T(8,128)(2,1)S(1)} %get-tuple-element.24.refs_1_.refs_2_, f32[2,2,256]{2,1,0:T(2,128)S(1)} %get-tuple-element.21.gain.refs_2_.refs_6_.refs_4_.refs_10_, ...), custom_call_target="tpu_custom_call" | custom-call | flops 2415919104 | bytes 3145728 | tf_op jit(solution)/shard_map/conv_inner/pallas_call | solution.py:434
  56.8 0.0 collective-permute-done.refs_2_.refs_4_
  56.8 2.4 %collective-permute-done.1.refs_3_.refs_6_ = bf16[7,64,256]{2,1,0:T(8,128)(2,1)S(1)} collective-permute-done((bf16[7,64,256]{2,1,0:T(8,128)(2,1)S(1)}, bf16[7,64,256]{2,1,0:T(8,128)(2,1)S(1)}, u32[]{:S(2)}, u32[]{:S(2)}) %collective-permute-start.1) | collective-permute-done | bytes 229408 | tf_op jit(solution)/shard_map/ppermute | solution.py:578
  59.2 3.7 %conv_edges.2 = bf16[16,6,16,256]{3,2,1,0:T(8,128)(2,1)} custom-call(bf16[7,256,256]{2,1,0:T(8,128)(2,1)S(1)} %get-tuple-element.23.refs_0_, bf16[7,256,256]{2,1,0:T(8,128)(2,1)S(1)} %get-tuple-element.24.refs_1_.refs_2_, bf16[7,64,256]{2,1,0:T(8,128)(2,1)S(1)} %collective-permute-done.refs_2_.refs_4_, ...), custom_call_target="tpu_custom_call" | custom-call | flops 2415919104 | bytes 3145728 | tf_op jit(solution)/shard_map/conv_edges/pallas_call | solution.py:434
  62.9 7.2 %all-to-all-done.2.arrived = bf16[16,9,16,256]{3,2,1,0:T(8,128)(2,1)S(1)} async-done(((bf16[16,9,16,256]{3,2,1,0:T(8,128)(2,1)}), bf16[16,9,16,256]{3,2,1,0:T(8,128)(2,1)S(1)}, u32[]{:S(2)}, u32[]{:S(2)}) %all-to-all-start.2) | async-done | bytes 1179680 | tf_op jit(solution)/shard_map/all_to_all | solution.py:509
  70.2 9.8 %all-to-all-start.1 = ((bf16[16,6,16,256]{3,2,1,0:T(8,128)(2,1)}), bf16[16,6,16,256]{3,2,1,0:T(8,128)(2,1)}, u32[]{:S(2)}, u32[]{:S(2)}) async-start(bf16[16,6,16,256]{3,2,1,0:T(8,128)(2,1)} %conv_edges.2), calls=%async_computation.1 | async-start | bytes 1572864 | tf_op jit(solution)/shard_map/all_to_all | solution.py:509
  80.0 4.7 %attend.3 = (bf16[9,256,256]{2,1,0:T(8,128)(2,1)S(1)}, bf16[9,256,256]{2,1,0:T(8,128)(2,1)S(1)}, bf16[9,64,256]{2,1,0:T(8,128)(2,1)S(1)}, bf16[9,64,256]{2,1,0:T(8,128)(2,1)S(1)}) custom-call(bf16[16,9,16,256]{3,2,1,0:T(8,128)(2,1)S(1)} %all-to-all-done.2.arrived, f32[2,2,256]{2,1,0:T(2,128)S(1)} %get-tuple-element.21.gain.refs_2_.refs_6_.refs_4_.refs_10_, ...), custom_call_target="tpu_custom_call" | custom-call | flops 1811939328 | bytes 4718592 | tf_op jit(solution)/shard_map/attend/pallas_call | solution.py:434
  84.7 2.4 %collective-permute-start.2 = (bf16[9,64,256]{2,1,0:T(8,128)(2,1)S(1)}, bf16[9,64,256]{2,1,0:T(8,128)(2,1)S(1)}, u32[]{:S(2)}, u32[]{:S(2)}) collective-permute-start(bf16[9,64,256]{2,1,0:T(8,128)(2,1)S(1)} %get-tuple-element.33), channel_id=1, source_target_pairs={{0,1},{1,2},{2,3},{3,6},{6,7},{7,4},{4,5},{5,8},{8,9},{9,10},{10,1... | collective-permute-start | bytes 884744 | tf_op jit(solution)/shard_map/ppermute | solution.py:577
  87.2 2.1 %collective-permute-start.3 = (bf16[9,64,256]{2,1,0:T(8,128)(2,1)S(1)}, bf16[9,64,256]{2,1,0:T(8,128)(2,1)S(1)}, u32[]{:S(2)}, u32[]{:S(2)}) collective-permute-start(bf16[9,64,256]{2,1,0:T(8,128)(2,1)S(1)} %get-tuple-element.34), channel_id=1, source_target_pairs={{1,0},{2,1},{3,2},{6,3},{7,6},{4,7},{5,4},{8,5},{9,8},{10,9},{11,1... | collective-permute-start | bytes 884744 | tf_op jit(solution)/shard_map/ppermute | solution.py:578
  89.3 7.6 %conv_inner.3 = (bf16[10,128,256]{2,1,0:T(8,128)(2,1)S(1)}, f32[10,128,512]{2,1,0:T(8,128)S(1)}) custom-call(bf16[7,256,256]{2,1,0:T(8,128)(2,1)S(1)} %copy-done.4, bf16[9,256,256]{2,1,0:T(8,128)(2,1)S(1)} %get-tuple-element.31.refs_1_, bf16[7,256,256]{2,1,0:T(8,128)(2,1)S(1)} %copy-done.6, bf16[9,256,256]{2,1,0:T(8,128)(2,1)S(1)} %get-tuple-element.32.refs_3_, ...), custom_call_target="tpu_custom_call" | custom-call | flops 4026531840 | bytes 5242880 | tf_op jit(solution)/shard_map/conv_inner/pallas_call | solution.py:434
  97.0 0.0 collective-permute-done.2.refs_5_
  97.0 0.4 collective-permute-done.3.refs_7_
  97.4 5.5 %conv_edges.3 = bf16[16,10,16,256]{3,2,1,0:T(8,128)(2,1)} custom-call(bf16[7,256,256]{2,1,0:T(8,128)(2,1)S(1)} %copy-done.4, bf16[9,256,256]{2,1,0:T(8,128)(2,1)S(1)} %get-tuple-element.31.refs_1_, bf16[7,256,256]{2,1,0:T(8,128)(2,1)S(1)} %copy-done.6, bf16[9,256,256]{2,1,0:T(8,128)(2,1)S(1)} %get-tuple-element.32.refs_3_, ...), custom_call_target="tpu_custom_call" | custom-call | flops 4026531840 | bytes 5242880 | tf_op jit(solution)/shard_map/conv_edges/pallas_call | solution.py:434
  102.9 0.0 all-to-all-done.1.refs_0_
  102.9 9.0 %all-to-all-start.3 = ((bf16[16,10,16,256]{3,2,1,0:T(8,128)(2,1)}), bf16[16,10,16,256]{3,2,1,0:T(8,128)(2,1)S(1)}, u32[]{:S(2)}, u32[]{:S(2)}) async-start(bf16[16,10,16,256]{3,2,1,0:T(8,128)(2,1)} %conv_edges.3), calls=%async_computation.3 | async-start | bytes 2621440 | tf_op jit(solution)/shard_map/all_to_all | solution.py:509
  112.0 2.5 %place.2.refs_0_ = bf16[4,16,64,256]{3,2,1,0:T(8,128)(2,1)} custom-call(bf16[16,6,16,256]{3,2,1,0:T(8,128)(2,1)} %all-to-all-done.1.refs_0_, bf16[2,6,256,256]{3,2,1,0:T(8,128)(2,1)S(1)} %get-tuple-element.22.stacks.refs_3_.refs_7_.refs_1_.refs_5_.refs_11_.refs_2_), custom_call_target="tpu_custom_call" | custom-call | flops 201326592 | bytes 1572864 | tf_op jit(solution)/shard_map/place/pallas_call | solution.py:434
  114.5 28.0 %all-to-all-done.3.refs_1_ = bf16[16,10,16,256]{3,2,1,0:T(8,128)(2,1)S(1)} async-done(((bf16[16,10,16,256]{3,2,1,0:T(8,128)(2,1)}), bf16[16,10,16,256]{3,2,1,0:T(8,128)(2,1)S(1)}, u32[]{:S(2)}, u32[]{:S(2)}) %all-to-all-start.3) | async-done | bytes 1310752 | tf_op jit(solution)/shard_map/all_to_all | solution.py:509
  142.5 1.6 %place.3 = bf16[4,16,64,256]{3,2,1,0:T(8,128)(2,1)} custom-call(bf16[4,16,64,256]{3,2,1,0:T(8,128)(2,1)} %place.2.refs_0_, bf16[16,10,16,256]{3,2,1,0:T(8,128)(2,1)S(1)} %all-to-all-done.3.refs_1_, bf16[2,6,256,256]{3,2,1,0:T(8,128)(2,1)S(1)} %get-tuple-element.22.stacks.refs_3_.refs_7_.refs_1_.refs_5_.refs_11_.refs_2_), custom_call_target="tpu_custom_call", output_to_operand_aliasing={{}: (0, {})} | custom-call | flops 335544320 | bytes 2621440 | tf_op jit(solution)/shard_map/place/pallas_call | solution.py:434
  (10 shorter events, 0.0 us)
Async XLA Ops:
  7.9 28.6 %all-to-all-start = ((bf16[16,7,16,256]{3,2,1,0:T(8,128)(2,1)}), bf16[16,7,16,256]{3,2,1,0:T(8,128)(2,1)S(1)}, u32[]{:S(2)}, u32[]{:S(2)}) async-start(bf16[16,7,16,256]{3,2,1,0:T(8,128)(2,1)} %conv_slab.2), calls=%async_computation | async-start | bytes 1835008 | tf_op jit(solution)/shard_map/all_to_all | solution.py:509
  24.0 1.4 copy-start
  36.5 0.9 copy-start.7
  37.5 32.7 %all-to-all-start.2 = ((bf16[16,9,16,256]{3,2,1,0:T(8,128)(2,1)}), bf16[16,9,16,256]{3,2,1,0:T(8,128)(2,1)S(1)}, u32[]{:S(2)}, u32[]{:S(2)}) async-start(bf16[16,9,16,256]{3,2,1,0:T(8,128)(2,1)} %get-tuple-element.30), calls=%async_computation.2 | async-start | bytes 2359296 | tf_op jit(solution)/shard_map/all_to_all | solution.py:509
  42.4 9.8 %copy-start.1 = (bf16[3,3,256,512]{3,2,1,0:T(8,128)(2,1)S(1)}, bf16[3,3,256,512]{3,2,1,0:T(8,128)(2,1)}, u32[]{:S(2)}) copy-start(bf16[3,3,256,512]{3,2,1,0:T(8,128)(2,1)} %copy-done) | copy-start | bytes 7077892
  47.8 11.4 %copy-start.3 = (bf16[7,256,256]{2,1,0:T(8,128)(2,1)}, bf16[7,256,256]{2,1,0:T(8,128)(2,1)S(1)}, u32[]{:S(2)}) copy-start(bf16[7,256,256]{2,1,0:T(8,128)(2,1)S(1)} %get-tuple-element.23.refs_0_) | copy-start | bytes 2752516
  47.8 11.4 %copy-start.5 = (bf16[7,256,256]{2,1,0:T(8,128)(2,1)}, bf16[7,256,256]{2,1,0:T(8,128)(2,1)S(1)}, u32[]{:S(2)}) copy-start(bf16[7,256,256]{2,1,0:T(8,128)(2,1)S(1)} %get-tuple-element.24.refs_1_.refs_2_) | copy-start | bytes 2752516
  47.8 9.0 %collective-permute-start = (bf16[7,64,256]{2,1,0:T(8,128)(2,1)S(1)}, bf16[7,64,256]{2,1,0:T(8,128)(2,1)S(1)}, u32[]{:S(2)}, u32[]{:S(2)}) collective-permute-start(bf16[7,64,256]{2,1,0:T(8,128)(2,1)S(1)} %get-tuple-element.25), channel_id=1, source_target_pairs={{0,1},{1,2},{2,3},{3,6},{6,7},{7,4},{4,5},{5,8},{8,9},{9,10},{10,1... | collective-permute-start | bytes 688136 | tf_op jit(solution)/shard_map/ppermute | solution.py:577
  50.3 8.9 %collective-permute-start.1 = (bf16[7,64,256]{2,1,0:T(8,128)(2,1)S(1)}, bf16[7,64,256]{2,1,0:T(8,128)(2,1)S(1)}, u32[]{:S(2)}, u32[]{:S(2)}) collective-permute-start(bf16[7,64,256]{2,1,0:T(8,128)(2,1)S(1)} %get-tuple-element.26), channel_id=1, source_target_pairs={{1,0},{2,1},{3,2},{6,3},{7,6},{4,7},{5,4},{8,5},{9,8},{10,9},{11,1... | collective-permute-start | bytes 688136 | tf_op jit(solution)/shard_map/ppermute | solution.py:578
  70.2 32.8 %all-to-all-start.1 = ((bf16[16,6,16,256]{3,2,1,0:T(8,128)(2,1)}), bf16[16,6,16,256]{3,2,1,0:T(8,128)(2,1)}, u32[]{:S(2)}, u32[]{:S(2)}) async-start(bf16[16,6,16,256]{3,2,1,0:T(8,128)(2,1)} %conv_edges.2), calls=%async_computation.1 | async-start | bytes 1572864 | tf_op jit(solution)/shard_map/all_to_all | solution.py:509
  80.0 9.3 %copy-start.2 = (bf16[3,3,256,512]{3,2,1,0:T(8,128)(2,1)S(1)}, bf16[3,3,256,512]{3,2,1,0:T(8,128)(2,1)}, u32[]{:S(2)}) copy-start(bf16[3,3,256,512]{3,2,1,0:T(8,128)(2,1)} %copy-done) | copy-start | bytes 7077892
  80.0 9.4 %copy-start.4 = (bf16[7,256,256]{2,1,0:T(8,128)(2,1)S(1)}, bf16[7,256,256]{2,1,0:T(8,128)(2,1)}, u32[]{:S(2)}) copy-start(bf16[7,256,256]{2,1,0:T(8,128)(2,1)} %copy-done.3) | copy-start | bytes 2752516
  80.0 9.4 %copy-start.6 = (bf16[7,256,256]{2,1,0:T(8,128)(2,1)S(1)}, bf16[7,256,256]{2,1,0:T(8,128)(2,1)}, u32[]{:S(2)}) copy-start(bf16[7,256,256]{2,1,0:T(8,128)(2,1)} %copy-done.5) | copy-start | bytes 2752516
  84.7 12.3 %collective-permute-start.2 = (bf16[9,64,256]{2,1,0:T(8,128)(2,1)S(1)}, bf16[9,64,256]{2,1,0:T(8,128)(2,1)S(1)}, u32[]{:S(2)}, u32[]{:S(2)}) collective-permute-start(bf16[9,64,256]{2,1,0:T(8,128)(2,1)S(1)} %get-tuple-element.33), channel_id=1, source_target_pairs={{0,1},{1,2},{2,3},{3,6},{6,7},{7,4},{4,5},{5,8},{8,9},{9,10},{10,1... | collective-permute-start | bytes 884744 | tf_op jit(solution)/shard_map/ppermute | solution.py:577
  87.2 10.2 %collective-permute-start.3 = (bf16[9,64,256]{2,1,0:T(8,128)(2,1)S(1)}, bf16[9,64,256]{2,1,0:T(8,128)(2,1)S(1)}, u32[]{:S(2)}, u32[]{:S(2)}) collective-permute-start(bf16[9,64,256]{2,1,0:T(8,128)(2,1)S(1)} %get-tuple-element.34), channel_id=1, source_target_pairs={{1,0},{2,1},{3,2},{6,3},{7,6},{4,7},{5,4},{8,5},{9,8},{10,9},{11,1... | collective-permute-start | bytes 884744 | tf_op jit(solution)/shard_map/ppermute | solution.py:578
  102.9 39.6 %all-to-all-start.3 = ((bf16[16,10,16,256]{3,2,1,0:T(8,128)(2,1)}), bf16[16,10,16,256]{3,2,1,0:T(8,128)(2,1)S(1)}, u32[]{:S(2)}, u32[]{:S(2)}) async-start(bf16[16,10,16,256]{3,2,1,0:T(8,128)(2,1)} %conv_edges.3), calls=%async_computation.3 | async-start | bytes 2621440 | tf_op jit(solution)/shard_map/all_to_all | solution.py:509

commit v4 on v3

--- a/solution.py
+++ b/solution.py
@@ -13,7 +13,7 @@
 LANES = 128
 epsilon = 1e-06
 VMEM_LIMIT = 40 * 1024 * 1024
-UNROLL = 4
+UNROLL = 5
 CUTS = (7,)
 AHEAD = 0
 SPLIT_TILE = True

time: 145 us -> 144 us (level)
  no operation moved by 1% of the time
where the time goes in v4:
time: 144 us
  Pallas kernels  52.2 us (36%)
  waiting for transfers between devices  49.3 us (34%)
  starting transfers between devices  39.6 us (28%)
  local copies, waits for them, and re-layouts  2.39 us (2%)
    pallas_call x10, Pallas kernels, call(): pl.pallas_call(kernel, out_shape=[(pltpu.VMEM if is_near else pltpu.HBM)(...  52.2 us
    all_to_all x4, waiting for transfers between devices, exchange(): lax.all_to_all(messages, 'mem', split_axis=0, concat_axis=0, tiled=True)  46.4 us
    all_to_all x4, starting transfers between devices, exchange(): lax.all_to_all(messages, 'mem', split_axis=0, concat_axis=0, tiled=True)  30.6 us
    ppermute x2, starting transfers between devices, attend_chunk(): from_left = lax.ppermute(high, 'mem', rightward)  4.88 us
    ppermute x2, starting transfers between devices, attend_chunk(): from_right = lax.ppermute(low, 'mem', leftward)  4.06 us
    ppermute x2, waiting for transfers between devices, attend_chunk(): from_right = lax.ppermute(low, 'mem', leftward)  2.94 us
  transfers between devices with their start and end apart: 8, of which 5 were waited for; matrix products, arithmetic and copies ran while one was open for 0% of the time, Pallas kernels for 30%

profile of v4, /device:TPU:15, one launch (start us, length us, event | category | flops | bytes accessed | tf_op | source)
XLA Modules:
  0.0 143.8 jit_solution(17526418674335136965)
XLA Ops:
  0.0 7.9 %conv_slab.2 = bf16[16,7,16,256]{3,2,1,0:T(8,128)(2,1)} custom-call(bf16[4,16,64,256]{3,2,1,0:T(8,128)(2,1)} %field_hbm.3, f32[2,2,256]{2,1,0:T(2,128)} %gain_hbm.3, bf16[2,3,3,256,512]{4,3,2,1,0:T(8,128)(2,1)} %weight_hbm.3, bf16[256,256]{1,0:T(8,128)(2,1)} %constant.8.clone.order_hbm), custom_call_target="tpu_custom_call" | custom-call | flops 4227858432 | bytes 1835008 | tf_op jit(solution)/shard_map/conv_slab/pallas_call | solution.py:434
  7.9 6.6 %all-to-all-start = ((bf16[16,7,16,256]{3,2,1,0:T(8,128)(2,1)}), bf16[16,7,16,256]{3,2,1,0:T(8,128)(2,1)S(1)}, u32[]{:S(2)}, u32[]{:S(2)}) async-start(bf16[16,7,16,256]{3,2,1,0:T(8,128)(2,1)} %conv_slab.2), calls=%async_computation | async-start | bytes 1835008 | tf_op jit(solution)/shard_map/all_to_all | solution.py:509
  14.5 9.5 %conv_slab.3 = (bf16[16,9,16,256]{3,2,1,0:T(8,128)(2,1)}, f32[2,2,256]{2,1,0:T(2,128)S(1)}, bf16[3,3,256,512]{3,2,1,0:T(8,128)(2,1)S(1)}, bf16[2,6,256,256]{3,2,1,0:T(8,128)(2,1)S(1)}) custom-call(bf16[4,16,64,256]{3,2,1,0:T(8,128)(2,1)} %field_hbm.3, f32[2,2,256]{2,1,0:T(2,128)} %gain_hbm.3, bf16[2,3,3,256,512]{4,3,2,1,0:T(8,128)(2,1)} %weight_hbm.3, ...), custom_call_target="tpu_custom_call" | custom-call | flops 5435817984 | bytes 2359296 | tf_op jit(solution)/shard_map/conv_slab/pallas_call | solution.py:434
  24.0 0.0 copy-start
  24.0 1.4 copy-done
  25.4 11.1 %all-to-all-done.arrived = bf16[16,7,16,256]{3,2,1,0:T(8,128)(2,1)S(1)} async-done(((bf16[16,7,16,256]{3,2,1,0:T(8,128)(2,1)}), bf16[16,7,16,256]{3,2,1,0:T(8,128)(2,1)S(1)}, u32[]{:S(2)}, u32[]{:S(2)}) %all-to-all-start) | async-done | bytes 917536 | tf_op jit(solution)/shard_map/all_to_all | solution.py:509
  36.5 0.9 copy-done.7
  37.5 5.0 %all-to-all-start.2 = ((bf16[16,9,16,256]{3,2,1,0:T(8,128)(2,1)}), bf16[16,9,16,256]{3,2,1,0:T(8,128)(2,1)S(1)}, u32[]{:S(2)}, u32[]{:S(2)}) async-start(bf16[16,9,16,256]{3,2,1,0:T(8,128)(2,1)} %get-tuple-element.30), calls=%async_computation.2 | async-start | bytes 2359296 | tf_op jit(solution)/shard_map/all_to_all | solution.py:509
  42.4 5.4 %attend.2 = (bf16[7,256,256]{2,1,0:T(8,128)(2,1)S(1)}, bf16[7,256,256]{2,1,0:T(8,128)(2,1)S(1)}, bf16[7,64,256]{2,1,0:T(8,128)(2,1)S(1)}, bf16[7,64,256]{2,1,0:T(8,128)(2,1)S(1)}) custom-call(bf16[16,7,16,256]{3,2,1,0:T(8,128)(2,1)} %copy-done.7, f32[2,2,256]{2,1,0:T(2,128)S(1)} %get-tuple-element.21.gain.refs_2_.refs_6_.refs_4_.refs_10_, ...), custom_call_target="tpu_custom_call" | custom-call | flops 1409286144 | bytes 3670016 | tf_op jit(solution)/shard_map/attend/pallas_call | solution.py:434
  47.8 0.0 copy-start.3
  47.8 0.0 copy-start.5
  47.8 2.4 %collective-permute-start = (bf16[7,64,256]{2,1,0:T(8,128)(2,1)S(1)}, bf16[7,64,256]{2,1,0:T(8,128)(2,1)S(1)}, u32[]{:S(2)}, u32[]{:S(2)}) collective-permute-start(bf16[7,64,256]{2,1,0:T(8,128)(2,1)S(1)} %get-tuple-element.25), channel_id=1, source_target_pairs={{0,1},{1,2},{2,3},{3,6},{6,7},{7,4},{4,5},{5,8},{8,9},{9,10},{10,1... | collective-permute-start | bytes 688136 | tf_op jit(solution)/shard_map/ppermute | solution.py:577
  50.3 1.9 %collective-permute-start.1 = (bf16[7,64,256]{2,1,0:T(8,128)(2,1)S(1)}, bf16[7,64,256]{2,1,0:T(8,128)(2,1)S(1)}, u32[]{:S(2)}, u32[]{:S(2)}) collective-permute-start(bf16[7,64,256]{2,1,0:T(8,128)(2,1)S(1)} %get-tuple-element.26), channel_id=1, source_target_pairs={{1,0},{2,1},{3,2},{6,3},{7,6},{4,7},{5,4},{8,5},{9,8},{10,9},{11,1... | collective-permute-start | bytes 688136 | tf_op jit(solution)/shard_map/ppermute | solution.py:578
  52.2 4.6 %conv_inner.2 = (bf16[6,128,256]{2,1,0:T(8,128)(2,1)S(1)}, f32[6,128,512]{2,1,0:T(8,128)S(1)}) custom-call(bf16[7,256,256]{2,1,0:T(8,128)(2,1)S(1)} %get-tuple-element.23.refs_0_, bf16[7,256,256]{2,1,0:T(8,128)(2,1)S(1)} %get-tuple-element.24.refs_1_.refs_2_, f32[2,2,256]{2,1,0:T(2,128)S(1)} %get-tuple-element.21.gain.refs_2_.refs_6_.refs_4_.refs_10_, ...), custom_call_target="tpu_custom_call" | custom-call | flops 2415919104 | bytes 3145728 | tf_op jit(solution)/shard_map/conv_inner/pallas_call | solution.py:434
  56.8 0.0 collective-permute-done.refs_2_.refs_4_
  56.8 2.4 %collective-permute-done.1.refs_3_.refs_6_ = bf16[7,64,256]{2,1,0:T(8,128)(2,1)S(1)} collective-permute-done((bf16[7,64,256]{2,1,0:T(8,128)(2,1)S(1)}, bf16[7,64,256]{2,1,0:T(8,128)(2,1)S(1)}, u32[]{:S(2)}, u32[]{:S(2)}) %collective-permute-start.1) | collective-permute-done | bytes 229408 | tf_op jit(solution)/shard_map/ppermute | solution.py:578
  59.2 0.0 copy-done.5
  59.2 3.7 %conv_edges.2 = bf16[16,6,16,256]{3,2,1,0:T(8,128)(2,1)} custom-call(bf16[7,256,256]{2,1,0:T(8,128)(2,1)S(1)} %get-tuple-element.23.refs_0_, bf16[7,256,256]{2,1,0:T(8,128)(2,1)S(1)} %get-tuple-element.24.refs_1_.refs_2_, bf16[7,64,256]{2,1,0:T(8,128)(2,1)S(1)} %collective-permute-done.refs_2_.refs_4_, ...), custom_call_target="tpu_custom_call" | custom-call | flops 2415919104 | bytes 3145728 | tf_op jit(solution)/shard_map/conv_edges/pallas_call | solution.py:434
  62.9 7.2 %all-to-all-done.2.arrived = bf16[16,9,16,256]{3,2,1,0:T(8,128)(2,1)S(1)} async-done(((bf16[16,9,16,256]{3,2,1,0:T(8,128)(2,1)}), bf16[16,9,16,256]{3,2,1,0:T(8,128)(2,1)S(1)}, u32[]{:S(2)}, u32[]{:S(2)}) %all-to-all-start.2) | async-done | bytes 1179680 | tf_op jit(solution)/shard_map/all_to_all | solution.py:509
  70.2 9.8 %all-to-all-start.1 = ((bf16[16,6,16,256]{3,2,1,0:T(8,128)(2,1)}), bf16[16,6,16,256]{3,2,1,0:T(8,128)(2,1)}, u32[]{:S(2)}, u32[]{:S(2)}) async-start(bf16[16,6,16,256]{3,2,1,0:T(8,128)(2,1)} %conv_edges.2), calls=%async_computation.1 | async-start | bytes 1572864 | tf_op jit(solution)/shard_map/all_to_all | solution.py:509
  80.0 4.4 %attend.3 = (bf16[9,256,256]{2,1,0:T(8,128)(2,1)S(1)}, bf16[9,256,256]{2,1,0:T(8,128)(2,1)S(1)}, bf16[9,64,256]{2,1,0:T(8,128)(2,1)S(1)}, bf16[9,64,256]{2,1,0:T(8,128)(2,1)S(1)}) custom-call(bf16[16,9,16,256]{3,2,1,0:T(8,128)(2,1)S(1)} %all-to-all-done.2.arrived, f32[2,2,256]{2,1,0:T(2,128)S(1)} %get-tuple-element.21.gain.refs_2_.refs_6_.refs_4_.refs_10_, ...), custom_call_target="tpu_custom_call" | custom-call | flops 1811939328 | bytes 4718592 | tf_op jit(solution)/shard_map/attend/pallas_call | solution.py:434
  84.4 2.4 %collective-permute-start.2 = (bf16[9,64,256]{2,1,0:T(8,128)(2,1)S(1)}, bf16[9,64,256]{2,1,0:T(8,128)(2,1)S(1)}, u32[]{:S(2)}, u32[]{:S(2)}) collective-permute-start(bf16[9,64,256]{2,1,0:T(8,128)(2,1)S(1)} %get-tuple-element.33), channel_id=1, source_target_pairs={{0,1},{1,2},{2,3},{3,6},{6,7},{7,4},{4,5},{5,8},{8,9},{9,10},{10,1... | collective-permute-start | bytes 884744 | tf_op jit(solution)/shard_map/ppermute | solution.py:577
  86.8 2.1 %collective-permute-start.3 = (bf16[9,64,256]{2,1,0:T(8,128)(2,1)S(1)}, bf16[9,64,256]{2,1,0:T(8,128)(2,1)S(1)}, u32[]{:S(2)}, u32[]{:S(2)}) collective-permute-start(bf16[9,64,256]{2,1,0:T(8,128)(2,1)S(1)} %get-tuple-element.34), channel_id=1, source_target_pairs={{1,0},{2,1},{3,2},{6,3},{7,6},{4,7},{5,4},{8,5},{9,8},{10,9},{11,1... | collective-permute-start | bytes 884744 | tf_op jit(solution)/shard_map/ppermute | solution.py:578
  89.0 7.4 %conv_inner.3 = (bf16[10,128,256]{2,1,0:T(8,128)(2,1)S(1)}, f32[10,128,512]{2,1,0:T(8,128)S(1)}) custom-call(bf16[7,256,256]{2,1,0:T(8,128)(2,1)S(1)} %copy-done.4, bf16[9,256,256]{2,1,0:T(8,128)(2,1)S(1)} %get-tuple-element.31.refs_1_, bf16[7,256,256]{2,1,0:T(8,128)(2,1)S(1)} %copy-done.6, bf16[9,256,256]{2,1,0:T(8,128)(2,1)S(1)} %get-tuple-element.32.refs_3_, ...), custom_call_target="tpu_custom_call" | custom-call | flops 4026531840 | bytes 5242880 | tf_op jit(solution)/shard_map/conv_inner/pallas_call | solution.py:434
  96.5 0.0 collective-permute-done.2.refs_5_
  96.5 0.6 collective-permute-done.3.refs_7_
  97.1 5.1 %conv_edges.3 = bf16[16,10,16,256]{3,2,1,0:T(8,128)(2,1)} custom-call(bf16[7,256,256]{2,1,0:T(8,128)(2,1)S(1)} %copy-done.4, bf16[9,256,256]{2,1,0:T(8,128)(2,1)S(1)} %get-tuple-element.31.refs_1_, bf16[7,256,256]{2,1,0:T(8,128)(2,1)S(1)} %copy-done.6, bf16[9,256,256]{2,1,0:T(8,128)(2,1)S(1)} %get-tuple-element.32.refs_3_, ...), custom_call_target="tpu_custom_call" | custom-call | flops 4026531840 | bytes 5242880 | tf_op jit(solution)/shard_map/conv_edges/pallas_call | solution.py:434
  102.2 0.0 all-to-all-done.1.refs_0_
  102.2 9.3 %all-to-all-start.3 = ((bf16[16,10,16,256]{3,2,1,0:T(8,128)(2,1)}), bf16[16,10,16,256]{3,2,1,0:T(8,128)(2,1)S(1)}, u32[]{:S(2)}, u32[]{:S(2)}) async-start(bf16[16,10,16,256]{3,2,1,0:T(8,128)(2,1)} %conv_edges.3), calls=%async_computation.3 | async-start | bytes 2621440 | tf_op jit(solution)/shard_map/all_to_all | solution.py:509
  111.5 2.5 %place.2.refs_0_ = bf16[4,16,64,256]{3,2,1,0:T(8,128)(2,1)} custom-call(bf16[16,6,16,256]{3,2,1,0:T(8,128)(2,1)} %all-to-all-done.1.refs_0_, bf16[2,6,256,256]{3,2,1,0:T(8,128)(2,1)S(1)} %get-tuple-element.22.stacks.refs_3_.refs_7_.refs_1_.refs_5_.refs_11_.refs_2_), custom_call_target="tpu_custom_call" | custom-call | flops 201326592 | bytes 1572864 | tf_op jit(solution)/shard_map/place/pallas_call | solution.py:434
  114.1 28.0 %all-to-all-done.3.refs_1_ = bf16[16,10,16,256]{3,2,1,0:T(8,128)(2,1)S(1)} async-done(((bf16[16,10,16,256]{3,2,1,0:T(8,128)(2,1)}), bf16[16,10,16,256]{3,2,1,0:T(8,128)(2,1)S(1)}, u32[]{:S(2)}, u32[]{:S(2)}) %all-to-all-start.3) | async-done | bytes 1310752 | tf_op jit(solution)/shard_map/all_to_all | solution.py:509
  142.1 1.6 %place.3 = bf16[4,16,64,256]{3,2,1,0:T(8,128)(2,1)} custom-call(bf16[4,16,64,256]{3,2,1,0:T(8,128)(2,1)} %place.2.refs_0_, bf16[16,10,16,256]{3,2,1,0:T(8,128)(2,1)S(1)} %all-to-all-done.3.refs_1_, bf16[2,6,256,256]{3,2,1,0:T(8,128)(2,1)S(1)} %get-tuple-element.22.stacks.refs_3_.refs_7_.refs_1_.refs_5_.refs_11_.refs_2_), custom_call_target="tpu_custom_call", output_to_operand_aliasing={{}: (0, {})} | custom-call | flops 335544320 | bytes 2621440 | tf_op jit(solution)/shard_map/place/pallas_call | solution.py:434
  (10 shorter events, 0.0 us)
Async XLA Ops:
  7.9 28.6 %all-to-all-start = ((bf16[16,7,16,256]{3,2,1,0:T(8,128)(2,1)}), bf16[16,7,16,256]{3,2,1,0:T(8,128)(2,1)S(1)}, u32[]{:S(2)}, u32[]{:S(2)}) async-start(bf16[16,7,16,256]{3,2,1,0:T(8,128)(2,1)} %conv_slab.2), calls=%async_computation | async-start | bytes 1835008 | tf_op jit(solution)/shard_map/all_to_all | solution.py:509
  24.0 1.4 copy-start
  36.5 0.9 copy-start.7
  37.5 32.7 %all-to-all-start.2 = ((bf16[16,9,16,256]{3,2,1,0:T(8,128)(2,1)}), bf16[16,9,16,256]{3,2,1,0:T(8,128)(2,1)S(1)}, u32[]{:S(2)}, u32[]{:S(2)}) async-start(bf16[16,9,16,256]{3,2,1,0:T(8,128)(2,1)} %get-tuple-element.30), calls=%async_computation.2 | async-start | bytes 2359296 | tf_op jit(solution)/shard_map/all_to_all | solution.py:509
  42.4 9.8 %copy-start.1 = (bf16[3,3,256,512]{3,2,1,0:T(8,128)(2,1)S(1)}, bf16[3,3,256,512]{3,2,1,0:T(8,128)(2,1)}, u32[]{:S(2)}) copy-start(bf16[3,3,256,512]{3,2,1,0:T(8,128)(2,1)} %copy-done) | copy-start | bytes 7077892
  47.8 11.4 %copy-start.3 = (bf16[7,256,256]{2,1,0:T(8,128)(2,1)}, bf16[7,256,256]{2,1,0:T(8,128)(2,1)S(1)}, u32[]{:S(2)}) copy-start(bf16[7,256,256]{2,1,0:T(8,128)(2,1)S(1)} %get-tuple-element.23.refs_0_) | copy-start | bytes 2752516
  47.8 11.4 %copy-start.5 = (bf16[7,256,256]{2,1,0:T(8,128)(2,1)}, bf16[7,256,256]{2,1,0:T(8,128)(2,1)S(1)}, u32[]{:S(2)}) copy-start(bf16[7,256,256]{2,1,0:T(8,128)(2,1)S(1)} %get-tuple-element.24.refs_1_.refs_2_) | copy-start | bytes 2752516
  47.8 9.0 %collective-permute-start = (bf16[7,64,256]{2,1,0:T(8,128)(2,1)S(1)}, bf16[7,64,256]{2,1,0:T(8,128)(2,1)S(1)}, u32[]{:S(2)}, u32[]{:S(2)}) collective-permute-start(bf16[7,64,256]{2,1,0:T(8,128)(2,1)S(1)} %get-tuple-element.25), channel_id=1, source_target_pairs={{0,1},{1,2},{2,3},{3,6},{6,7},{7,4},{4,5},{5,8},{8,9},{9,10},{10,1... | collective-permute-start | bytes 688136 | tf_op jit(solution)/shard_map/ppermute | solution.py:577
  50.3 8.9 %collective-permute-start.1 = (bf16[7,64,256]{2,1,0:T(8,128)(2,1)S(1)}, bf16[7,64,256]{2,1,0:T(8,128)(2,1)S(1)}, u32[]{:S(2)}, u32[]{:S(2)}) collective-permute-start(bf16[7,64,256]{2,1,0:T(8,128)(2,1)S(1)} %get-tuple-element.26), channel_id=1, source_target_pairs={{1,0},{2,1},{3,2},{6,3},{7,6},{4,7},{5,4},{8,5},{9,8},{10,9},{11,1... | collective-permute-start | bytes 688136 | tf_op jit(solution)/shard_map/ppermute | solution.py:578
  70.2 32.0 %all-to-all-start.1 = ((bf16[16,6,16,256]{3,2,1,0:T(8,128)(2,1)}), bf16[16,6,16,256]{3,2,1,0:T(8,128)(2,1)}, u32[]{:S(2)}, u32[]{:S(2)}) async-start(bf16[16,6,16,256]{3,2,1,0:T(8,128)(2,1)} %conv_edges.2), calls=%async_computation.1 | async-start | bytes 1572864 | tf_op jit(solution)/shard_map/all_to_all | solution.py:509
  80.0 9.0 %copy-start.2 = (bf16[3,3,256,512]{3,2,1,0:T(8,128)(2,1)S(1)}, bf16[3,3,256,512]{3,2,1,0:T(8,128)(2,1)}, u32[]{:S(2)}) copy-start(bf16[3,3,256,512]{3,2,1,0:T(8,128)(2,1)} %copy-done) | copy-start | bytes 7077892
  80.0 9.0 %copy-start.4 = (bf16[7,256,256]{2,1,0:T(8,128)(2,1)S(1)}, bf16[7,256,256]{2,1,0:T(8,128)(2,1)}, u32[]{:S(2)}) copy-start(bf16[7,256,256]{2,1,0:T(8,128)(2,1)} %copy-done.3) | copy-start | bytes 2752516
  80.0 9.0 %copy-start.6 = (bf16[7,256,256]{2,1,0:T(8,128)(2,1)S(1)}, bf16[7,256,256]{2,1,0:T(8,128)(2,1)}, u32[]{:S(2)}) copy-start(bf16[7,256,256]{2,1,0:T(8,128)(2,1)} %copy-done.5) | copy-start | bytes 2752516
  84.4 12.1 %collective-permute-start.2 = (bf16[9,64,256]{2,1,0:T(8,128)(2,1)S(1)}, bf16[9,64,256]{2,1,0:T(8,128)(2,1)S(1)}, u32[]{:S(2)}, u32[]{:S(2)}) collective-permute-start(bf16[9,64,256]{2,1,0:T(8,128)(2,1)S(1)} %get-tuple-element.33), channel_id=1, source_target_pairs={{0,1},{1,2},{2,3},{3,6},{6,7},{7,4},{4,5},{5,8},{8,9},{9,10},{10,1... | collective-permute-start | bytes 884744 | tf_op jit(solution)/shard_map/ppermute | solution.py:577
  86.8 10.2 %collective-permute-start.3 = (bf16[9,64,256]{2,1,0:T(8,128)(2,1)S(1)}, bf16[9,64,256]{2,1,0:T(8,128)(2,1)S(1)}, u32[]{:S(2)}, u32[]{:S(2)}) collective-permute-start(bf16[9,64,256]{2,1,0:T(8,128)(2,1)S(1)} %get-tuple-element.34), channel_id=1, source_target_pairs={{1,0},{2,1},{3,2},{6,3},{7,6},{4,7},{5,4},{8,5},{9,8},{10,9},{11,1... | collective-permute-start | bytes 884744 | tf_op jit(solution)/shard_map/ppermute | solution.py:578
  102.2 39.9 %all-to-all-start.3 = ((bf16[16,10,16,256]{3,2,1,0:T(8,128)(2,1)}), bf16[16,10,16,256]{3,2,1,0:T(8,128)(2,1)S(1)}, u32[]{:S(2)}, u32[]{:S(2)}) async-start(bf16[16,10,16,256]{3,2,1,0:T(8,128)(2,1)} %conv_edges.3), calls=%async_computation.3 | async-start | bytes 2621440 | tf_op jit(solution)/shard_map/all_to_all | solution.py:509

commit v5 on v4

--- a/solution.py
+++ b/solution.py
@@ -412,7 +412,7 @@
     local, total, cols, channels = out.shape
     copies = Copies(semaphores)
     outputs = []
-    for begin, end in groups_of(total, 2):
+    for begin, end in groups_of(total, 1):
         for i in range(begin, end):
             moved = shuffled(stacks[0, FINAL], arrived[:, i].reshape(local * cols, channels))
             out[:, i] = moved.reshape(local, cols, channels).astype(BF16)

time: 144 us -> 144 us (level)
  no operation moved by 1% of the time
where the time goes in v5:
time: 144 us
  Pallas kernels  52.2 us (36%)
  waiting for transfers between devices  49.3 us (34%)
  starting transfers between devices  39.6 us (28%)
  local copies, waits for them, and re-layouts  2.39 us (2%)
    pallas_call x10, Pallas kernels, call(): pl.pallas_call(kernel, out_shape=[(pltpu.VMEM if is_near else pltpu.HBM)(...  52.2 us
    all_to_all x4, waiting for transfers between devices, exchange(): lax.all_to_all(messages, 'mem', split_axis=0, concat_axis=0, tiled=True)  46.4 us
    all_to_all x4, starting transfers between devices, exchange(): lax.all_to_all(messages, 'mem', split_axis=0, concat_axis=0, tiled=True)  30.6 us
    ppermute x2, starting transfers between devices, attend_chunk(): from_left = lax.ppermute(high, 'mem', rightward)  4.88 us
    ppermute x2, starting transfers between devices, attend_chunk(): from_right = lax.ppermute(low, 'mem', leftward)  4.06 us
    ppermute x2, waiting for transfers between devices, attend_chunk(): from_right = lax.ppermute(low, 'mem', leftward)  2.94 us
  transfers between devices with their start and end apart: 8, of which 5 were waited for; matrix products, arithmetic and copies ran while one was open for 0% of the time, Pallas kernels for 30%

profile of v5, /device:TPU:15, one launch (start us, length us, event | category | flops | bytes accessed | tf_op | source)
XLA Modules:
  0.0 143.8 jit_solution(9293178634042634510)
XLA Ops:
  0.0 7.9 %conv_slab.2 = bf16[16,7,16,256]{3,2,1,0:T(8,128)(2,1)} custom-call(bf16[4,16,64,256]{3,2,1,0:T(8,128)(2,1)} %field_hbm.3, f32[2,2,256]{2,1,0:T(2,128)} %gain_hbm.3, bf16[2,3,3,256,512]{4,3,2,1,0:T(8,128)(2,1)} %weight_hbm.3, bf16[256,256]{1,0:T(8,128)(2,1)} %constant.8.clone.order_hbm), custom_call_target="tpu_custom_call" | custom-call | flops 4227858432 | bytes 1835008 | tf_op jit(solution)/shard_map/conv_slab/pallas_call | solution.py:434
  7.9 6.6 %all-to-all-start = ((bf16[16,7,16,256]{3,2,1,0:T(8,128)(2,1)}), bf16[16,7,16,256]{3,2,1,0:T(8,128)(2,1)S(1)}, u32[]{:S(2)}, u32[]{:S(2)}) async-start(bf16[16,7,16,256]{3,2,1,0:T(8,128)(2,1)} %conv_slab.2), calls=%async_computation | async-start | bytes 1835008 | tf_op jit(solution)/shard_map/all_to_all | solution.py:509
  14.5 9.5 %conv_slab.3 = (bf16[16,9,16,256]{3,2,1,0:T(8,128)(2,1)}, f32[2,2,256]{2,1,0:T(2,128)S(1)}, bf16[3,3,256,512]{3,2,1,0:T(8,128)(2,1)S(1)}, bf16[2,6,256,256]{3,2,1,0:T(8,128)(2,1)S(1)}) custom-call(bf16[4,16,64,256]{3,2,1,0:T(8,128)(2,1)} %field_hbm.3, f32[2,2,256]{2,1,0:T(2,128)} %gain_hbm.3, bf16[2,3,3,256,512]{4,3,2,1,0:T(8,128)(2,1)} %weight_hbm.3, ...), custom_call_target="tpu_custom_call" | custom-call | flops 5435817984 | bytes 2359296 | tf_op jit(solution)/shard_map/conv_slab/pallas_call | solution.py:434
  24.0 0.0 copy-start
  24.0 1.4 copy-done
  25.4 11.1 %all-to-all-done.arrived = bf16[16,7,16,256]{3,2,1,0:T(8,128)(2,1)S(1)} async-done(((bf16[16,7,16,256]{3,2,1,0:T(8,128)(2,1)}), bf16[16,7,16,256]{3,2,1,0:T(8,128)(2,1)S(1)}, u32[]{:S(2)}, u32[]{:S(2)}) %all-to-all-start) | async-done | bytes 917536 | tf_op jit(solution)/shard_map/all_to_all | solution.py:509
  36.5 0.9 copy-done.7
  37.5 5.0 %all-to-all-start.2 = ((bf16[16,9,16,256]{3,2,1,0:T(8,128)(2,1)}), bf16[16,9,16,256]{3,2,1,0:T(8,128)(2,1)S(1)}, u32[]{:S(2)}, u32[]{:S(2)}) async-start(bf16[16,9,16,256]{3,2,1,0:T(8,128)(2,1)} %get-tuple-element.30), calls=%async_computation.2 | async-start | bytes 2359296 | tf_op jit(solution)/shard_map/all_to_all | solution.py:509
  42.4 5.4 %attend.2 = (bf16[7,256,256]{2,1,0:T(8,128)(2,1)S(1)}, bf16[7,256,256]{2,1,0:T(8,128)(2,1)S(1)}, bf16[7,64,256]{2,1,0:T(8,128)(2,1)S(1)}, bf16[7,64,256]{2,1,0:T(8,128)(2,1)S(1)}) custom-call(bf16[16,7,16,256]{3,2,1,0:T(8,128)(2,1)} %copy-done.7, f32[2,2,256]{2,1,0:T(2,128)S(1)} %get-tuple-element.21.gain.refs_2_.refs_6_.refs_4_.refs_10_, ...), custom_call_target="tpu_custom_call" | custom-call | flops 1409286144 | bytes 3670016 | tf_op jit(solution)/shard_map/attend/pallas_call | solution.py:434
  47.8 0.0 copy-start.3
  47.8 0.0 copy-start.5
  47.8 2.4 %collective-permute-start = (bf16[7,64,256]{2,1,0:T(8,128)(2,1)S(1)}, bf16[7,64,256]{2,1,0:T(8,128)(2,1)S(1)}, u32[]{:S(2)}, u32[]{:S(2)}) collective-permute-start(bf16[7,64,256]{2,1,0:T(8,128)(2,1)S(1)} %get-tuple-element.25), channel_id=1, source_target_pairs={{0,1},{1,2},{2,3},{3,6},{6,7},{7,4},{4,5},{5,8},{8,9},{9,10},{10,1... | collective-permute-start | bytes 688136 | tf_op jit(solution)/shard_map/ppermute | solution.py:577
  50.3 1.9 %collective-permute-start.1 = (bf16[7,64,256]{2,1,0:T(8,128)(2,1)S(1)}, bf16[7,64,256]{2,1,0:T(8,128)(2,1)S(1)}, u32[]{:S(2)}, u32[]{:S(2)}) collective-permute-start(bf16[7,64,256]{2,1,0:T(8,128)(2,1)S(1)} %get-tuple-element.26), channel_id=1, source_target_pairs={{1,0},{2,1},{3,2},{6,3},{7,6},{4,7},{5,4},{8,5},{9,8},{10,9},{11,1... | collective-permute-start | bytes 688136 | tf_op jit(solution)/shard_map/ppermute | solution.py:578
  52.2 4.6 %conv_inner.2 = (bf16[6,128,256]{2,1,0:T(8,128)(2,1)S(1)}, f32[6,128,512]{2,1,0:T(8,128)S(1)}) custom-call(bf16[7,256,256]{2,1,0:T(8,128)(2,1)S(1)} %get-tuple-element.23.refs_0_, bf16[7,256,256]{2,1,0:T(8,128)(2,1)S(1)} %get-tuple-element.24.refs_1_.refs_2_, f32[2,2,256]{2,1,0:T(2,128)S(1)} %get-tuple-element.21.gain.refs_2_.refs_6_.refs_4_.refs_10_, ...), custom_call_target="tpu_custom_call" | custom-call | flops 2415919104 | bytes 3145728 | tf_op jit(solution)/shard_map/conv_inner/pallas_call | solution.py:434
  56.8 0.0 collective-permute-done.refs_2_.refs_4_
  56.8 2.4 %collective-permute-done.1.refs_3_.refs_6_ = bf16[7,64,256]{2,1,0:T(8,128)(2,1)S(1)} collective-permute-done((bf16[7,64,256]{2,1,0:T(8,128)(2,1)S(1)}, bf16[7,64,256]{2,1,0:T(8,128)(2,1)S(1)}, u32[]{:S(2)}, u32[]{:S(2)}) %collective-permute-start.1) | collective-permute-done | bytes 229408 | tf_op jit(solution)/shard_map/ppermute | solution.py:578
  59.2 0.0 copy-done.5
  59.2 3.7 %conv_edges.2 = bf16[16,6,16,256]{3,2,1,0:T(8,128)(2,1)} custom-call(bf16[7,256,256]{2,1,0:T(8,128)(2,1)S(1)} %get-tuple-element.23.refs_0_, bf16[7,256,256]{2,1,0:T(8,128)(2,1)S(1)} %get-tuple-element.24.refs_1_.refs_2_, bf16[7,64,256]{2,1,0:T(8,128)(2,1)S(1)} %collective-permute-done.refs_2_.refs_4_, ...), custom_call_target="tpu_custom_call" | custom-call | flops 2415919104 | bytes 3145728 | tf_op jit(solution)/shard_map/conv_edges/pallas_call | solution.py:434
  62.9 7.2 %all-to-all-done.2.arrived = bf16[16,9,16,256]{3,2,1,0:T(8,128)(2,1)S(1)} async-done(((bf16[16,9,16,256]{3,2,1,0:T(8,128)(2,1)}), bf16[16,9,16,256]{3,2,1,0:T(8,128)(2,1)S(1)}, u32[]{:S(2)}, u32[]{:S(2)}) %all-to-all-start.2) | async-done | bytes 1179680 | tf_op jit(solution)/shard_map/all_to_all | solution.py:509
  70.2 9.8 %all-to-all-start.1 = ((bf16[16,6,16,256]{3,2,1,0:T(8,128)(2,1)}), bf16[16,6,16,256]{3,2,1,0:T(8,128)(2,1)}, u32[]{:S(2)}, u32[]{:S(2)}) async-start(bf16[16,6,16,256]{3,2,1,0:T(8,128)(2,1)} %conv_edges.2), calls=%async_computation.1 | async-start | bytes 1572864 | tf_op jit(solution)/shard_map/all_to_all | solution.py:509
  80.0 4.4 %attend.3 = (bf16[9,256,256]{2,1,0:T(8,128)(2,1)S(1)}, bf16[9,256,256]{2,1,0:T(8,128)(2,1)S(1)}, bf16[9,64,256]{2,1,0:T(8,128)(2,1)S(1)}, bf16[9,64,256]{2,1,0:T(8,128)(2,1)S(1)}) custom-call(bf16[16,9,16,256]{3,2,1,0:T(8,128)(2,1)S(1)} %all-to-all-done.2.arrived, f32[2,2,256]{2,1,0:T(2,128)S(1)} %get-tuple-element.21.gain.refs_2_.refs_6_.refs_4_.refs_10_, ...), custom_call_target="tpu_custom_call" | custom-call | flops 1811939328 | bytes 4718592 | tf_op jit(solution)/shard_map/attend/pallas_call | solution.py:434
  84.4 2.4 %collective-permute-start.2 = (bf16[9,64,256]{2,1,0:T(8,128)(2,1)S(1)}, bf16[9,64,256]{2,1,0:T(8,128)(2,1)S(1)}, u32[]{:S(2)}, u32[]{:S(2)}) collective-permute-start(bf16[9,64,256]{2,1,0:T(8,128)(2,1)S(1)} %get-tuple-element.33), channel_id=1, source_target_pairs={{0,1},{1,2},{2,3},{3,6},{6,7},{7,4},{4,5},{5,8},{8,9},{9,10},{10,1... | collective-permute-start | bytes 884744 | tf_op jit(solution)/shard_map/ppermute | solution.py:577
  86.8 2.1 %collective-permute-start.3 = (bf16[9,64,256]{2,1,0:T(8,128)(2,1)S(1)}, bf16[9,64,256]{2,1,0:T(8,128)(2,1)S(1)}, u32[]{:S(2)}, u32[]{:S(2)}) collective-permute-start(bf16[9,64,256]{2,1,0:T(8,128)(2,1)S(1)} %get-tuple-element.34), channel_id=1, source_target_pairs={{1,0},{2,1},{3,2},{6,3},{7,6},{4,7},{5,4},{8,5},{9,8},{10,9},{11,1... | collective-permute-start | bytes 884744 | tf_op jit(solution)/shard_map/ppermute | solution.py:578
  89.0 7.4 %conv_inner.3 = (bf16[10,128,256]{2,1,0:T(8,128)(2,1)S(1)}, f32[10,128,512]{2,1,0:T(8,128)S(1)}) custom-call(bf16[7,256,256]{2,1,0:T(8,128)(2,1)S(1)} %copy-done.4, bf16[9,256,256]{2,1,0:T(8,128)(2,1)S(1)} %get-tuple-element.31.refs_1_, bf16[7,256,256]{2,1,0:T(8,128)(2,1)S(1)} %copy-done.6, bf16[9,256,256]{2,1,0:T(8,128)(2,1)S(1)} %get-tuple-element.32.refs_3_, ...), custom_call_target="tpu_custom_call" | custom-call | flops 4026531840 | bytes 5242880 | tf_op jit(solution)/shard_map/conv_inner/pallas_call | solution.py:434
  96.5 0.0 collective-permute-done.2.refs_5_
  96.5 0.6 collective-permute-done.3.refs_7_
  97.1 5.1 %conv_edges.3 = bf16[16,10,16,256]{3,2,1,0:T(8,128)(2,1)} custom-call(bf16[7,256,256]{2,1,0:T(8,128)(2,1)S(1)} %copy-done.4, bf16[9,256,256]{2,1,0:T(8,128)(2,1)S(1)} %get-tuple-element.31.refs_1_, bf16[7,256,256]{2,1,0:T(8,128)(2,1)S(1)} %copy-done.6, bf16[9,256,256]{2,1,0:T(8,128)(2,1)S(1)} %get-tuple-element.32.refs_3_, ...), custom_call_target="tpu_custom_call" | custom-call | flops 4026531840 | bytes 5242880 | tf_op jit(solution)/shard_map/conv_edges/pallas_call | solution.py:434
  102.2 0.0 all-to-all-done.1.refs_0_
  102.2 9.3 %all-to-all-start.3 = ((bf16[16,10,16,256]{3,2,1,0:T(8,128)(2,1)}), bf16[16,10,16,256]{3,2,1,0:T(8,128)(2,1)S(1)}, u32[]{:S(2)}, u32[]{:S(2)}) async-start(bf16[16,10,16,256]{3,2,1,0:T(8,128)(2,1)} %conv_edges.3), calls=%async_computation.3 | async-start | bytes 2621440 | tf_op jit(solution)/shard_map/all_to_all | solution.py:509
  111.5 2.5 %place.2.refs_0_ = bf16[4,16,64,256]{3,2,1,0:T(8,128)(2,1)} custom-call(bf16[16,6,16,256]{3,2,1,0:T(8,128)(2,1)} %all-to-all-done.1.refs_0_, bf16[2,6,256,256]{3,2,1,0:T(8,128)(2,1)S(1)} %get-tuple-element.22.stacks.refs_3_.refs_7_.refs_1_.refs_5_.refs_11_.refs_2_), custom_call_target="tpu_custom_call" | custom-call | flops 201326592 | bytes 1572864 | tf_op jit(solution)/shard_map/place/pallas_call | solution.py:434
  114.1 28.0 %all-to-all-done.3.refs_1_ = bf16[16,10,16,256]{3,2,1,0:T(8,128)(2,1)S(1)} async-done(((bf16[16,10,16,256]{3,2,1,0:T(8,128)(2,1)}), bf16[16,10,16,256]{3,2,1,0:T(8,128)(2,1)S(1)}, u32[]{:S(2)}, u32[]{:S(2)}) %all-to-all-start.3) | async-done | bytes 1310752 | tf_op jit(solution)/shard_map/all_to_all | solution.py:509
  142.1 1.6 %place.3 = bf16[4,16,64,256]{3,2,1,0:T(8,128)(2,1)} custom-call(bf16[4,16,64,256]{3,2,1,0:T(8,128)(2,1)} %place.2.refs_0_, bf16[16,10,16,256]{3,2,1,0:T(8,128)(2,1)S(1)} %all-to-all-done.3.refs_1_, bf16[2,6,256,256]{3,2,1,0:T(8,128)(2,1)S(1)} %get-tuple-element.22.stacks.refs_3_.refs_7_.refs_1_.refs_5_.refs_11_.refs_2_), custom_call_target="tpu_custom_call", output_to_operand_aliasing={{}: (0, {})} | custom-call | flops 335544320 | bytes 2621440 | tf_op jit(solution)/shard_map/place/pallas_call | solution.py:434
  (10 shorter events, 0.0 us)
Async XLA Ops:
  7.9 28.6 %all-to-all-start = ((bf16[16,7,16,256]{3,2,1,0:T(8,128)(2,1)}), bf16[16,7,16,256]{3,2,1,0:T(8,128)(2,1)S(1)}, u32[]{:S(2)}, u32[]{:S(2)}) async-start(bf16[16,7,16,256]{3,2,1,0:T(8,128)(2,1)} %conv_slab.2), calls=%async_computation | async-start | bytes 1835008 | tf_op jit(solution)/shard_map/all_to_all | solution.py:509
  24.0 1.4 copy-start
  36.5 0.9 copy-start.7
  37.5 32.7 %all-to-all-start.2 = ((bf16[16,9,16,256]{3,2,1,0:T(8,128)(2,1)}), bf16[16,9,16,256]{3,2,1,0:T(8,128)(2,1)S(1)}, u32[]{:S(2)}, u32[]{:S(2)}) async-start(bf16[16,9,16,256]{3,2,1,0:T(8,128)(2,1)} %get-tuple-element.30), calls=%async_computation.2 | async-start | bytes 2359296 | tf_op jit(solution)/shard_map/all_to_all | solution.py:509
  42.4 9.8 %copy-start.1 = (bf16[3,3,256,512]{3,2,1,0:T(8,128)(2,1)S(1)}, bf16[3,3,256,512]{3,2,1,0:T(8,128)(2,1)}, u32[]{:S(2)}) copy-start(bf16[3,3,256,512]{3,2,1,0:T(8,128)(2,1)} %copy-done) | copy-start | bytes 7077892
  47.8 11.4 %copy-start.3 = (bf16[7,256,256]{2,1,0:T(8,128)(2,1)}, bf16[7,256,256]{2,1,0:T(8,128)(2,1)S(1)}, u32[]{:S(2)}) copy-start(bf16[7,256,256]{2,1,0:T(8,128)(2,1)S(1)} %get-tuple-element.23.refs_0_) | copy-start | bytes 2752516
  47.8 11.4 %copy-start.5 = (bf16[7,256,256]{2,1,0:T(8,128)(2,1)}, bf16[7,256,256]{2,1,0:T(8,128)(2,1)S(1)}, u32[]{:S(2)}) copy-start(bf16[7,256,256]{2,1,0:T(8,128)(2,1)S(1)} %get-tuple-element.24.refs_1_.refs_2_) | copy-start | bytes 2752516
  47.8 9.0 %collective-permute-start = (bf16[7,64,256]{2,1,0:T(8,128)(2,1)S(1)}, bf16[7,64,256]{2,1,0:T(8,128)(2,1)S(1)}, u32[]{:S(2)}, u32[]{:S(2)}) collective-permute-start(bf16[7,64,256]{2,1,0:T(8,128)(2,1)S(1)} %get-tuple-element.25), channel_id=1, source_target_pairs={{0,1},{1,2},{2,3},{3,6},{6,7},{7,4},{4,5},{5,8},{8,9},{9,10},{10,1... | collective-permute-start | bytes 688136 | tf_op jit(solution)/shard_map/ppermute | solution.py:577
  50.3 8.9 %collective-permute-start.1 = (bf16[7,64,256]{2,1,0:T(8,128)(2,1)S(1)}, bf16[7,64,256]{2,1,0:T(8,128)(2,1)S(1)}, u32[]{:S(2)}, u32[]{:S(2)}) collective-permute-start(bf16[7,64,256]{2,1,0:T(8,128)(2,1)S(1)} %get-tuple-element.26), channel_id=1, source_target_pairs={{1,0},{2,1},{3,2},{6,3},{7,6},{4,7},{5,4},{8,5},{9,8},{10,9},{11,1... | collective-permute-start | bytes 688136 | tf_op jit(solution)/shard_map/ppermute | solution.py:578
  70.2 32.0 %all-to-all-start.1 = ((bf16[16,6,16,256]{3,2,1,0:T(8,128)(2,1)}), bf16[16,6,16,256]{3,2,1,0:T(8,128)(2,1)}, u32[]{:S(2)}, u32[]{:S(2)}) async-start(bf16[16,6,16,256]{3,2,1,0:T(8,128)(2,1)} %conv_edges.2), calls=%async_computation.1 | async-start | bytes 1572864 | tf_op jit(solution)/shard_map/all_to_all | solution.py:509
  80.0 9.0 %copy-start.2 = (bf16[3,3,256,512]{3,2,1,0:T(8,128)(2,1)S(1)}, bf16[3,3,256,512]{3,2,1,0:T(8,128)(2,1)}, u32[]{:S(2)}) copy-start(bf16[3,3,256,512]{3,2,1,0:T(8,128)(2,1)} %copy-done) | copy-start | bytes 7077892
  80.0 9.0 %copy-start.4 = (bf16[7,256,256]{2,1,0:T(8,128)(2,1)S(1)}, bf16[7,256,256]{2,1,0:T(8,128)(2,1)}, u32[]{:S(2)}) copy-start(bf16[7,256,256]{2,1,0:T(8,128)(2,1)} %copy-done.3) | copy-start | bytes 2752516
  80.0 9.0 %copy-start.6 = (bf16[7,256,256]{2,1,0:T(8,128)(2,1)S(1)}, bf16[7,256,256]{2,1,0:T(8,128)(2,1)}, u32[]{:S(2)}) copy-start(bf16[7,256,256]{2,1,0:T(8,128)(2,1)} %copy-done.5) | copy-start | bytes 2752516
  84.4 12.1 %collective-permute-start.2 = (bf16[9,64,256]{2,1,0:T(8,128)(2,1)S(1)}, bf16[9,64,256]{2,1,0:T(8,128)(2,1)S(1)}, u32[]{:S(2)}, u32[]{:S(2)}) collective-permute-start(bf16[9,64,256]{2,1,0:T(8,128)(2,1)S(1)} %get-tuple-element.33), channel_id=1, source_target_pairs={{0,1},{1,2},{2,3},{3,6},{6,7},{7,4},{4,5},{5,8},{8,9},{9,10},{10,1... | collective-permute-start | bytes 884744 | tf_op jit(solution)/shard_map/ppermute | solution.py:577
  86.8 10.2 %collective-permute-start.3 = (bf16[9,64,256]{2,1,0:T(8,128)(2,1)S(1)}, bf16[9,64,256]{2,1,0:T(8,128)(2,1)S(1)}, u32[]{:S(2)}, u32[]{:S(2)}) collective-permute-start(bf16[9,64,256]{2,1,0:T(8,128)(2,1)S(1)} %get-tuple-element.34), channel_id=1, source_target_pairs={{1,0},{2,1},{3,2},{6,3},{7,6},{4,7},{5,4},{8,5},{9,8},{10,9},{11,1... | collective-permute-start | bytes 884744 | tf_op jit(solution)/shard_map/ppermute | solution.py:578
  102.2 39.9 %all-to-all-start.3 = ((bf16[16,10,16,256]{3,2,1,0:T(8,128)(2,1)}), bf16[16,10,16,256]{3,2,1,0:T(8,128)(2,1)S(1)}, u32[]{:S(2)}, u32[]{:S(2)}) async-start(bf16[16,10,16,256]{3,2,1,0:T(8,128)(2,1)} %conv_edges.3), calls=%async_computation.3 | async-start | bytes 2621440 | tf_op jit(solution)/shard_map/all_to_all | solution.py:509
